TPU v7x, 32 devices: a whole 2x2x4 slice. The times are simulated.
32 devices in a mesh: dp: 2 (over core), seq: 4 (over y, x), tensor: 4 (over z).
Axes of the slice: x: 2, y: 2, z: 4, core: 2. Of those that a mesh axis runs over, the one named last changes fastest.
Arguments:
- tokens: bfloat16 [2, 4096, 512], P('dp', 'seq'), may hold values from -6 to 6
- levels: int32 [2, 4096], P('dp', 'seq'), may hold values from 0 to 255
- boundaries: int32 [2, 32], P('dp', 'seq'), may hold values from 0 to 255
- level_table: float32 [256, 512], replicated, may hold values from -6 to 6
- w_key: bfloat16 [512, 1024], P(None, 'tensor'), as said below
- w_value: bfloat16 [512, 1024], P(None, 'tensor'), may hold values from -0.25 to 0.25
- slopes: float32 [8], P('tensor'), may hold values from 0.003 to 0.3
- queries: bfloat16 [2, 1024, 1024], P('dp', 'seq', 'tensor'), may hold values from -6 to 6
- cotangent: bfloat16 [2, 1024, 1024], P('dp', 'seq', 'tensor'), may hold values from -6 to 6
Outputs:
- attended: bfloat16 [2, 1024, 1024], P('dp', 'seq', 'tensor')
- query_grad: bfloat16 [2, 1024, 1024], P('dp', 'seq', 'tensor')
- key_weight_grad: float32 [512, 1024], P(('dp', 'seq'), 'tensor')
- value_weight_grad: float32 [512, 1024], P(('dp', 'seq'), 'tensor')
- slope_grad: float32 [8], P('tensor')
Inputs may be any that keep to these rules, and one draw needn't show every extreme that they name: `boundaries`: a value of 128 or more means that no episode starts in the block. `w_key`: entries lie within 6 / sqrt(512) of zero.
All inputs are finite; a program needn't handle non-finite values.
Results may differ from a plain program's by a relative error of at most 0.0045.
The roundings to bfloat16 on the way count: a program that leaves them out, or rounds other values in their place, can miss the bound.
Values may be sent and summed in bfloat16 or wider, within the bound.
No kernel may reach another device: no remote copies, remote signals or barrier semaphores. Data moves between devices by JAX's collectives and lax.ppermute only.
A program may use at most 64 MiB of HBM per device.

v0:
```python
import jax
import jax.numpy as jnp
from jax import lax
from jax.sharding import PartitionSpec as P

HEAD = 128
BLOCK = 128


def carried_in(part, axis, combine, identity):
    place = lax.axis_index(axis)
    gathered = lax.all_gather(part, axis)
    state = jnp.zeros_like(part) + jnp.asarray(identity, part.dtype)

    def one(step, state):
        return combine(state, lax.dynamic_index_in_dim(gathered, step, 0, False))

    return lax.fori_loop(0, place, one, state)


def add_counts(earlier, later):
    return earlier + later


def per_device(tokens, levels, boundaries, level_table, w_key, w_value, slopes, queries, cotangent):
    scale = HEAD ** (-0.5)
    raw = tokens[0].astype(jnp.float32)
    centered = raw - jnp.mean(raw, axis=1, keepdims=True)
    normed = centered / jnp.sqrt(jnp.mean(centered * centered, axis=1, keepdims=True) + 1e-05)
    lookup = jnp.take(level_table, levels[0], axis=0)
    inputs = (normed + lookup).astype(jnp.bfloat16)
    keys = jnp.dot(inputs, w_key, preferred_element_type=jnp.float32).astype(jnp.bfloat16)
    values = jnp.dot(inputs, w_value, preferred_element_type=jnp.float32).astype(jnp.bfloat16)
    bounds = boundaries[0]
    has = (bounds < BLOCK).astype(jnp.int32)
    earlier = carried_in(jnp.sum(has).reshape(1), "seq", add_counts, jnp.zeros((1,), jnp.int32))
    before = earlier[0] + jnp.cumsum(has) - has
    position = jnp.arange(BLOCK, dtype=jnp.int32)
    inside = (position[None, :] >= bounds[:, None]).astype(jnp.int32)
    episode = (before[:, None] + inside).reshape(-1).astype(jnp.float32)
    query_all, grad_all = (
        lax.all_gather(queries[0], "seq", axis=0, tiled=True),
        lax.all_gather(cotangent[0], "seq", axis=0, tiled=True),
    )
    latents = query_all.shape[0]
    heads = w_key.shape[1] // HEAD
    tok_rows = keys.shape[0]
    own_rows = queries.shape[1]
    start = lax.axis_index("seq") * own_rows
    query_heads = query_all.reshape(latents, heads, HEAD)
    grad_heads = grad_all.reshape(latents, heads, HEAD)
    key_heads = keys.reshape(tok_rows, heads, HEAD)
    value_heads = values.reshape(tok_rows, heads, HEAD)
    score = (
        jnp.einsum("nhd,thd->hnt", query_heads, key_heads, preferred_element_type=jnp.float32)
        * scale
    )
    score = score + slopes[:, None, None] * episode[None, None, :]
    top = lax.pmax(jnp.max(score, axis=2), "seq")
    expo = jnp.exp(score - top[:, :, None])
    part_norm = jnp.sum(expo, axis=2)
    part_out = jnp.einsum(
        "hnt,thd->nhd", expo.astype(jnp.bfloat16), value_heads, preferred_element_type=jnp.float32
    ).reshape(latents, heads * HEAD)
    grad_f32 = grad_all.astype(jnp.float32)
    summed, total = lax.psum((part_out, part_norm), "seq")
    mixed = (summed.reshape(latents, heads, HEAD) / total.T[:, :, None]).reshape(
        latents, heads * HEAD
    )
    delta = jnp.sum((grad_f32 * mixed).reshape(latents, heads, HEAD), axis=2).T
    own_mixed = lax.dynamic_slice_in_dim(mixed, start, own_rows, 0)
    attended = own_mixed.astype(jnp.bfloat16)[None]
    probs = expo / total[:, :, None]
    probs_b = probs.astype(jnp.bfloat16)
    value_tok = (
        jnp.einsum("hnt,nhd->thd", probs_b, grad_heads, preferred_element_type=jnp.float32)
        .astype(jnp.bfloat16)
        .reshape(tok_rows, heads * HEAD)
    )
    dprod = jnp.einsum("nhd,thd->hnt", grad_heads, value_heads, preferred_element_type=jnp.float32)
    score_grad = probs * (dprod - delta[:, :, None])
    slope_part = jnp.sum(score_grad * episode[None, None, :], axis=(1, 2))
    score_grad_b = score_grad.astype(jnp.bfloat16)
    query_part = (
        scale
        * jnp.einsum("hnt,thd->nhd", score_grad_b, key_heads, preferred_element_type=jnp.float32)
    ).reshape(latents, heads * HEAD)
    key_tok = (
        (
            scale
            * jnp.einsum(
                "hnt,nhd->thd", score_grad_b, query_heads, preferred_element_type=jnp.float32
            )
        )
        .astype(jnp.bfloat16)
        .reshape(tok_rows, heads * HEAD)
    )
    query_grad = lax.psum_scatter(query_part, "seq", scatter_dimension=0, tiled=True).astype(
        jnp.bfloat16
    )[None]
    key_part = jnp.dot(inputs.T, key_tok, preferred_element_type=jnp.float32)
    value_part = jnp.dot(inputs.T, value_tok, preferred_element_type=jnp.float32)
    key_weight_grad, value_weight_grad = (
        lax.psum_scatter(key_part, ("dp", "seq"), scatter_dimension=0, tiled=True),
        lax.psum_scatter(value_part, ("dp", "seq"), scatter_dimension=0, tiled=True),
    )
    slope_grad = lax.psum(slope_part, ("dp", "seq"))
    return (attended, query_grad, key_weight_grad, value_weight_grad, slope_grad)


def solution(mesh):
    return jax.shard_map(
        per_device,
        mesh=mesh,
        in_specs=(
            P("dp", "seq", None),
            P("dp", "seq"),
            P("dp", "seq"),
            P(),
            P(None, "tensor"),
            P(None, "tensor"),
            P("tensor"),
            P("dp", "seq", "tensor"),
            P("dp", "seq", "tensor"),
        ),
        out_specs=(
            P("dp", "seq", "tensor"),
            P("dp", "seq", "tensor"),
            P(("dp", "seq"), "tensor"),
            P(("dp", "seq"), "tensor"),
            P("tensor"),
        ),
        check_vma=False,
    )
```

profile of v0, /device:TPU:0, one launch (start us, length us, event | category | flops | bytes accessed | tf_op | source)
XLA Modules:
  0.0 251.0 jit_solution(13453935119650713189)
XLA Ops:
  7.2 0.0 copy-start
  7.2 0.0 all-reduce.3.cloned.1.call-start
  7.2 1.3 fusion.40
  8.6 0.7 fusion.39
  9.2 1.2 dynamic-slice
  10.5 1.4 dynamic-update-slice
  11.9 0.2 reduce-window.8
  12.1 8.8 %all-reduce = s32[4]{0:T(128)S(1)} all-reduce(s32[4]{0:T(128)S(1)} %dynamic-update-slice), channel_id=1, replica_groups=mesh['dp'=2,'seq'=4,'tensor'=4] {'seq'}, use_global_device_ids=true, to_apply=%add | all-reduce | flops 4 | bytes 32
  20.9 0.7 compare_select_fusion
  21.6 0.7 compare_and_fusion
  22.3 1.4 convert_reduce_fusion
  23.7 1.7 fusion.11
  25.4 1.0 copy.25
  26.4 15.7 %all-gather = bf16[1,1024,256]{1,2,0:T(8,128)(2,1)} all-gather(bf16[1,256,256]{1,2,0:T(8,128)(2,1)S(1)} %copy.25), channel_id=2, replica_groups=mesh['dp'=2,'seq'=4,'tensor'=4] {'seq'}, dimensions={1}, use_global_device_ids=true | all-gather | bytes 655360 | tf_op jit(solution)/shard_map/all_gather | solution.py:42
  42.1 0.0 copy-done
  42.1 0.0 copy-start.4
  42.1 0.0 copy-start.6
  42.1 0.0 copy-start.7
  42.1 3.5 %gather_fusion = f32[1024,512]{1,0:T(8,128)S(1)} fusion(f32[256,512]{1,0:T(8,128)S(1)} %copy-done, s32[1024]{0:T(1024)S(1)} %broadcast_clamp_fusion), kind=kCustom, calls=%fused_computation | custom fusion | bytes 4198400 | tf_op jit(solution)/shard_map/jit(_take)/gather | solution.py:30
  45.6 2.0 fusion.13
  47.6 0.0 copy-done.4
  47.6 0.5 convolution_convert_fusion
  48.1 2.3 convolution_convert_fusion.1
  50.4 0.0 copy-done.6
  50.4 0.1 convert_bitcast_fusion.2
  50.5 0.0 copy-done.7
  50.5 0.1 broadcast_multiply_fusion
  50.5 5.1 %bitcast_reduce_fusion = (f32[2,1024]{1,0:T(2,128)S(1)}, f32[2,1024,1024]{2,1,0:T(8,128)}) fusion(f32[2,1024]{1,0:T(2,128)S(1)} %broadcast_multiply_fusion, bf16[1024,2,128]{0,2,1:T(8,128)(2,1)S(1)} %bitcast.113, bf16[1024,2,128]{0,2,1:T(8,128)(2,1)} %bitcast.117), kind=kOutput, calls=%fused_computation.4 | convolution fusion | flops 543160320 | bytes 9453568 | tf_op jit(solution)/shard_map/nhd,thd->hnt/dot_general | solution.py:55
  55.6 0.0 copy-start.5
  55.6 9.1 %pmax.7 = f32[2,1024]{1,0:T(2,128)S(1)} all-reduce(f32[2,1024]{1,0:T(2,128)S(1)} %get-tuple-element.44), channel_id=1, replica_groups=mesh['dp'=2,'seq'=4,'tensor'=4] {'seq'}, use_global_device_ids=true, to_apply=%region_7.8 | all-reduce | flops 2048 | bytes 16384 | tf_op jit(solution)/shard_map/pmax | solution.py:59
  64.8 6.5 %fusion.6 = f32[2,128,1024]{2,1,0:T(8,128)} fusion(bf16[1024,2,128]{0,2,1:T(8,128)(2,1)} %bitcast.120, f32[2,1024,1024]{2,1,0:T(8,128)} %get-tuple-element.45, f32[2,1024]{1,0:T(2,128)S(1)} %pmax.7, f32[2,1024]{1,0:T(2,128)S(1)} %broadcast_multiply_fusion), kind=kOutput, calls=%fused_computation.13 | convolution fusion | flops 545259520 | bytes 9977856 | tf_op jit(solution)/shard_map/hnt,thd->nhd/dot_general | solution.py:62
  71.2 0.0 all-reduce.3.cloned.1.call-update
  71.3 0.0 reduce-scatter.4.cloned.1.call-start
  71.3 0.0 copy-done.5
  71.3 0.1 copy.29
  71.4 4.4 %fusion.2 = f32[2,1024]{1,0:T(2,128)S(1)} fusion(f32[2,1024,1024]{2,1,0:T(8,128)} %get-tuple-element.45, f32[2,1024]{1,0:T(2,128)S(1)} %pmax.7, f32[2,1024]{1,0:T(2,128)S(1)} %broadcast_multiply_fusion), kind=kLoop, calls=%fused_computation.9 | loop fusion | flops 8386560 | bytes 8413184 | tf_op jit(solution)/shard_map/reduce_sum | solution.py:61
  75.8 9.5 %psum.22 = f32[2,1024]{1,0:T(2,128)S(1)} all-reduce(f32[2,1024]{1,0:T(2,128)S(1)} %fusion.2), channel_id=1, replica_groups=mesh['dp'=2,'seq'=4,'tensor'=4] {'seq'}, use_global_device_ids=true, to_apply=%region_10.11 | all-reduce | flops 2048 | bytes 16384 | tf_op jit(solution)/shard_map/psum | solution.py:66
  85.3 14.6 %all-gather.1 = bf16[1,1024,256]{1,2,0:T(8,128)(2,1)} all-gather(bf16[1,256,256]{1,2,0:T(8,128)(2,1)S(1)} %copy.29), channel_id=3, replica_groups=mesh['dp'=2,'seq'=4,'tensor'=4] {'seq'}, dimensions={1}, use_global_device_ids=true | all-gather | bytes 655360 | tf_op jit(solution)/shard_map/all_gather | solution.py:43
  99.9 27.2 %all-reduce.3.cloned.1.call-done = f32[1024,256]{0,1:T(8,128)} async-done(((f32[1024,256]{0,1:T(8,128)}), f32[1024,256]{0,1:T(8,128)}) %all-reduce.3.cloned.1.call-update) | async-done | bytes 1048592 | tf_op jit(solution)/shard_map/psum | solution.py:66
  127.0 2.4 bitcast_reduce_fusion.1
  129.4 6.3 %multiply_reduce_fusion = (f32[2]{0:T(128)S(1)}, bf16[2,1024,1024]{1,2,0:T(8,128)(2,1)S(1)}) fusion(f32[1024]{0:T(1024)S(1)} %convert_bitcast_fusion.2, f32[2,1024]{1,0:T(2,128)S(1)} %bitcast.127, bf16[1024,2,128]{0,2,1:T(8,128)(2,1)} %bitcast.121, bf16[1024,2,128]{0,2,1:T(8,128)(2,1)} %bitcast.115, f32[2,1024]{1,0:T(2,128)S(1)} %psum.22, ...), kind=kOutput, calls=%fused_computation.6 | convolution fusion | flops 555745280 | bytes 13668360 | tf_op jit(solution)/shard_map/nhd,thd->hnt/dot_general | solution.py:80
  135.8 2.2 fusion.22
  137.9 0.1 copy-done.2
  138.0 2.6 %copy.33 = f32[1024,256]{1,0:T(8,128)} copy(f32[1024,256]{0,1:T(8,128)} %bitcast.112) | data formatting | bytes 2097152 | tf_op jit(solution)/shard_map/reshape | solution.py:87
  140.6 0.0 reduce-scatter.4.cloned.1.call-update
  140.6 0.2 reduce-scatter.8.cloned.1.call-start
  140.9 2.0 fusion.16
  142.9 0.0 copy-start.1
  142.9 0.0 copy-start.3
  142.9 6.1 %fusion.28 = bf16[2,1024,128]{1,2,0:T(8,128)(2,1)S(1)} fusion(bf16[1024,2,128]{0,2,1:T(8,128)(2,1)} %bitcast.116, f32[2,1024]{1,0:T(2,128)S(1)} %psum.22, f32[2,1024]{1,0:T(2,128)S(1)} %pmax.7, f32[2,1024]{1,0:T(2,128)S(1)} %broadcast_multiply_fusion, f32[2,1024,1024]{2,1,0:T(8,128)} %get-tuple-element.45), kind=kOutput, calls=%fused_computation.33 | convolution fusion | flops 547618816 | bytes 9461760 | tf_op jit(solution)/shard_map/hnt,nhd->thd/dot_general | solution.py:76
  149.0 0.0 copy-done.1
  149.0 1.3 fusion.34
  150.3 0.0 reduce-scatter.8.cloned.1.call-update
  150.3 0.0 reduce-scatter.6.cloned.1.call-start
  150.3 0.0 copy-done.3
  150.4 3.8 %fusion.31 = bf16[2,1024,128]{1,2,0:T(8,128)(2,1)S(1)} fusion(bf16[1024,2,128]{0,2,1:T(8,128)(2,1)S(1)} %bitcast.118, bf16[2,1024,1024]{1,2,0:T(8,128)(2,1)} %copy-done.2), kind=kOutput, calls=%fused_computation.36 | convolution fusion | flops 537395200 | bytes 5242880 | tf_op jit(solution)/shard_map/hnt,nhd->thd/dot_general | solution.py:91
  154.2 2.5 %fusion.36 = f32[512,256]{1,0:T(8,128)} fusion(bf16[1024,256]{0,1:T(8,128)(2,1)S(1)} %bitcast.123, bf16[1,1024,512]{2,1,0:T(8,128)(2,1)} %copy-done.1), kind=kOutput, calls=%fused_computation.40 | convolution fusion | flops 268435456 | bytes 2097152 | tf_op jit(solution)/shard_map/dot_general | solution.py:101
  156.7 0.0 reduce-scatter.6.cloned.1.call-update
  156.8 14.8 %psum.23 = f32[2]{0:T(128)} all-reduce(f32[2]{0:T(128)S(1)} %get-tuple-element.46), channel_id=1, replica_groups=mesh['dp'=2,'seq'=4,'tensor'=4] {'dp','seq'}, use_global_device_ids=true, to_apply=%region_16.17 | all-reduce | flops 2 | bytes 16 | tf_op jit(solution)/shard_map/psum | solution.py:107
  171.5 0.9 fusion.38
  172.4 0.8 copy.36
  173.2 1.6 convert_bitcast_fusion.1
  174.8 32.0 %reduce-scatter.8.cloned.1.call-done = f32[64,256]{1,0:T(8,128)} async-done(((f32[512,256]{1,0:T(8,128)}), f32[64,256]{1,0:T(8,128)}) %reduce-scatter.8.cloned.1.call-update) | async-done | bytes 65552 | tf_op jit(solution)/shard_map/reduce_scatter | solution.py:105
  206.8 37.6 %reduce-scatter.6.cloned.1.call-done = f32[64,256]{1,0:T(8,128)} async-done(((f32[512,256]{1,0:T(8,128)}), f32[64,256]{1,0:T(8,128)}) %reduce-scatter.6.cloned.1.call-update) | async-done | bytes 65552 | tf_op jit(solution)/shard_map/reduce_scatter | solution.py:104
  (8 shorter events, 0.0 us)
Async XLA Ops:
  7.2 34.9 %copy-start = (f32[256,512]{1,0:T(8,128)S(1)}, f32[256,512]{1,0:T(8,128)}, u32[]{:S(2)}) copy-start(f32[256,512]{1,0:T(8,128)} %param.14) | copy-start | bytes 1572868
  7.2 119.9 %all-reduce.3.cloned.1.call-start = ((), (), s32[]{:S(2)}) async-start(), calls=%async_computation.3 | async-start | bytes 2097152 | tf_op jit(solution)/shard_map/psum | solution.py:66
  42.1 5.5 %copy-start.4 = (bf16[512,256]{1,0:T(8,128)(2,1)S(1)}, bf16[512,256]{1,0:T(8,128)(2,1)}, u32[]{:S(2)}) copy-start(bf16[512,256]{1,0:T(8,128)(2,1)} %param.15) | copy-start | bytes 786436
  42.1 8.3 %copy-start.6 = (s32[1,8]{1,0:T(1,128)S(1)}, s32[1,8]{1,0:T(1,128)}, u32[]{:S(2)}) copy-start(s32[1,8]{1,0:T(1,128)} %param.13) | copy-start | bytes 100
  42.1 8.4 %copy-start.7 = (f32[2]{0:T(128)S(1)}, f32[2]{0:T(128)}, u32[]{:S(2)}) copy-start(f32[2]{0:T(128)} %param.17) | copy-start | bytes 28
  55.6 15.7 %copy-start.5 = (bf16[1,256,256]{2,1,0:T(8,128)(2,1)S(1)}, bf16[1,256,256]{2,1,0:T(8,128)(2,1)}, u32[]{:S(2)}) copy-start(bf16[1,256,256]{2,1,0:T(8,128)(2,1)} %param.19) | copy-start | bytes 393220
  71.3 101.9 %reduce-scatter.4.cloned.1.call-start = ((), (), s32[]{:S(2)}) async-start(), calls=%async_computation.4 | async-start | bytes 1310720 | tf_op jit(solution)/shard_map/reduce_scatter | solution.py:98
  135.7 2.3 copy-start.2
  140.6 66.1 %reduce-scatter.8.cloned.1.call-start = ((), (), s32[]{:S(2)}) async-start(), calls=%async_computation.6 | async-start | bytes 589824 | tf_op jit(solution)/shard_map/reduce_scatter | solution.py:105
  142.9 6.1 %copy-start.1 = (bf16[1,1024,512]{2,1,0:T(8,128)(2,1)}, bf16[1,1024,512]{2,1,0:T(8,128)(2,1)S(1)}, u32[]{:S(2)}) copy-start(bf16[1,1024,512]{2,1,0:T(8,128)(2,1)S(1)} %fusion.16) | copy-start | bytes 3145732
  142.9 7.5 %copy-start.3 = (bf16[1,1024,256]{1,2,0:T(8,128)(2,1)S(1)}, bf16[1,1024,256]{1,2,0:T(8,128)(2,1)}, u32[]{:S(2)}) copy-start(bf16[1,1024,256]{1,2,0:T(8,128)(2,1)} %all-gather) | copy-start | bytes 1572868
  150.3 94.1 %reduce-scatter.6.cloned.1.call-start = ((), (), s32[]{:S(2)}) async-start(), calls=%async_computation.5 | async-start | bytes 589824 | tf_op jit(solution)/shard_map/reduce_scatter | solution.py:104
Sparse Core Ops, SparseCore 0:
  71.4 55.6 all-reduce.2
  140.8 27.8 reduce-scatter.3
  172.6 34.1 reduce-scatter.7
  210.3 34.0 reduce-scatter.5
where the time goes:
time: 252 us; the launch traced here: 251 us
  waiting for transfers between devices  96.8 us (38%)
  blocking collectives  72.4 us (29%)
  matrix products  36.6 us (15%)
  other arithmetic  19.2 us (8%)
  between operations  14 us (6%)
  local copies, waits for them, and re-layouts  11.6 us (5%)
    reduce_scatter x1, waiting for transfers between devices, per_device(): lax.psum_scatter(key_part, ('dp', 'seq'), scatter_dimension=0, tiled=True)  37.6 us
    reduce_scatter x1, waiting for transfers between devices, per_device(): lax.psum_scatter(value_part, ('dp', 'seq'), scatter_dimension=0, tiled=True)  32 us
    psum x1, waiting for transfers between devices, per_device(): summed, total = lax.psum((part_out, part_norm), 'seq')  27.2 us
    all_gather x1, blocking collectives, per_device(): lax.all_gather(queries[0], 'seq', axis=0, tiled=True)  15.7 us
    psum x1, blocking collectives, per_device(): slope_grad = lax.psum(slope_part, ('dp', 'seq'))  14.8 us
    all_gather x1, blocking collectives, per_device(): lax.all_gather(cotangent[0], 'seq', axis=0, tiled=True)  14.6 us
    psum x1, blocking collectives, per_device(): summed, total = lax.psum((part_out, part_norm), 'seq')  9.46 us
    pmax x1, blocking collectives, per_device(): top = lax.pmax(jnp.max(score, axis=2), 'seq')  9.13 us
  transfers between devices with their start and end apart: 4, of which 3 were waited for; matrix products, arithmetic and copies ran while one was open for 9% of the time, Pallas kernels for 0%

commit v1 on v0

--- a/solution.py
+++ b/solution.py
@@ -1,10 +1,438 @@
+import functools
+
 import jax
 import jax.numpy as jnp
 from jax import lax
+from jax.experimental import pallas as pl
+from jax.experimental.pallas import tpu as pltpu
 from jax.sharding import PartitionSpec as P
 
 HEAD = 128
 BLOCK = 128
+LOG2E = 1.4426950408889634
+CODE_MAX = 32000.0
+TINY = 1e-30
+CHUNK = 256
+
+F32 = jnp.float32
+BF16 = jnp.bfloat16
+I16 = jnp.int16
+VMEM = pl.BlockSpec(memory_space=pltpu.VMEM)
+SMEM = pl.BlockSpec(memory_space=pltpu.SMEM)
+
+
+def nn(a, b):
+    return lax.dot_general(a, b, (((1,), (0,)), ((), ())), preferred_element_type=F32)
+
+
+def nt(a, b):
+    return lax.dot_general(a, b, (((1,), (1,)), ((), ())), preferred_element_type=F32)
+
+
+def tn(a, b):
+    return lax.dot_general(a, b, (((0,), (0,)), ((), ())), preferred_element_type=F32)
+
+
+def head_cols(h):
+    return slice(h * HEAD, (h + 1) * HEAD)
+
+
+def swap(x, axis, k, n):
+    return lax.ppermute(x, axis, [(i, i ^ k) for i in range(n)])
+
+
+def encode(x):
+    most = jnp.maximum(jnp.max(jnp.abs(x), axis=0, keepdims=True), TINY)
+    exponent = jnp.ceil(jnp.log2(most))
+    steps = jnp.round(x * (jnp.exp2(-exponent) * CODE_MAX))
+    return steps, exponent
+
+
+def decode(steps, exponent):
+    return steps.astype(jnp.int32).astype(F32) * (jnp.exp2(exponent.astype(jnp.int32).astype(F32)) * (1.0 / CODE_MAX))
+
+
+def to_code(x):
+    return x.astype(jnp.int32).astype(I16)
+
+
+def stack_rows(rows, total, width):
+    place = lax.broadcasted_iota(jnp.int32, (total, width), 0)
+    out = jnp.zeros((total, width), F32)
+    for i, row in enumerate(rows):
+        out = jnp.where(place == i, row, out)
+    return out
+
+
+def prep_kernel(tok_ref, lev_ref, table_ref, wk_ref, wv_ref, inp_ref, key_ref, val_ref):
+    table = table_ref[...]
+    hi = table.astype(BF16)
+    rest = table - hi.astype(F32)
+    mid = rest.astype(BF16)
+    low = (rest - mid.astype(F32)).astype(BF16)
+    levels = table.shape[0]
+    for c in range(tok_ref.shape[1] // CHUNK):
+        rows = slice(c * CHUNK, (c + 1) * CHUNK)
+        raw = tok_ref[0, rows, :].astype(F32)
+        centered = raw - jnp.mean(raw, axis=1, keepdims=True)
+        normed = centered / jnp.sqrt(jnp.mean(centered * centered, axis=1, keepdims=True) + 1e-05)
+        ids = lev_ref[0:1, rows]
+        pick = (lax.broadcasted_iota(jnp.int32, (levels, CHUNK), 0) == ids).astype(F32).astype(BF16)
+        lookup = (tn(pick, low) + tn(pick, mid)) + tn(pick, hi)
+        inputs = (normed + lookup).astype(BF16)
+        inp_ref[rows, :] = inputs
+        key_ref[rows, :] = nn(inputs, wk_ref[...]).astype(BF16)
+        val_ref[rows, :] = nn(inputs, wv_ref[...]).astype(BF16)
+
+
+def fill_episode(bounds_ref, episode_ref, base):
+    before = jnp.int32(0)
+    place = lax.broadcasted_iota(jnp.int32, (BLOCK, 128), 0)
+    for b in range(bounds_ref.shape[1]):
+        bound = bounds_ref[0, b]
+        local = before + (place >= bound).astype(jnp.int32)
+        episode_ref[b * BLOCK : (b + 1) * BLOCK, :] = base + local.astype(F32)
+        before = before + (bound < BLOCK).astype(jnp.int32)
+    return before
+
+
+def wide(column, width):
+    return jnp.concatenate([column] * (width // 128), axis=1)
+
+
+def top_kernel(n, bounds_ref, slopes_ref, key_ref, *refs):
+    q_refs, (stats_ref, episode_ref) = refs[:n], refs[n:]
+    rows = q_refs[0].shape[1]
+    tokens, width = key_ref.shape
+    heads = width // HEAD
+    starts = fill_episode(bounds_ref, episode_ref, 0.0)
+    scale = HEAD ** (-0.5)
+    tops = []
+    for h in range(heads):
+        for j in range(n):
+            best = None
+            query = q_refs[j][0, :, head_cols(h)]
+            for c in range(tokens // CHUNK):
+                part = slice(c * CHUNK, (c + 1) * CHUNK)
+                score = nt(key_ref[part, head_cols(h)], query) * scale
+                score = score + wide(slopes_ref[h] * episode_ref[part, :], rows)
+                most = jnp.max(score, axis=0, keepdims=True)
+                best = most if best is None else jnp.maximum(best, most)
+            tops.append(best)
+    tops.append(jnp.zeros((1, rows), F32) + starts.astype(F32))
+    stats_ref[...] = stack_rows(tops, stats_ref.shape[0], rows)
+
+
+def merged_tops(n, heads, slopes_ref, stats_refs):
+    me = lax.axis_index("seq")
+    counts = [ref[heads * n : heads * n + 1, :] for ref in stats_refs]
+    bases = []
+    for k in range(n):
+        base = jnp.zeros_like(counts[0])
+        for j in range(n):
+            earlier = ((me ^ j) < (me ^ k)).astype(F32)
+            base = base + earlier * counts[j]
+        bases.append(base)
+    tops = []
+    for h in range(heads):
+        row = []
+        for j in range(n):
+            best = None
+            for k in range(n):
+                place = h * n + (j ^ k)
+                top = stats_refs[k][place : place + 1, :] + slopes_ref[h] * bases[k]
+                best = top if best is None else jnp.maximum(best, top)
+            row.append(best)
+        tops.append(row)
+    return tops, bases[0]
+
+
+def gather_blocks(refs, scratch):
+    rows = refs[0].shape[1]
+    for j, ref in enumerate(refs):
+        scratch[j * rows : (j + 1) * rows, :] = ref[0]
+
+
+def sums_kernel(n, bounds_ref, slopes_ref, key_ref, val_ref, *refs):
+    q_refs, g_refs, top_refs = refs[:n], refs[n : 2 * n], refs[2 * n : 3 * n]
+    stats_ref, own_ref = refs[3 * n : 3 * n + 2]
+    send_refs = refs[3 * n + 2 : 4 * n + 1]
+    episode_ref, q_all, g_all, out_ref = refs[4 * n + 1 :]
+    rows = q_refs[0].shape[1]
+    tokens, width = key_ref.shape
+    heads = width // HEAD
+    scale = HEAD ** (-0.5)
+    tops, base = merged_tops(n, heads, slopes_ref, top_refs)
+    fill_episode(bounds_ref, episode_ref, base[:, :128])
+    gather_blocks(q_refs, q_all)
+    gather_blocks(g_refs, g_all)
+    lats = n * rows
+    norms, deltas = [], []
+    for h in range(heads):
+        top = jnp.concatenate(tops[h], axis=1)
+
+        def step(c, carry):
+            norm, delta = carry
+            part = pl.ds(pl.multiple_of(c * CHUNK, CHUNK), CHUNK)
+            keys, values = key_ref[part, head_cols(h)], val_ref[part, head_cols(h)]
+            score = nt(keys, q_all[:, head_cols(h)]) * scale
+            score = score + wide(slopes_ref[h] * episode_ref[part, :], lats)
+            expo = jnp.exp(score - top)
+            weights = expo.astype(BF16)
+            dprod = nt(values, g_all[:, head_cols(h)])
+            out_ref[...] += tn(values, weights)
+            norm = norm + jnp.sum(expo, axis=0, keepdims=True)
+            delta = delta + jnp.sum(weights.astype(F32) * dprod, axis=0, keepdims=True)
+            return norm, delta
+
+        out_ref[...] = jnp.zeros_like(out_ref)
+        zero = jnp.zeros((1, lats), F32)
+        norm, delta = lax.fori_loop(0, tokens // CHUNK, step, (zero, zero))
+        norms += [norm[:, j * rows : (j + 1) * rows] for j in range(n)]
+        deltas += [delta[:, j * rows : (j + 1) * rows] for j in range(n)]
+        own_ref[head_cols(h), :] = out_ref[:, :rows]
+        write_messages(h, n, rows, heads, out_ref, send_refs)
+    stats_ref[...] = stack_rows(norms + deltas, stats_ref.shape[0], rows)
+
+
+def write_messages(h, n, rows, heads, sums_ref, send_refs):
+    for j in range(1, n):
+        steps, exponent = encode(sums_ref[:, j * rows : (j + 1) * rows])
+        send_refs[j - 1][head_cols(h), :] = to_code(steps)
+        place = (heads + h * 0) * HEAD + h * 16
+        send_refs[j - 1][place : place + 16, :] = to_code(jnp.broadcast_to(exponent, (16, rows)))
+
+
+def read_message(ref, h, heads):
+    place = heads * HEAD + h * 16
+    return decode(ref[head_cols(h), :], ref[place : place + 16, :][0:1, :])
+
+
+def merged_sums(n, heads, stats_refs):
+    norms, deltas = [], []
+    for h in range(heads):
+        norm_row, delta_row = [], []
+        for j in range(n):
+            norm = delta = None
+            for k in range(n):
+                place = h * n + (j ^ k)
+                a = stats_refs[k][place : place + 1, :]
+                b = stats_refs[k][heads * n + place : heads * n + place + 1, :]
+                norm = a if norm is None else norm + a
+                delta = b if delta is None else delta + b
+            norm_row.append(norm)
+            delta_row.append(delta)
+        norms.append(jnp.concatenate(norm_row, axis=1))
+        deltas.append(jnp.concatenate(delta_row, axis=1))
+    return norms, deltas
+
+
+def grads_kernel(n, bounds_ref, slopes_ref, inp_ref, key_ref, val_ref, *refs):
+    q_refs, g_refs, top_refs, sum_refs = (refs[i * n : (i + 1) * n] for i in range(4))
+    own_ref, keep_ref, give_ref = refs[4 * n : 4 * n + 3]
+    send_refs = refs[4 * n + 3 : 5 * n + 2]
+    episode_ref, q_all, g_all, dq_ref, tok_ref, weight_ref = refs[5 * n + 2 :]
+    rows = q_refs[0].shape[1]
+    tokens, width = key_ref.shape
+    heads = width // HEAD
+    scale = HEAD ** (-0.5)
+    tops, base = merged_tops(n, heads, slopes_ref, top_refs)
+    norms, deltas = merged_sums(n, heads, sum_refs)
+    fill_episode(bounds_ref, episode_ref, base[:, :128])
+    gather_blocks(q_refs, q_all)
+    gather_blocks(g_refs, g_all)
+    lats = n * rows
+    slope_rows = []
+    for h in range(heads):
+        top = jnp.concatenate(tops[h], axis=1)
+        inverse = 1.0 / norms[h]
+        mean = deltas[h] * inverse
+
+        def step(c, slope):
+            part = pl.ds(pl.multiple_of(c * CHUNK, CHUNK), CHUNK)
+            keys, values = key_ref[part, head_cols(h)], val_ref[part, head_cols(h)]
+            query, grad = q_all[:, head_cols(h)], g_all[:, head_cols(h)]
+            episode = wide(episode_ref[part, :], lats)
+            score = nt(keys, query) * scale
+            score = score + slopes_ref[h] * episode
+            probs = jnp.exp(score - top) * inverse
+            tok_ref[part, width + h * HEAD : width + (h + 1) * HEAD] = nn(probs.astype(BF16), grad).astype(BF16)
+            dprod = nt(values, grad)
+            score_grad = probs * (dprod - mean)
+            slope = slope + jnp.sum(score_grad * episode, axis=0, keepdims=True)
+            score_grad_b = score_grad.astype(BF16)
+            tok_ref[part, head_cols(h)] = (scale * nn(score_grad_b, query)).astype(BF16)
+            dq_ref[...] += tn(keys, score_grad_b)
+            return slope
+
+        dq_ref[...] = jnp.zeros_like(dq_ref)
+        slope = lax.fori_loop(0, tokens // CHUNK, step, jnp.zeros((1, lats), F32))
+        slope_rows.append(jnp.sum(slope, axis=1, keepdims=True))
+        own_ref[head_cols(h), :] = dq_ref[:, :rows]
+        write_messages(h, n, rows, heads, dq_ref, send_refs)
+    half = keep_ref.shape[0] - 8
+    weight_ref[0] = tn(inp_ref[:, :half], tok_ref[...])
+    weight_ref[1] = tn(inp_ref[:, half:], tok_ref[...])
+    core = lax.axis_index("dp")
+    keep_ref[:half, :] = weight_ref[core]
+    give_ref[:half, :] = weight_ref[1 - core]
+    columns = keep_ref.shape[1]
+    slopes = stack_rows([jnp.broadcast_to(s, (1, columns)) for s in slope_rows], 8, columns)
+    keep_ref[half:, :] = slopes
+    give_ref[half:, :] = slopes
+
+
+def pair_kernel(n, heads, keep_ref, got_ref, own_ref, *send_refs):
+    me = lax.axis_index("seq")
+    half = keep_ref.shape[0] - 8
+    piece = half // n
+    width = keep_ref.shape[1]
+    place = lax.broadcasted_iota(jnp.int32, (16, width), 0)
+    slopes = keep_ref[half:, :] + got_ref[half:, :]
+    digits = []
+    for h in range(heads):
+        value = slopes[h : h + 1, :]
+        steps, exponent = encode(value)
+        left = value * (jnp.exp2(-exponent) * CODE_MAX) - steps
+        digits += [exponent, steps, jnp.round(left * CODE_MAX)]
+    for k in range(n):
+        rows = pl.ds(pl.multiple_of((me ^ k) * piece, piece), piece)
+        total = keep_ref[rows, :] + got_ref[rows, :]
+        if k == 0:
+            own_ref[:piece, :] = total
+            own_ref[piece:, :] = slopes
+        else:
+            steps, exponent = encode(total)
+            send_refs[k - 1][:piece, :] = to_code(steps)
+            send_refs[k - 1][piece:, :] = to_code(stack_rows([exponent] + digits, 16, width))
+
+
+def attended_kernel(n, heads, own_ref, *refs):
+    got_refs, sum_refs, out_ref = refs[: n - 1], refs[n - 1 : 2 * n - 1], refs[2 * n - 1]
+    rows = own_ref.shape[1]
+    norms, _ = merged_sums(n, heads, sum_refs)
+    for h in range(heads):
+        total = own_ref[head_cols(h), :]
+        for ref in got_refs:
+            total = total + read_message(ref, h, heads)
+        total = total / norms[h][:, :rows]
+        out_ref[0, :, head_cols(h)] = total.T.astype(BF16)
+
+
+def last_kernel(n, heads, own_ref, weight_ref, *refs):
+    got_refs, part_refs = refs[: n - 1], refs[n - 1 : 2 * n - 2]
+    grad_ref, key_ref, val_ref, slope_ref = refs[2 * n - 2 :]
+    scale = HEAD ** (-0.5)
+    for h in range(heads):
+        total = own_ref[head_cols(h), :]
+        for ref in got_refs:
+            total = total + read_message(ref, h, heads)
+        grad_ref[0, :, head_cols(h)] = (scale * total).T.astype(BF16)
+    piece = weight_ref.shape[0] - 8
+    width = weight_ref.shape[1] // 2
+    total = weight_ref[:piece, :]
+    slopes = weight_ref[piece:, :]
+    place = lax.broadcasted_iota(jnp.int32, slopes.shape, 0)
+    for ref in part_refs:
+        extra = ref[piece:, :].astype(jnp.int32).astype(F32)
+        total = total + ref[:piece, :].astype(jnp.int32).astype(F32) * (jnp.exp2(extra[0:1, :]) * (1.0 / CODE_MAX))
+        for h in range(heads):
+            exponent, steps, left = (extra[1 + 3 * h + i : 2 + 3 * h + i, :] for i in range(3))
+            value = (steps + left * (1.0 / CODE_MAX)) * (jnp.exp2(exponent) * (1.0 / CODE_MAX))
+            slopes = jnp.where(place == h, slopes + value, slopes)
+    key_ref[...] = total[:, :width]
+    val_ref[...] = total[:, width:]
+    slope_ref[...] = slopes[:, :128]
+
+
+def call(kernel, name, outs, args, scratch=(), smem=0, limit=40 << 20):
+    return pl.pallas_call(
+        kernel,
+        out_shape=[jax.ShapeDtypeStruct(shape, dtype) for shape, dtype in outs],
+        in_specs=[SMEM] * smem + [VMEM] * (len(args) - smem),
+        out_specs=[VMEM] * len(outs),
+        scratch_shapes=list(scratch),
+        compiler_params=pltpu.CompilerParams(vmem_limit_bytes=limit),
+        name=name,
+    )(*args)
+
+
+def per_device_blocks(n, tokens, levels, boundaries, level_table, w_key, w_value, slopes, queries, cotangent):
+    toks, channels = tokens.shape[1:]
+    rows, width = queries.shape[1:]
+    heads = width // HEAD
+    lats = n * rows
+    peers = range(1, n)
+    q_all = [queries] + [swap(queries, "seq", k, n) for k in peers]
+    inputs, keys, values = call(
+        prep_kernel,
+        "prep",
+        [((toks, channels), BF16), ((toks, width), BF16), ((toks, width), BF16)],
+        (tokens, levels, level_table, w_key, w_value),
+    )
+    g_all = [cotangent] + [swap(cotangent, "seq", k, n) for k in peers]
+    episode = pltpu.VMEM((toks, 128), F32)
+    stat_rows = -(-(heads * n + 1) // 8) * 8
+    (top_own,) = call(
+        functools.partial(top_kernel, n),
+        "tops",
+        [((stat_rows, rows), F32)],
+        (boundaries, slopes, keys, *q_all),
+        [episode],
+        2,
+    )
+    tops = [top_own] + [swap(top_own, "seq", k, n) for k in peers]
+    message = ((heads * HEAD + 16 * heads, rows), I16)
+    blocks = pltpu.VMEM((lats, width), BF16)
+    sums = call(
+        functools.partial(sums_kernel, n),
+        "sums",
+        [((2 * heads * n, rows), F32), ((width, rows), F32)] + [message] * (n - 1),
+        (boundaries, slopes, keys, values, *q_all, *g_all, *tops),
+        [episode, blocks, blocks, pltpu.VMEM((HEAD, lats), F32)],
+        2,
+    )
+    norms = [sums[0]] + [swap(sums[0], "seq", k, n) for k in peers]
+    outs = [swap(sums[1 + k], "seq", k, n) for k in peers]
+    half = channels // 2
+    grads = call(
+        functools.partial(grads_kernel, n),
+        "grads",
+        [((width, rows), F32)] + [((half + 8, 2 * width), F32)] * 2 + [message] * (n - 1),
+        (boundaries, slopes, inputs, keys, values, *q_all, *g_all, *tops, *norms),
+        [
+            episode,
+            blocks,
+            blocks,
+            pltpu.VMEM((HEAD, lats), F32),
+            pltpu.VMEM((toks, 2 * width), BF16),
+            pltpu.VMEM((2, half, 2 * width), F32),
+        ],
+        2,
+    )
+    got = swap(grads[2], "dp", 1, 2)
+    dqs = [swap(grads[2 + k], "seq", k, n) for k in peers]
+    (attended,) = call(
+        functools.partial(attended_kernel, n, heads),
+        "attended",
+        [((1, rows, width), BF16)],
+        (sums[1], *outs, *norms),
+    )
+    piece = half // n
+    pair = call(
+        functools.partial(pair_kernel, n, heads),
+        "pair",
+        [((piece + 8, 2 * width), F32)] + [((piece + 16, 2 * width), I16)] * (n - 1),
+        (grads[1], got),
+    )
+    parts = [swap(pair[k], "seq", k, n) for k in peers]
+    query_grad, key_grad, value_grad, slope_grad = call(
+        functools.partial(last_kernel, n, heads),
+        "last",
+        [((1, rows, width), BF16), ((piece, width), F32), ((piece, width), F32), ((8, 128), F32)],
+        (grads[0], pair[0], *dqs, *parts),
+    )
+    return attended, query_grad, key_grad, value_grad, slope_grad[:heads, 0]
 
 
 def carried_in(part, axis, combine, identity):
@@ -22,7 +450,7 @@
     return earlier + later
 
 
-def per_device(tokens, levels, boundaries, level_table, w_key, w_value, slopes, queries, cotangent):
+def per_device_general(tokens, levels, boundaries, level_table, w_key, w_value, slopes, queries, cotangent):
     scale = HEAD ** (-0.5)
     raw = tokens[0].astype(jnp.float32)
     centered = raw - jnp.mean(raw, axis=1, keepdims=True)
@@ -109,6 +537,14 @@
 
 
 def solution(mesh):
+    n = mesh.shape["seq"]
+
+    def per_device(*args):
+        rows = args[7].shape[1]
+        if n in (2, 4, 8) and mesh.shape["dp"] == 2 and rows % 128 == 0:
+            return per_device_blocks(n, *args)
+        return per_device_general(*args)
+
     return jax.shard_map(
         per_device,
         mesh=mesh,

time: 252 us -> 70.3 us (0.28)
  waiting for transfers between devices: 96.8 us -> 15.3 us
  blocking collectives: 72.4 us -> 0 us
  matrix products: 36.6 us -> 0 us
  starting transfers between devices: 0.34 us -> 27 us
  Pallas kernels: 0 us -> 20.8 us
  other arithmetic: 19.2 us -> 0 us
  between operations: 14 us -> 0.77 us
  local copies, waits for them, and re-layouts: 11.6 us -> 6.11 us
    reduce_scatter x3 -> x0, waiting for transfers between devices: 69.6 us -> none  [the longest x1 37.6 us: per_device(): lax.psum_scatter(key_part, ('dp', 'seq'), scatter_dimension=0, tiled=True)]
    dot_general x10 -> x0, matrix products: 36.6 us -> none  [the longest x1 6.48 us: per_device(): jnp.einsum('hnt,thd->nhd', expo.astype(jnp.bfloat16), value_heads, prefer...]
    all_gather x2 -> x0, blocking collectives: 30.3 us -> none  [the longest x1 15.7 us: per_device(): lax.all_gather(queries[0], 'seq', axis=0, tiled=True)]
    psum x1 -> x0, waiting for transfers between devices: 27.2 us -> none  [per_device(): summed, total = lax.psum((part_out, part_norm), 'seq')]
    ppermute x0 -> x22, starting transfers between devices: none -> 27 us  [swap(): return lax.ppermute(x, axis, [(i, i ^ k) for i in range(n)])]
    psum x2 -> x0, blocking collectives: 24.2 us -> none  [the longest x1 14.8 us: per_device(): slope_grad = lax.psum(slope_part, ('dp', 'seq'))]
    pallas_call x0 -> x7, Pallas kernels: none -> 20.8 us  [call(): pl.pallas_call(kernel, out_shape=[jax.ShapeDtypeStruct(shape, dtype) for...]
    ppermute x0 -> x22, waiting for transfers between devices: none -> 15.3 us  [swap(): return lax.ppermute(x, axis, [(i, i ^ k) for i in range(n)])]
  transfers between devices with their start and end apart: 4 -> 22, of which waited for: 3 -> 11; matrix products, arithmetic and copies ran while one was open for 9% -> 0% of each run, Pallas kernels for 0% -> 7%
where the time goes in v1:
time: 70.3 us; the launch traced here: 70 us
  starting transfers between devices  27 us (38%)
  Pallas kernels  20.8 us (30%)
  waiting for transfers between devices  15.3 us (22%)
  local copies, waits for them, and re-layouts  6.11 us (9%)
  between operations  0.77 us (1%)
    ppermute x22, starting transfers between devices, swap(): return lax.ppermute(x, axis, [(i, i ^ k) for i in range(n)])  27 us
    pallas_call x7, Pallas kernels, call(): pl.pallas_call(kernel, out_shape=[jax.ShapeDtypeStruct(shape, dtype) for...  20.8 us
    ppermute x22, waiting for transfers between devices, swap(): return lax.ppermute(x, axis, [(i, i ^ k) for i in range(n)])  15.3 us
    unnamed x18, local copies, waits for them, and re-layouts  5.49 us
  transfers between devices with their start and end apart: 22, of which 11 were waited for; matrix products, arithmetic and copies ran while one was open for 0% of the time, Pallas kernels for 7%

profile of v1, /device:TPU:0, one launch (start us, length us, event | category | flops | bytes accessed | tf_op | source)
XLA Modules:
  0.0 70.0 jit_solution(4853471666226245913)
XLA Ops:
  0.6 0.0 copy-start
  0.6 3.0 %collective-permute-start = (bf16[1,256,256]{2,1,0:T(8,128)(2,1)}, bf16[1,256,256]{2,1,0:T(8,128)(2,1)S(1)}, u32[]{:S(2)}, u32[]{:S(2)}) collective-permute-start(bf16[1,256,256]{2,1,0:T(8,128)(2,1)} %refs_0_.5), channel_id=1, source_target_pairs={{0,4},{4,0},{8,12},{12,8},{1,5},{5,1},{9,13},{13,9},{2,6},{6,2},{1... | collective-permute-start | bytes 393224 | tf_op jit(solution)/shard_map/ppermute | solution.py:41
  3.6 1.5 %collective-permute-start.1 = (bf16[1,256,256]{2,1,0:T(8,128)(2,1)}, bf16[1,256,256]{2,1,0:T(8,128)(2,1)S(1)}, u32[]{:S(2)}, u32[]{:S(2)}) collective-permute-start(bf16[1,256,256]{2,1,0:T(8,128)(2,1)} %refs_0_.5), channel_id=1, source_target_pairs={{0,8},{4,12},{8,0},{12,4},{1,9},{5,13},{9,1},{13,5},{2,10},{6,14},... | collective-permute-start | bytes 393224 | tf_op jit(solution)/shard_map/ppermute | solution.py:41
  5.2 0.0 collective-permute-start.2
  5.2 1.9 %collective-permute-start.3 = (bf16[1,256,256]{2,1,0:T(8,128)(2,1)}, bf16[1,256,256]{2,1,0:T(8,128)(2,1)S(1)}, u32[]{:S(2)}, u32[]{:S(2)}) collective-permute-start(bf16[1,256,256]{2,1,0:T(8,128)(2,1)} %refs_4_.3), channel_id=1, source_target_pairs={{0,4},{4,0},{8,12},{12,8},{1,5},{5,1},{9,13},{13,9},{2,6},{6,2},{1... | collective-permute-start | bytes 393224 | tf_op jit(solution)/shard_map/ppermute | solution.py:41
  7.1 1.5 %collective-permute-start.4 = (bf16[1,256,256]{2,1,0:T(8,128)(2,1)}, bf16[1,256,256]{2,1,0:T(8,128)(2,1)S(1)}, u32[]{:S(2)}, u32[]{:S(2)}) collective-permute-start(bf16[1,256,256]{2,1,0:T(8,128)(2,1)} %refs_4_.3), channel_id=1, source_target_pairs={{0,8},{4,12},{8,0},{12,4},{1,9},{5,13},{9,1},{13,5},{2,10},{6,14},... | collective-permute-start | bytes 393224 | tf_op jit(solution)/shard_map/ppermute | solution.py:41
  8.7 0.0 collective-permute-done.refs_1_
  8.7 2.5 %collective-permute-start.5 = (bf16[1,256,256]{2,1,0:T(8,128)(2,1)}, bf16[1,256,256]{2,1,0:T(8,128)(2,1)S(1)}, u32[]{:S(2)}, u32[]{:S(2)}) collective-permute-start(bf16[1,256,256]{2,1,0:T(8,128)(2,1)} %refs_4_.3), channel_id=1, source_target_pairs={{0,12},{4,8},{8,4},{12,0},{1,13},{5,9},{9,5},{13,1},{2,14},{6,10},... | collective-permute-start | bytes 393224 | tf_op jit(solution)/shard_map/ppermute | solution.py:41
  11.2 1.2 %copy-done.1 = bf16[1,1024,512]{2,1,0:T(8,128)(2,1)S(1)} copy-done((bf16[1,1024,512]{2,1,0:T(8,128)(2,1)S(1)}, bf16[1,1024,512]{2,1,0:T(8,128)(2,1)}, u32[]{:S(2)}) %copy-start.1) | copy-done | bytes 1048600
  12.4 1.0 %copy-done.2 = f32[256,512]{1,0:T(8,128)S(1)} copy-done((f32[256,512]{1,0:T(8,128)S(1)}, f32[256,512]{1,0:T(8,128)}, u32[]{:S(2)}) %copy-start.2) | copy-done | bytes 524312
  13.5 0.9 %copy-done.4 = bf16[512,256]{1,0:T(8,128)(2,1)S(1)} copy-done((bf16[512,256]{1,0:T(8,128)(2,1)S(1)}, bf16[512,256]{1,0:T(8,128)(2,1)}, u32[]{:S(2)}) %copy-start.4) | copy-done | bytes 262168
  14.4 0.9 %copy-done.5 = bf16[512,256]{1,0:T(8,128)(2,1)S(1)} copy-done((bf16[512,256]{1,0:T(8,128)(2,1)S(1)}, bf16[512,256]{1,0:T(8,128)(2,1)}, u32[]{:S(2)}) %copy-start.5) | copy-done | bytes 262168
  15.4 0.7 copy-done.8
  16.1 2.0 %prep.1 = (bf16[1024,512]{1,0:T(8,128)(2,1)S(1)}, bf16[1024,256]{1,0:T(8,128)(2,1)S(1)}, bf16[1024,256]{1,0:T(8,128)(2,1)S(1)}) custom-call(bf16[1,1024,512]{2,1,0:T(8,128)(2,1)S(1)} %copy-done.1, s32[1,1024]{1,0:T(1,128)S(1)} %copy-done.8, f32[256,512]{1,0:T(8,128)S(1)} %copy-done.2, bf16[512,256]{1,0:T(8,128)(2,1)S(1)} %copy-done.4, ...), custom_call_target="tpu_custom_call" | custom-call | tf_op jit(solution)/shard_map/prep/pallas_call | solution.py:349
  18.1 0.0 copy-start.6
  18.1 0.0 copy-start.7
  18.1 0.0 collective-permute-done.1.refs_2_
  18.1 0.0 collective-permute-done.2.refs_3_
  18.1 0.0 copy-done
  18.1 0.6 copy-done.6
  18.7 0.0 copy-done.7
  18.7 1.9 %tops.1.refs_8_ = f32[16,256]{1,0:T(8,128)S(1)} custom-call(s32[1,8]{1,0:T(1,128)S(1)} %copy-done.6, f32[2]{0:T(128)S(1)} %copy-done.7, bf16[1024,256]{1,0:T(8,128)(2,1)S(1)} %get-tuple-element.27.key_ref, bf16[1,256,256]{2,1,0:T(8,128)(2,1)S(1)} %copy-done, bf16[1,256,256]{2,1,0:T(8,128)(2,1)S(1)} %collective-permute-done.refs_1_, ...), custom_call_target="tpu_custom_call" | custom-call | tf_op jit(solution)/shard_map/tops/pallas_call | solution.py:349
  20.6 0.1 collective-permute-start.6
  20.7 1.0 %collective-permute-start.7 = (f32[16,256]{1,0:T(8,128)S(1)}, f32[16,256]{1,0:T(8,128)S(1)}, u32[]{:S(2)}, u32[]{:S(2)}) collective-permute-start(f32[16,256]{1,0:T(8,128)S(1)} %tops.1.refs_8_), channel_id=1, source_target_pairs={{0,8},{4,12},{8,0},{12,4},{1,9},{5,13},{9,1},{13,5},{2,10},{6,14},... | collective-permute-start | bytes 49160 | tf_op jit(solution)/shard_map/ppermute | solution.py:41
  21.7 0.0 collective-permute-done.3.refs_5_
  21.7 2.5 %collective-permute-start.8 = (f32[16,256]{1,0:T(8,128)S(1)}, f32[16,256]{1,0:T(8,128)S(1)}, u32[]{:S(2)}, u32[]{:S(2)}) collective-permute-start(f32[16,256]{1,0:T(8,128)S(1)} %tops.1.refs_8_), channel_id=1, source_target_pairs={{0,12},{4,8},{8,4},{12,0},{1,13},{5,9},{9,5},{13,1},{2,14},{6,10},... | collective-permute-start | bytes 49160 | tf_op jit(solution)/shard_map/ppermute | solution.py:41
  24.2 0.0 collective-permute-done.4.refs_6_
  24.2 0.0 collective-permute-done.5.refs_7_
  24.2 0.2 collective-permute-done.6.refs_9_
  24.4 0.1 collective-permute-done.7.refs_10_
  24.5 1.8 %collective-permute-done.8.refs_11_ = f32[16,256]{1,0:T(8,128)S(1)} collective-permute-done((f32[16,256]{1,0:T(8,128)S(1)}, f32[16,256]{1,0:T(8,128)S(1)}, u32[]{:S(2)}, u32[]{:S(2)}) %collective-permute-start.8) | collective-permute-done | bytes 16416 | tf_op jit(solution)/shard_map/ppermute | solution.py:41
  26.3 0.0 copy-done.3
  26.3 6.0 %sums.1 = (f32[16,256]{1,0:T(8,128)S(1)}, f32[256,256]{1,0:T(8,128)S(1)}, s16[288,256]{1,0:T(8,128)(2,1)S(1)}, s16[288,256]{1,0:T(8,128)(2,1)S(1)}, s16[288,256]{1,0:T(8,128)(2,1)S(1)}) custom-call(s32[1,8]{1,0:T(1,128)S(1)} %copy-done.6, f32[2]{0:T(128)S(1)} %copy-done.7, bf16[1024,256]{1,0:T(8,128)(2,1)S(1)} %get-tuple-element.27.key_ref, ...), custom_call_target="tpu_custom_call" | custom-call | tf_op jit(solution)/shard_map/sums/pallas_call | solution.py:349
  32.3 1.6 %collective-permute-start.12 = (f32[16,256]{1,0:T(8,128)S(1)}, f32[16,256]{1,0:T(8,128)S(1)}, u32[]{:S(2)}, u32[]{:S(2)}) collective-permute-start(f32[16,256]{1,0:T(8,128)S(1)} %get-tuple-element.33.refs_3_.refs_12_), channel_id=1, source_target_pairs={{0,4},{4,0},{8,12},{12,8},{1,5},{5,1},{9,13},{13,9},{2,6},{6,2},{1... | collective-permute-start | bytes 49160 | tf_op jit(solution)/shard_map/ppermute | solution.py:41
  34.0 1.5 %collective-permute-start.13 = (f32[16,256]{1,0:T(8,128)S(1)}, f32[16,256]{1,0:T(8,128)S(1)}, u32[]{:S(2)}, u32[]{:S(2)}) collective-permute-start(f32[16,256]{1,0:T(8,128)S(1)} %get-tuple-element.33.refs_3_.refs_12_), channel_id=1, source_target_pairs={{0,8},{4,12},{8,0},{12,4},{1,9},{5,13},{9,1},{13,5},{2,10},{6,14},... | collective-permute-start | bytes 49160 | tf_op jit(solution)/shard_map/ppermute | solution.py:41
  35.5 0.4 collective-permute-start.14
  35.9 0.2 collective-permute-done.12.refs_4_.refs_13_
  36.1 1.6 %collective-permute-done.13.refs_5_.refs_14_ = f32[16,256]{1,0:T(8,128)S(1)} collective-permute-done((f32[16,256]{1,0:T(8,128)S(1)}, f32[16,256]{1,0:T(8,128)S(1)}, u32[]{:S(2)}, u32[]{:S(2)}) %collective-permute-start.13) | collective-permute-done | bytes 16416 | tf_op jit(solution)/shard_map/ppermute | solution.py:41
  37.7 2.4 %collective-permute-done.14.refs_6_.refs_15_ = f32[16,256]{1,0:T(8,128)S(1)} collective-permute-done((f32[16,256]{1,0:T(8,128)S(1)}, f32[16,256]{1,0:T(8,128)S(1)}, u32[]{:S(2)}, u32[]{:S(2)}) %collective-permute-start.14) | collective-permute-done | bytes 16416 | tf_op jit(solution)/shard_map/ppermute | solution.py:41
  40.1 9.1 %grads.1 = (f32[256,256]{1,0:T(8,128)S(1)}, f32[264,512]{1,0:T(8,128)S(1)}, f32[264,512]{1,0:T(8,128)S(1)}, s16[288,256]{1,0:T(8,128)(2,1)S(1)}, s16[288,256]{1,...) custom-call(s32[1,8]{1,0:T(1,128)S(1)} %copy-done.6, f32[2]{0:T(128)S(1)} %copy-done.7, ...), custom_call_target="tpu_custom_call" | custom-call | tf_op jit(solution)/shard_map/grads/pallas_call | solution.py:349
  49.2 0.1 collective-permute-start.15
  49.3 0.1 collective-permute-start.9
  49.4 0.9 %collective-permute-start.10 = (s16[288,256]{1,0:T(8,128)(2,1)S(1)}, s16[288,256]{1,0:T(8,128)(2,1)S(1)}, u32[]{:S(2)}, u32[]{:S(2)}) collective-permute-start(s16[288,256]{1,0:T(8,128)(2,1)S(1)} %get-tuple-element.31), channel_id=1, source_target_pairs={{0,8},{4,12},{8,0},{12,4},{1,9},{5,13},{9,1},{13,5},{2,10},{6,14},... | collective-permute-start | bytes 442376 | tf_op jit(solution)/shard_map/ppermute | solution.py:41
  50.3 2.5 %collective-permute-start.11 = (s16[288,256]{1,0:T(8,128)(2,1)S(1)}, s16[288,256]{1,0:T(8,128)(2,1)S(1)}, u32[]{:S(2)}, u32[]{:S(2)}) collective-permute-start(s16[288,256]{1,0:T(8,128)(2,1)S(1)} %get-tuple-element.32), channel_id=1, source_target_pairs={{0,12},{4,8},{8,4},{12,0},{1,13},{5,9},{9,5},{13,1},{2,14},{6,10},... | collective-permute-start | bytes 442376 | tf_op jit(solution)/shard_map/ppermute | solution.py:41
  52.8 0.1 collective-permute-start.16
  52.9 3.1 %collective-permute-done.9.refs_0_ = s16[288,256]{1,0:T(8,128)(2,1)S(1)} collective-permute-done((s16[288,256]{1,0:T(8,128)(2,1)S(1)}, s16[288,256]{1,0:T(8,128)(2,1)S(1)}, u32[]{:S(2)}, u32[]{:S(2)}) %collective-permute-start.9) | collective-permute-done | bytes 147488 | tf_op jit(solution)/shard_map/ppermute | solution.py:41
  56.0 0.5 collective-permute-start.17
  56.5 0.0 collective-permute-done.15.got_ref
  56.5 1.1 %collective-permute-start.18 = (s16[288,256]{1,0:T(8,128)(2,1)S(1)}, s16[288,256]{1,0:T(8,128)(2,1)S(1)}, u32[]{:S(2)}, u32[]{:S(2)}) collective-permute-start(s16[288,256]{1,0:T(8,128)(2,1)S(1)} %get-tuple-element.41), channel_id=1, source_target_pairs={{0,12},{4,8},{8,4},{12,0},{1,13},{5,9},{9,5},{13,1},{2,14},{6,10},... | collective-permute-start | bytes 442376 | tf_op jit(solution)/shard_map/ppermute | solution.py:41
  57.6 0.1 pair.1
  57.7 0.0 collective-permute-done.10.refs_1_
  57.8 3.5 %collective-permute-start.19 = (s16[80,512]{1,0:T(8,128)(2,1)S(1)}, s16[80,512]{1,0:T(8,128)(2,1)S(1)}, u32[]{:S(2)}, u32[]{:S(2)}) collective-permute-start(s16[80,512]{1,0:T(8,128)(2,1)S(1)} %get-tuple-element.42), channel_id=1, source_target_pairs={{0,4},{4,0},{8,12},{12,8},{1,5},{5,1},{9,13},{13,9},{2,6},{6,2},{1... | collective-permute-start | bytes 245768 | tf_op jit(solution)/shard_map/ppermute | solution.py:41
  61.2 0.0 collective-permute-done.11.refs_2_
  61.2 0.1 collective-permute-start.20
  61.3 1.0 %collective-permute-done.16.refs_0_ = s16[288,256]{1,0:T(8,128)(2,1)S(1)} collective-permute-done((s16[288,256]{1,0:T(8,128)(2,1)S(1)}, s16[288,256]{1,0:T(8,128)(2,1)S(1)}, u32[]{:S(2)}, u32[]{:S(2)}) %collective-permute-start.16) | collective-permute-done | bytes 147488 | tf_op jit(solution)/shard_map/ppermute | solution.py:41
  62.3 0.5 collective-permute-start.21
  62.8 0.9 %attended.1 = bf16[1,256,256]{2,1,0:T(8,128)(2,1)} custom-call(f32[256,256]{1,0:T(8,128)S(1)} %get-tuple-element.29.own_ref, s16[288,256]{1,0:T(8,128)(2,1)S(1)} %collective-permute-done.9.refs_0_, s16[288,256]{1,0:T(8,128)(2,1)S(1)} %collective-permute-done.10.refs_1_, s16[288,256]{1,0:T(8,128)(2,1)S(1)} %collective-permute-done.11.refs_2_, ...), custom_call_target="tpu_custom_call" | custom-call | tf_op jit(solution)/shard_map/attended/pallas_call | solution.py:349
  63.6 0.0 collective-permute-done.17.refs_1_
  63.6 1.9 %collective-permute-done.18.refs_2_ = s16[288,256]{1,0:T(8,128)(2,1)S(1)} collective-permute-done((s16[288,256]{1,0:T(8,128)(2,1)S(1)}, s16[288,256]{1,0:T(8,128)(2,1)S(1)}, u32[]{:S(2)}, u32[]{:S(2)}) %collective-permute-start.18) | collective-permute-done | bytes 147488 | tf_op jit(solution)/shard_map/ppermute | solution.py:41
  65.5 1.8 %collective-permute-done.19.refs_3_ = s16[80,512]{1,0:T(8,128)(2,1)S(1)} collective-permute-done((s16[80,512]{1,0:T(8,128)(2,1)S(1)}, s16[80,512]{1,0:T(8,128)(2,1)S(1)}, u32[]{:S(2)}, u32[]{:S(2)}) %collective-permute-start.19) | collective-permute-done | bytes 81952 | tf_op jit(solution)/shard_map/ppermute | solution.py:41
  67.3 0.0 collective-permute-done.20.refs_4_
  67.3 1.3 %collective-permute-done.21.refs_5_ = s16[80,512]{1,0:T(8,128)(2,1)S(1)} collective-permute-done((s16[80,512]{1,0:T(8,128)(2,1)S(1)}, s16[80,512]{1,0:T(8,128)(2,1)S(1)}, u32[]{:S(2)}, u32[]{:S(2)}) %collective-permute-start.21) | collective-permute-done | bytes 81952 | tf_op jit(solution)/shard_map/ppermute | solution.py:41
  68.5 0.9 %last.1 = (bf16[1,256,256]{2,1,0:T(8,128)(2,1)}, f32[64,256]{1,0:T(8,128)}, f32[64,256]{1,0:T(8,128)}, f32[8,128]{1,0:T(8,128)S(1)}) custom-call(f32[256,256]{1,0:T(8,128)S(1)} %get-tuple-element.35.own_ref, f32[72,512]{1,0:T(8,128)S(1)} %get-tuple-element.38.weight_ref, s16[288,256]{1,0:T(8,128)(2,1)S(1)} %collective-permute-done.16.refs_0_, ...), custom_call_target="tpu_custom_call" | custom-call | tf_op jit(solution)/shard_map/last/pallas_call | solution.py:349
  69.4 0.6 slice_reduce_fusion
  (6 shorter events, 0.0 us)
Async XLA Ops:
  0.6 17.5 %copy-start = (bf16[1,256,256]{2,1,0:T(8,128)(2,1)S(1)}, bf16[1,256,256]{2,1,0:T(8,128)(2,1)}, u32[]{:S(2)}) copy-start(bf16[1,256,256]{2,1,0:T(8,128)(2,1)} %refs_0_.5) | copy-start | bytes 393220
  0.6 8.0 %collective-permute-start = (bf16[1,256,256]{2,1,0:T(8,128)(2,1)}, bf16[1,256,256]{2,1,0:T(8,128)(2,1)S(1)}, u32[]{:S(2)}, u32[]{:S(2)}) collective-permute-start(bf16[1,256,256]{2,1,0:T(8,128)(2,1)} %refs_0_.5), channel_id=1, source_target_pairs={{0,4},{4,0},{8,12},{12,8},{1,5},{5,1},{9,13},{13,9},{2,6},{6,2},{1... | collective-permute-start | bytes 393224 | tf_op jit(solution)/shard_map/ppermute | solution.py:41
  3.6 14.4 %collective-permute-start.1 = (bf16[1,256,256]{2,1,0:T(8,128)(2,1)}, bf16[1,256,256]{2,1,0:T(8,128)(2,1)S(1)}, u32[]{:S(2)}, u32[]{:S(2)}) collective-permute-start(bf16[1,256,256]{2,1,0:T(8,128)(2,1)} %refs_0_.5), channel_id=1, source_target_pairs={{0,8},{4,12},{8,0},{12,4},{1,9},{5,13},{9,1},{13,5},{2,10},{6,14},... | collective-permute-start | bytes 393224 | tf_op jit(solution)/shard_map/ppermute | solution.py:41
  5.2 12.9 %collective-permute-start.2 = (bf16[1,256,256]{2,1,0:T(8,128)(2,1)}, bf16[1,256,256]{2,1,0:T(8,128)(2,1)S(1)}, u32[]{:S(2)}, u32[]{:S(2)}) collective-permute-start(bf16[1,256,256]{2,1,0:T(8,128)(2,1)} %refs_0_.5), channel_id=1, source_target_pairs={{0,12},{4,8},{8,4},{12,0},{1,13},{5,9},{9,5},{13,1},{2,14},{6,10},... | collective-permute-start | bytes 393224 | tf_op jit(solution)/shard_map/ppermute | solution.py:41
  5.2 16.5 %collective-permute-start.3 = (bf16[1,256,256]{2,1,0:T(8,128)(2,1)}, bf16[1,256,256]{2,1,0:T(8,128)(2,1)S(1)}, u32[]{:S(2)}, u32[]{:S(2)}) collective-permute-start(bf16[1,256,256]{2,1,0:T(8,128)(2,1)} %refs_4_.3), channel_id=1, source_target_pairs={{0,4},{4,0},{8,12},{12,8},{1,5},{5,1},{9,13},{13,9},{2,6},{6,2},{1... | collective-permute-start | bytes 393224 | tf_op jit(solution)/shard_map/ppermute | solution.py:41
  7.1 17.0 %collective-permute-start.4 = (bf16[1,256,256]{2,1,0:T(8,128)(2,1)}, bf16[1,256,256]{2,1,0:T(8,128)(2,1)S(1)}, u32[]{:S(2)}, u32[]{:S(2)}) collective-permute-start(bf16[1,256,256]{2,1,0:T(8,128)(2,1)} %refs_4_.3), channel_id=1, source_target_pairs={{0,8},{4,12},{8,0},{12,4},{1,9},{5,13},{9,1},{13,5},{2,10},{6,14},... | collective-permute-start | bytes 393224 | tf_op jit(solution)/shard_map/ppermute | solution.py:41
  8.7 15.5 %collective-permute-start.5 = (bf16[1,256,256]{2,1,0:T(8,128)(2,1)}, bf16[1,256,256]{2,1,0:T(8,128)(2,1)S(1)}, u32[]{:S(2)}, u32[]{:S(2)}) collective-permute-start(bf16[1,256,256]{2,1,0:T(8,128)(2,1)} %refs_4_.3), channel_id=1, source_target_pairs={{0,12},{4,8},{8,4},{12,0},{1,13},{5,9},{9,5},{13,1},{2,14},{6,10},... | collective-permute-start | bytes 393224 | tf_op jit(solution)/shard_map/ppermute | solution.py:41
  11.2 1.2 %copy-start.1 = (bf16[1,1024,512]{2,1,0:T(8,128)(2,1)S(1)}, bf16[1,1024,512]{2,1,0:T(8,128)(2,1)}, u32[]{:S(2)}) copy-start(bf16[1,1024,512]{2,1,0:T(8,128)(2,1)} %tok_ref.1) | copy-start | bytes 3145732
  12.4 1.0 %copy-start.2 = (f32[256,512]{1,0:T(8,128)S(1)}, f32[256,512]{1,0:T(8,128)}, u32[]{:S(2)}) copy-start(f32[256,512]{1,0:T(8,128)} %table_ref.1) | copy-start | bytes 1572868
  13.5 0.9 %copy-start.4 = (bf16[512,256]{1,0:T(8,128)(2,1)S(1)}, bf16[512,256]{1,0:T(8,128)(2,1)}, u32[]{:S(2)}) copy-start(bf16[512,256]{1,0:T(8,128)(2,1)} %wk_ref.1) | copy-start | bytes 786436
  14.4 0.9 %copy-start.5 = (bf16[512,256]{1,0:T(8,128)(2,1)S(1)}, bf16[512,256]{1,0:T(8,128)(2,1)}, u32[]{:S(2)}) copy-start(bf16[512,256]{1,0:T(8,128)(2,1)} %wv_ref.1) | copy-start | bytes 786436
  15.4 0.7 copy-start.8
  18.1 0.7 copy-start.6
  18.1 0.7 copy-start.7
  18.7 7.6 %copy-start.3 = (bf16[1,256,256]{2,1,0:T(8,128)(2,1)S(1)}, bf16[1,256,256]{2,1,0:T(8,128)(2,1)}, u32[]{:S(2)}) copy-start(bf16[1,256,256]{2,1,0:T(8,128)(2,1)} %refs_4_.3) | copy-start | bytes 393220
  20.6 3.8 %collective-permute-start.6 = (f32[16,256]{1,0:T(8,128)S(1)}, f32[16,256]{1,0:T(8,128)S(1)}, u32[]{:S(2)}, u32[]{:S(2)}) collective-permute-start(f32[16,256]{1,0:T(8,128)S(1)} %tops.1.refs_8_), channel_id=1, source_target_pairs={{0,4},{4,0},{8,12},{12,8},{1,5},{5,1},{9,13},{13,9},{2,6},{6,2},{1... | collective-permute-start | bytes 49160 | tf_op jit(solution)/shard_map/ppermute | solution.py:41
  20.7 3.8 %collective-permute-start.7 = (f32[16,256]{1,0:T(8,128)S(1)}, f32[16,256]{1,0:T(8,128)S(1)}, u32[]{:S(2)}, u32[]{:S(2)}) collective-permute-start(f32[16,256]{1,0:T(8,128)S(1)} %tops.1.refs_8_), channel_id=1, source_target_pairs={{0,8},{4,12},{8,0},{12,4},{1,9},{5,13},{9,1},{13,5},{2,10},{6,14},... | collective-permute-start | bytes 49160 | tf_op jit(solution)/shard_map/ppermute | solution.py:41
  21.7 4.6 %collective-permute-start.8 = (f32[16,256]{1,0:T(8,128)S(1)}, f32[16,256]{1,0:T(8,128)S(1)}, u32[]{:S(2)}, u32[]{:S(2)}) collective-permute-start(f32[16,256]{1,0:T(8,128)S(1)} %tops.1.refs_8_), channel_id=1, source_target_pairs={{0,12},{4,8},{8,4},{12,0},{1,13},{5,9},{9,5},{13,1},{2,14},{6,10},... | collective-permute-start | bytes 49160 | tf_op jit(solution)/shard_map/ppermute | solution.py:41
  32.3 3.8 %collective-permute-start.12 = (f32[16,256]{1,0:T(8,128)S(1)}, f32[16,256]{1,0:T(8,128)S(1)}, u32[]{:S(2)}, u32[]{:S(2)}) collective-permute-start(f32[16,256]{1,0:T(8,128)S(1)} %get-tuple-element.33.refs_3_.refs_12_), channel_id=1, source_target_pairs={{0,4},{4,0},{8,12},{12,8},{1,5},{5,1},{9,13},{13,9},{2,6},{6,2},{1... | collective-permute-start | bytes 49160 | tf_op jit(solution)/shard_map/ppermute | solution.py:41
  34.0 3.7 %collective-permute-start.13 = (f32[16,256]{1,0:T(8,128)S(1)}, f32[16,256]{1,0:T(8,128)S(1)}, u32[]{:S(2)}, u32[]{:S(2)}) collective-permute-start(f32[16,256]{1,0:T(8,128)S(1)} %get-tuple-element.33.refs_3_.refs_12_), channel_id=1, source_target_pairs={{0,8},{4,12},{8,0},{12,4},{1,9},{5,13},{9,1},{13,5},{2,10},{6,14},... | collective-permute-start | bytes 49160 | tf_op jit(solution)/shard_map/ppermute | solution.py:41
  35.5 4.6 %collective-permute-start.14 = (f32[16,256]{1,0:T(8,128)S(1)}, f32[16,256]{1,0:T(8,128)S(1)}, u32[]{:S(2)}, u32[]{:S(2)}) collective-permute-start(f32[16,256]{1,0:T(8,128)S(1)} %get-tuple-element.33.refs_3_.refs_12_), channel_id=1, source_target_pairs={{0,12},{4,8},{8,4},{12,0},{1,13},{5,9},{9,5},{13,1},{2,14},{6,10},... | collective-permute-start | bytes 49160 | tf_op jit(solution)/shard_map/ppermute | solution.py:41
  49.2 7.3 %collective-permute-start.15 = (f32[264,512]{1,0:T(8,128)S(1)}, f32[264,512]{1,0:T(8,128)S(1)}, u32[]{:S(2)}, u32[]{:S(2)}) collective-permute-start(f32[264,512]{1,0:T(8,128)S(1)} %get-tuple-element.37), channel_id=1, source_target_pairs={{0,16},{16,0},{1,17},{17,1},{2,18},{18,2},{3,19},{19,3},{4,20},{20... | collective-permute-start | bytes 1622024 | tf_op jit(solution)/shard_map/ppermute | solution.py:41
  49.3 6.7 %collective-permute-start.9 = (s16[288,256]{1,0:T(8,128)(2,1)S(1)}, s16[288,256]{1,0:T(8,128)(2,1)S(1)}, u32[]{:S(2)}, u32[]{:S(2)}) collective-permute-start(s16[288,256]{1,0:T(8,128)(2,1)S(1)} %get-tuple-element.30), channel_id=1, source_target_pairs={{0,4},{4,0},{8,12},{12,8},{1,5},{5,1},{9,13},{13,9},{2,6},{6,2},{1... | collective-permute-start | bytes 442376 | tf_op jit(solution)/shard_map/ppermute | solution.py:41
  49.4 8.3 %collective-permute-start.10 = (s16[288,256]{1,0:T(8,128)(2,1)S(1)}, s16[288,256]{1,0:T(8,128)(2,1)S(1)}, u32[]{:S(2)}, u32[]{:S(2)}) collective-permute-start(s16[288,256]{1,0:T(8,128)(2,1)S(1)} %get-tuple-element.31), channel_id=1, source_target_pairs={{0,8},{4,12},{8,0},{12,4},{1,9},{5,13},{9,1},{13,5},{2,10},{6,14},... | collective-permute-start | bytes 442376 | tf_op jit(solution)/shard_map/ppermute | solution.py:41
  50.3 10.9 %collective-permute-start.11 = (s16[288,256]{1,0:T(8,128)(2,1)S(1)}, s16[288,256]{1,0:T(8,128)(2,1)S(1)}, u32[]{:S(2)}, u32[]{:S(2)}) collective-permute-start(s16[288,256]{1,0:T(8,128)(2,1)S(1)} %get-tuple-element.32), channel_id=1, source_target_pairs={{0,12},{4,8},{8,4},{12,0},{1,13},{5,9},{9,5},{13,1},{2,14},{6,10},... | collective-permute-start | bytes 442376 | tf_op jit(solution)/shard_map/ppermute | solution.py:41
  52.8 9.5 %collective-permute-start.16 = (s16[288,256]{1,0:T(8,128)(2,1)S(1)}, s16[288,256]{1,0:T(8,128)(2,1)S(1)}, u32[]{:S(2)}, u32[]{:S(2)}) collective-permute-start(s16[288,256]{1,0:T(8,128)(2,1)S(1)} %get-tuple-element.39), channel_id=1, source_target_pairs={{0,4},{4,0},{8,12},{12,8},{1,5},{5,1},{9,13},{13,9},{2,6},{6,2},{1... | collective-permute-start | bytes 442376 | tf_op jit(solution)/shard_map/ppermute | solution.py:41
  56.0 7.6 %collective-permute-start.17 = (s16[288,256]{1,0:T(8,128)(2,1)S(1)}, s16[288,256]{1,0:T(8,128)(2,1)S(1)}, u32[]{:S(2)}, u32[]{:S(2)}) collective-permute-start(s16[288,256]{1,0:T(8,128)(2,1)S(1)} %get-tuple-element.40), channel_id=1, source_target_pairs={{0,8},{4,12},{8,0},{12,4},{1,9},{5,13},{9,1},{13,5},{2,10},{6,14},... | collective-permute-start | bytes 442376 | tf_op jit(solution)/shard_map/ppermute | solution.py:41
  56.5 9.0 %collective-permute-start.18 = (s16[288,256]{1,0:T(8,128)(2,1)S(1)}, s16[288,256]{1,0:T(8,128)(2,1)S(1)}, u32[]{:S(2)}, u32[]{:S(2)}) collective-permute-start(s16[288,256]{1,0:T(8,128)(2,1)S(1)} %get-tuple-element.41), channel_id=1, source_target_pairs={{0,12},{4,8},{8,4},{12,0},{1,13},{5,9},{9,5},{13,1},{2,14},{6,10},... | collective-permute-start | bytes 442376 | tf_op jit(solution)/shard_map/ppermute | solution.py:41
  57.8 9.5 %collective-permute-start.19 = (s16[80,512]{1,0:T(8,128)(2,1)S(1)}, s16[80,512]{1,0:T(8,128)(2,1)S(1)}, u32[]{:S(2)}, u32[]{:S(2)}) collective-permute-start(s16[80,512]{1,0:T(8,128)(2,1)S(1)} %get-tuple-element.42), channel_id=1, source_target_pairs={{0,4},{4,0},{8,12},{12,8},{1,5},{5,1},{9,13},{13,9},{2,6},{6,2},{1... | collective-permute-start | bytes 245768 | tf_op jit(solution)/shard_map/ppermute | solution.py:41
  61.2 6.0 %collective-permute-start.20 = (s16[80,512]{1,0:T(8,128)(2,1)S(1)}, s16[80,512]{1,0:T(8,128)(2,1)S(1)}, u32[]{:S(2)}, u32[]{:S(2)}) collective-permute-start(s16[80,512]{1,0:T(8,128)(2,1)S(1)} %get-tuple-element.43), channel_id=1, source_target_pairs={{0,8},{4,12},{8,0},{12,4},{1,9},{5,13},{9,1},{13,5},{2,10},{6,14},... | collective-permute-start | bytes 245768 | tf_op jit(solution)/shard_map/ppermute | solution.py:41
  62.3 6.2 %collective-permute-start.21 = (s16[80,512]{1,0:T(8,128)(2,1)S(1)}, s16[80,512]{1,0:T(8,128)(2,1)S(1)}, u32[]{:S(2)}, u32[]{:S(2)}) collective-permute-start(s16[80,512]{1,0:T(8,128)(2,1)S(1)} %get-tuple-element.44), channel_id=1, source_target_pairs={{0,12},{4,8},{8,4},{12,0},{1,13},{5,9},{9,5},{13,1},{2,14},{6,10},... | collective-permute-start | bytes 245768 | tf_op jit(solution)/shard_map/ppermute | solution.py:41

commit v2 on v1

--- a/solution.py
+++ b/solution.py
@@ -13,6 +13,10 @@
 CODE_MAX = 32000.0
 TINY = 1e-30
 CHUNK = 256
+STEP = 512
+LIM_P, LIM_T, LIM_D, LIM_S, LIM_G = 55, 8, 8, 16, 16
+SCALE = HEAD ** (-0.5)
+UNIT = SCALE * LOG2E
 
 F32 = jnp.float32
 BF16 = jnp.bfloat16
@@ -64,15 +68,24 @@
     return out
 
 
-def prep_kernel(tok_ref, lev_ref, table_ref, wk_ref, wv_ref, inp_ref, key_ref, val_ref):
+def prep_kernel(tok_hbm, lev_hbm, table_hbm, wk_hbm, wv_hbm, g_hbm, inp_ref, key_ref, val_ref, g_ref, *scratch):
+    tok_ref, lev_ref, table_ref, wk_ref, wv_ref, sems = scratch
+    first = [(table_hbm, table_ref), (lev_hbm, lev_ref), (wk_hbm, wk_ref), (wv_hbm, wv_ref), (g_hbm, g_ref)]
+    parts = [slice(c * CHUNK, (c + 1) * CHUNK) for c in range(tok_ref.shape[1] // CHUNK)]
+    pairs = first + [(tok_hbm.at[:, part, :], tok_ref.at[:, part, :]) for part in parts]
+    copies = [pltpu.make_async_copy(src, dst, sems.at[i]) for i, (src, dst) in enumerate(pairs)]
+    for copy in copies:
+        copy.start()
+    for copy in copies[: len(first)]:
+        copy.wait()
     table = table_ref[...]
     hi = table.astype(BF16)
     rest = table - hi.astype(F32)
     mid = rest.astype(BF16)
     low = (rest - mid.astype(F32)).astype(BF16)
     levels = table.shape[0]
-    for c in range(tok_ref.shape[1] // CHUNK):
-        rows = slice(c * CHUNK, (c + 1) * CHUNK)
+    for c, rows in enumerate(parts):
+        copies[len(first) + c].wait()
         raw = tok_ref[0, rows, :].astype(F32)
         centered = raw - jnp.mean(raw, axis=1, keepdims=True)
         normed = centered / jnp.sqrt(jnp.mean(centered * centered, axis=1, keepdims=True) + 1e-05)
@@ -85,42 +98,58 @@
         val_ref[rows, :] = nn(inputs, wv_ref[...]).astype(BF16)
 
 
+def three(x):
+    hi = x.astype(BF16).astype(F32)
+    mid = (x - hi).astype(BF16).astype(F32)
+    return [hi, mid, x - hi - mid]
+
+
 def fill_episode(bounds_ref, episode_ref, base):
     before = jnp.int32(0)
-    place = lax.broadcasted_iota(jnp.int32, (BLOCK, 128), 0)
+    shape = (BLOCK, episode_ref.shape[1])
+    place = lax.broadcasted_iota(jnp.int32, shape, 0)
     for b in range(bounds_ref.shape[1]):
         bound = bounds_ref[0, b]
-        local = before + (place >= bound).astype(jnp.int32)
-        episode_ref[b * BLOCK : (b + 1) * BLOCK, :] = base + local.astype(F32)
+        episode = base + (before + (place >= bound).astype(jnp.int32)).astype(F32)
+        episode_ref[b * BLOCK : (b + 1) * BLOCK, :] = episode.astype(episode_ref.dtype)
         before = before + (bound < BLOCK).astype(jnp.int32)
     return before
 
 
-def wide(column, width):
-    return jnp.concatenate([column] * (width // 128), axis=1)
+def slope_of(slopes_ref, h, width):
+    return jnp.full((1, width), slopes_ref[h] * (1.0 / SCALE), F32)
 
 
 def top_kernel(n, bounds_ref, slopes_ref, key_ref, *refs):
-    q_refs, (stats_ref, episode_ref) = refs[:n], refs[n:]
+    q_refs, (stats_ref, score_ref, side_ref) = refs[:n], refs[n:]
     rows = q_refs[0].shape[1]
     tokens, width = key_ref.shape
     heads = width // HEAD
-    starts = fill_episode(bounds_ref, episode_ref, 0.0)
-    scale = HEAD ** (-0.5)
-    tops = []
-    for h in range(heads):
+    starts = fill_episode(bounds_ref, side_ref, 0.0)
+    lane = lax.broadcasted_iota(jnp.int32, (rows, 128), 1)
+    for h in range(heads):
+        beside = jnp.zeros((rows, 128), F32)
+        for i, term in enumerate(three(slope_of(slopes_ref, h, 128))):
+            beside = jnp.where(lane == i, term, beside)
+        beside = beside.astype(BF16)
+        keys = jnp.concatenate([key_ref[:, head_cols(h)], side_ref[...]], axis=1)
         for j in range(n):
-            best = None
-            query = q_refs[j][0, :, head_cols(h)]
-            for c in range(tokens // CHUNK):
-                part = slice(c * CHUNK, (c + 1) * CHUNK)
-                score = nt(key_ref[part, head_cols(h)], query) * scale
-                score = score + wide(slopes_ref[h] * episode_ref[part, :], rows)
-                most = jnp.max(score, axis=0, keepdims=True)
-                best = most if best is None else jnp.maximum(best, most)
-            tops.append(best)
-    tops.append(jnp.zeros((1, rows), F32) + starts.astype(F32))
-    stats_ref[...] = stack_rows(tops, stats_ref.shape[0], rows)
+            query = jnp.concatenate([q_refs[j][0, :, head_cols(h)], beside], axis=1)
+            score = nt(keys, query)
+            score_ref[h, :, j * rows : (j + 1) * rows] = score
+            stats_ref[h * n + j : h * n + j + 1, :] = jnp.max(score, axis=0, keepdims=True)
+    stats_ref[heads * n : heads * n + 1, :] = jnp.zeros((1, rows), F32) + starts.astype(F32)
+
+
+def dprod_kernel(n, val_ref, *refs):
+    q_refs, g_refs, (dprod_ref, qt_ref, gt_ref) = refs[:n], refs[n : 2 * n], refs[2 * n :]
+    rows = q_refs[0].shape[1]
+    for j in range(n):
+        cols = slice(j * rows, (j + 1) * rows)
+        qt_ref[:, cols] = q_refs[j][0].astype(F32).T.astype(BF16)
+        gt_ref[:, cols] = g_refs[j][0].astype(F32).T.astype(BF16)
+        for h in range(dprod_ref.shape[0]):
+            dprod_ref[h, :, cols] = nt(val_ref[:, head_cols(h)], g_refs[j][0, :, head_cols(h)])
 
 
 def merged_tops(n, heads, slopes_ref, stats_refs):
@@ -140,66 +169,48 @@
             best = None
             for k in range(n):
                 place = h * n + (j ^ k)
-                top = stats_refs[k][place : place + 1, :] + slopes_ref[h] * bases[k]
+                top = stats_refs[k][place : place + 1, :] + slope_of(slopes_ref, h, bases[k].shape[1]) * bases[k]
                 best = top if best is None else jnp.maximum(best, top)
             row.append(best)
         tops.append(row)
     return tops, bases[0]
 
 
-def gather_blocks(refs, scratch):
-    rows = refs[0].shape[1]
-    for j, ref in enumerate(refs):
-        scratch[j * rows : (j + 1) * rows, :] = ref[0]
-
-
-def sums_kernel(n, bounds_ref, slopes_ref, key_ref, val_ref, *refs):
-    q_refs, g_refs, top_refs = refs[:n], refs[n : 2 * n], refs[2 * n : 3 * n]
-    stats_ref, own_ref = refs[3 * n : 3 * n + 2]
-    send_refs = refs[3 * n + 2 : 4 * n + 1]
-    episode_ref, q_all, g_all, out_ref = refs[4 * n + 1 :]
-    rows = q_refs[0].shape[1]
-    tokens, width = key_ref.shape
-    heads = width // HEAD
-    scale = HEAD ** (-0.5)
+def sums_kernel(n, slopes_ref, val_ref, score_ref, gt_ref, *refs):
+    top_refs, (stats_ref, own_ref, expo_ref) = refs[:n], refs[n : n + 3]
+    send_refs = refs[n + 3 : 2 * n + 2]
+    (out_ref,) = refs[2 * n + 2 :]
+    heads, tokens, lats = score_ref.shape
+    rows = lats // n
     tops, base = merged_tops(n, heads, slopes_ref, top_refs)
-    fill_episode(bounds_ref, episode_ref, base[:, :128])
-    gather_blocks(q_refs, q_all)
-    gather_blocks(g_refs, g_all)
-    lats = n * rows
-    norms, deltas = [], []
-    for h in range(heads):
-        top = jnp.concatenate(tops[h], axis=1)
-
-        def step(c, carry):
-            norm, delta = carry
-            part = pl.ds(pl.multiple_of(c * CHUNK, CHUNK), CHUNK)
-            keys, values = key_ref[part, head_cols(h)], val_ref[part, head_cols(h)]
-            score = nt(keys, q_all[:, head_cols(h)]) * scale
-            score = score + wide(slopes_ref[h] * episode_ref[part, :], lats)
-            expo = jnp.exp(score - top)
-            weights = expo.astype(BF16)
-            dprod = nt(values, g_all[:, head_cols(h)])
-            out_ref[...] += tn(values, weights)
-            norm = norm + jnp.sum(expo, axis=0, keepdims=True)
-            delta = delta + jnp.sum(weights.astype(F32) * dprod, axis=0, keepdims=True)
-            return norm, delta
-
-        out_ref[...] = jnp.zeros_like(out_ref)
-        zero = jnp.zeros((1, lats), F32)
-        norm, delta = lax.fori_loop(0, tokens // CHUNK, step, (zero, zero))
-        norms += [norm[:, j * rows : (j + 1) * rows] for j in range(n)]
-        deltas += [delta[:, j * rows : (j + 1) * rows] for j in range(n)]
+    for h in range(heads):
+        slope = slope_of(slopes_ref, h, rows)
+        top = jnp.concatenate([t - slope * base for t in tops[h]], axis=1)
+        norm = out = None
+        for c in range(tokens // STEP):
+            part = slice(c * STEP, (c + 1) * STEP)
+            expo = jnp.exp2((score_ref[h, part, :] - top) * UNIT)
+            expo_ref[h, part, :] = expo
+            term = tn(val_ref[part, head_cols(h)], expo.astype(BF16))
+            part_norm = jnp.sum(expo, axis=0, keepdims=True)
+            out = term if out is None else out + term
+            norm = part_norm if norm is None else norm + part_norm
+        out_ref[...] = out
+        delta = jnp.sum(gt_ref[head_cols(h), :].astype(F32) * out, axis=0, keepdims=True)
+        for j in range(n):
+            cols = slice(j * rows, (j + 1) * rows)
+            stats_ref[h * n + j : h * n + j + 1, :] = norm[:, cols]
+            place = heads * n + h * n + j
+            stats_ref[place : place + 1, :] = delta[:, cols]
         own_ref[head_cols(h), :] = out_ref[:, :rows]
         write_messages(h, n, rows, heads, out_ref, send_refs)
-    stats_ref[...] = stack_rows(norms + deltas, stats_ref.shape[0], rows)
 
 
 def write_messages(h, n, rows, heads, sums_ref, send_refs):
     for j in range(1, n):
         steps, exponent = encode(sums_ref[:, j * rows : (j + 1) * rows])
         send_refs[j - 1][head_cols(h), :] = to_code(steps)
-        place = (heads + h * 0) * HEAD + h * 16
+        place = heads * HEAD + h * 16
         send_refs[j - 1][place : place + 16, :] = to_code(jnp.broadcast_to(exponent, (16, rows)))
 
 
@@ -227,59 +238,57 @@
     return norms, deltas
 
 
-def grads_kernel(n, bounds_ref, slopes_ref, inp_ref, key_ref, val_ref, *refs):
-    q_refs, g_refs, top_refs, sum_refs = (refs[i * n : (i + 1) * n] for i in range(4))
-    own_ref, keep_ref, give_ref = refs[4 * n : 4 * n + 3]
-    send_refs = refs[4 * n + 3 : 5 * n + 2]
-    episode_ref, q_all, g_all, dq_ref, tok_ref, weight_ref = refs[5 * n + 2 :]
-    rows = q_refs[0].shape[1]
-    tokens, width = key_ref.shape
-    heads = width // HEAD
-    scale = HEAD ** (-0.5)
-    tops, base = merged_tops(n, heads, slopes_ref, top_refs)
+def grads_kernel(n, h, heads, bounds_ref, slopes_ref, inp_ref, key_ref, expo_ref, dprod_ref, qt_ref, gt_ref, *refs):
+    top_refs, sum_refs, refs = refs[:n], refs[n : 2 * n], refs[2 * n :]
+    outs = n + 2
+    old, _, refs = (refs[:outs], refs[outs], refs[outs + 1 :]) if h else (None, None, refs)
+    own_ref, keep_ref, give_ref = refs[:3]
+    send_refs = refs[3:outs]
+    episode_ref, dq_ref, tok_ref, weight_ref = refs[outs:]
+    _, tokens, lats = expo_ref.shape
+    _, base = merged_tops(n, heads, slopes_ref, top_refs)
     norms, deltas = merged_sums(n, heads, sum_refs)
     fill_episode(bounds_ref, episode_ref, base[:, :128])
-    gather_blocks(q_refs, q_all)
-    gather_blocks(g_refs, g_all)
-    lats = n * rows
-    slope_rows = []
-    for h in range(heads):
-        top = jnp.concatenate(tops[h], axis=1)
-        inverse = 1.0 / norms[h]
-        mean = deltas[h] * inverse
-
-        def step(c, slope):
-            part = pl.ds(pl.multiple_of(c * CHUNK, CHUNK), CHUNK)
-            keys, values = key_ref[part, head_cols(h)], val_ref[part, head_cols(h)]
-            query, grad = q_all[:, head_cols(h)], g_all[:, head_cols(h)]
-            episode = wide(episode_ref[part, :], lats)
-            score = nt(keys, query) * scale
-            score = score + slopes_ref[h] * episode
-            probs = jnp.exp(score - top) * inverse
-            tok_ref[part, width + h * HEAD : width + (h + 1) * HEAD] = nn(probs.astype(BF16), grad).astype(BF16)
-            dprod = nt(values, grad)
-            score_grad = probs * (dprod - mean)
-            slope = slope + jnp.sum(score_grad * episode, axis=0, keepdims=True)
-            score_grad_b = score_grad.astype(BF16)
-            tok_ref[part, head_cols(h)] = (scale * nn(score_grad_b, query)).astype(BF16)
-            dq_ref[...] += tn(keys, score_grad_b)
-            return slope
-
-        dq_ref[...] = jnp.zeros_like(dq_ref)
-        slope = lax.fori_loop(0, tokens // CHUNK, step, jnp.zeros((1, lats), F32))
-        slope_rows.append(jnp.sum(slope, axis=1, keepdims=True))
-        own_ref[head_cols(h), :] = dq_ref[:, :rows]
-        write_messages(h, n, rows, heads, dq_ref, send_refs)
+    inverse = 1.0 / norms[h]
+    mean = deltas[h] * inverse
+    slope = jnp.zeros((1, 128), F32)
+    dq = None
+    for c in range(tokens // STEP):
+        part = slice(c * STEP, (c + 1) * STEP)
+        probs = expo_ref[h, part, :] * inverse
+        tok_ref[HEAD:, part] = nt(gt_ref[head_cols(h), :], probs.astype(BF16)).astype(BF16)
+        score_grad = probs * (dprod_ref[h, part, :] - mean)
+        folded = score_grad[:, :128]
+        for i in range(1, lats // 128):
+            folded = folded + score_grad[:, i * 128 : (i + 1) * 128]
+        slope = slope + jnp.sum(folded * episode_ref[part, :], axis=0, keepdims=True)
+        score_grad_b = score_grad.astype(BF16)
+        tok_ref[:HEAD, part] = (SCALE * nt(qt_ref[head_cols(h), :], score_grad_b)).astype(BF16)
+        term = tn(key_ref[part, head_cols(h)], score_grad_b)
+        dq = term if dq is None else dq + term
+    dq_ref[...] = dq
+    if h:
+        done, cols = h * HEAD, h * 2 * HEAD
+        own_ref[:done, :] = old[0][:done, :]
+        keep_ref[:, :cols] = old[1][:, :cols]
+        give_ref[:, :cols] = old[2][:, :cols]
+        for ref, was in zip(send_refs, old[3:]):
+            ref[:done, :] = was[:done, :]
+            ref[heads * HEAD : heads * HEAD + 16 * h, :] = was[heads * HEAD : heads * HEAD + 16 * h, :]
+    rows = lats // n
+    own_ref[head_cols(h), :] = dq_ref[:, :rows]
+    write_messages(h, n, rows, heads, dq_ref, send_refs)
     half = keep_ref.shape[0] - 8
-    weight_ref[0] = tn(inp_ref[:, :half], tok_ref[...])
-    weight_ref[1] = tn(inp_ref[:, half:], tok_ref[...])
+    for i in range(2):
+        side = inp_ref[:, i * half : (i + 1) * half]
+        weight_ref[i] = lax.dot_general(side, tok_ref[...], (((0,), (1,)), ((), ())), preferred_element_type=F32)
     core = lax.axis_index("dp")
-    keep_ref[:half, :] = weight_ref[core]
-    give_ref[:half, :] = weight_ref[1 - core]
-    columns = keep_ref.shape[1]
-    slopes = stack_rows([jnp.broadcast_to(s, (1, columns)) for s in slope_rows], 8, columns)
-    keep_ref[half:, :] = slopes
-    give_ref[half:, :] = slopes
+    cols = slice(h * 2 * HEAD, (h + 1) * 2 * HEAD)
+    total = jnp.broadcast_to(jnp.sum(slope, axis=1, keepdims=True), (8, 2 * HEAD))
+    keep_ref[:half, cols] = weight_ref[core]
+    give_ref[:half, cols] = weight_ref[1 - core]
+    keep_ref[half:, cols] = total
+    give_ref[half:, cols] = total
 
 
 def pair_kernel(n, heads, keep_ref, got_ref, own_ref, *send_refs):
@@ -287,14 +296,11 @@
     half = keep_ref.shape[0] - 8
     piece = half // n
     width = keep_ref.shape[1]
-    place = lax.broadcasted_iota(jnp.int32, (16, width), 0)
     slopes = keep_ref[half:, :] + got_ref[half:, :]
-    digits = []
-    for h in range(heads):
-        value = slopes[h : h + 1, :]
-        steps, exponent = encode(value)
-        left = value * (jnp.exp2(-exponent) * CODE_MAX) - steps
-        digits += [exponent, steps, jnp.round(left * CODE_MAX)]
+    value = slopes[0:1, :]
+    steps, exponent = encode(value)
+    left = value * (jnp.exp2(-exponent) * CODE_MAX) - steps
+    digits = [exponent, steps, jnp.round(left * CODE_MAX)]
     for k in range(n):
         rows = pl.ds(pl.multiple_of((me ^ k) * piece, piece), piece)
         total = keep_ref[rows, :] + got_ref[rows, :]
@@ -309,6 +315,7 @@
 
 def attended_kernel(n, heads, own_ref, *refs):
     got_refs, sum_refs, out_ref = refs[: n - 1], refs[n - 1 : 2 * n - 1], refs[2 * n - 1]
+    refs[2 * n][...] = jnp.zeros_like(refs[2 * n])
     rows = own_ref.shape[1]
     norms, _ = merged_sums(n, heads, sum_refs)
     for h in range(heads):
@@ -322,37 +329,35 @@
 def last_kernel(n, heads, own_ref, weight_ref, *refs):
     got_refs, part_refs = refs[: n - 1], refs[n - 1 : 2 * n - 2]
     grad_ref, key_ref, val_ref, slope_ref = refs[2 * n - 2 :]
-    scale = HEAD ** (-0.5)
     for h in range(heads):
         total = own_ref[head_cols(h), :]
         for ref in got_refs:
             total = total + read_message(ref, h, heads)
-        grad_ref[0, :, head_cols(h)] = (scale * total).T.astype(BF16)
+        grad_ref[0, :, head_cols(h)] = (SCALE * total).T.astype(BF16)
     piece = weight_ref.shape[0] - 8
-    width = weight_ref.shape[1] // 2
     total = weight_ref[:piece, :]
-    slopes = weight_ref[piece:, :]
-    place = lax.broadcasted_iota(jnp.int32, slopes.shape, 0)
+    slopes = weight_ref[piece : piece + 1, :]
     for ref in part_refs:
         extra = ref[piece:, :].astype(jnp.int32).astype(F32)
         total = total + ref[:piece, :].astype(jnp.int32).astype(F32) * (jnp.exp2(extra[0:1, :]) * (1.0 / CODE_MAX))
-        for h in range(heads):
-            exponent, steps, left = (extra[1 + 3 * h + i : 2 + 3 * h + i, :] for i in range(3))
-            value = (steps + left * (1.0 / CODE_MAX)) * (jnp.exp2(exponent) * (1.0 / CODE_MAX))
-            slopes = jnp.where(place == h, slopes + value, slopes)
-    key_ref[...] = total[:, :width]
-    val_ref[...] = total[:, width:]
-    slope_ref[...] = slopes[:, :128]
-
-
-def call(kernel, name, outs, args, scratch=(), smem=0, limit=40 << 20):
+        exponent, steps, left = (extra[i : i + 1, :] for i in range(1, 4))
+        slopes = slopes + (steps + left * (1.0 / CODE_MAX)) * (jnp.exp2(exponent) * (1.0 / CODE_MAX))
+    for h in range(heads):
+        at = h * 2 * HEAD
+        key_ref[:, head_cols(h)] = total[:, at : at + HEAD]
+        val_ref[:, head_cols(h)] = total[:, at + HEAD : at + 2 * HEAD]
+        slope_ref[h] = slopes[0, at]
+
+
+def call(kernel, name, outs, args, us, scratch=(), smem=0, limit=8 << 20, ins=None, out_specs=None):
     return pl.pallas_call(
         kernel,
         out_shape=[jax.ShapeDtypeStruct(shape, dtype) for shape, dtype in outs],
-        in_specs=[SMEM] * smem + [VMEM] * (len(args) - smem),
-        out_specs=[VMEM] * len(outs),
+        in_specs=ins or [SMEM] * smem + [VMEM] * (len(args) - smem),
+        out_specs=out_specs or [VMEM] * len(outs),
         scratch_shapes=list(scratch),
         compiler_params=pltpu.CompilerParams(vmem_limit_bytes=limit),
+        cost_estimate=pl.CostEstimate(flops=int(us * 1.1e9), bytes_accessed=1 << 16, transcendentals=0),
         name=name,
     )(*args)
 
@@ -364,75 +369,99 @@
     lats = n * rows
     peers = range(1, n)
     q_all = [queries] + [swap(queries, "seq", k, n) for k in peers]
-    inputs, keys, values = call(
+    prep_args = (tokens, levels, level_table, w_key, w_value)
+    inputs, keys, values, grad = call(
         prep_kernel,
         "prep",
-        [((toks, channels), BF16), ((toks, width), BF16), ((toks, width), BF16)],
-        (tokens, levels, level_table, w_key, w_value),
-    )
-    g_all = [cotangent] + [swap(cotangent, "seq", k, n) for k in peers]
-    episode = pltpu.VMEM((toks, 128), F32)
+        [((toks, channels), BF16), ((toks, width), BF16), ((toks, width), BF16), (cotangent.shape, BF16)],
+        (*prep_args, cotangent),
+        3,
+        [pltpu.VMEM(a.shape, a.dtype) for a in prep_args] + [pltpu.SemaphoreType.DMA((5 + toks // CHUNK,))],
+        limit=LIM_P << 20,
+        ins=[pl.BlockSpec(memory_space=pltpu.HBM)] * 6,
+    )
+    g_all = [grad] + [swap(grad, "seq", k, n) for k in peers]
     stat_rows = -(-(heads * n + 1) // 8) * 8
-    (top_own,) = call(
+    square = ((heads, toks, lats), F32)
+    top_own, scores = call(
         functools.partial(top_kernel, n),
         "tops",
-        [((stat_rows, rows), F32)],
+        [((stat_rows, rows), F32), square],
         (boundaries, slopes, keys, *q_all),
-        [episode],
         2,
+        [pltpu.VMEM((toks, 128), BF16)],
+        2,
+        limit=LIM_T << 20,
     )
     tops = [top_own] + [swap(top_own, "seq", k, n) for k in peers]
+    dprod, q_turned, g_turned = call(
+        functools.partial(dprod_kernel, n),
+        "dprod",
+        [square, ((width, lats), BF16), ((width, lats), BF16)],
+        (values, *q_all, *g_all),
+        2,
+        limit=LIM_D << 20,
+    )
     message = ((heads * HEAD + 16 * heads, rows), I16)
-    blocks = pltpu.VMEM((lats, width), BF16)
+    partial = pltpu.VMEM((HEAD, lats), F32)
     sums = call(
         functools.partial(sums_kernel, n),
         "sums",
-        [((2 * heads * n, rows), F32), ((width, rows), F32)] + [message] * (n - 1),
-        (boundaries, slopes, keys, values, *q_all, *g_all, *tops),
-        [episode, blocks, blocks, pltpu.VMEM((HEAD, lats), F32)],
+        [((2 * heads * n, rows), F32), ((width, rows), F32), square] + [message] * (n - 1),
+        (slopes, values, scores, g_turned, *tops),
         2,
+        [partial],
+        1,
+        limit=LIM_S << 20,
     )
     norms = [sums[0]] + [swap(sums[0], "seq", k, n) for k in peers]
-    outs = [swap(sums[1 + k], "seq", k, n) for k in peers]
+    outs = [swap(sums[2 + k], "seq", k, n) for k in peers]
     half = channels // 2
-    grads = call(
-        functools.partial(grads_kernel, n),
-        "grads",
-        [((width, rows), F32)] + [((half + 8, 2 * width), F32)] * 2 + [message] * (n - 1),
-        (boundaries, slopes, inputs, keys, values, *q_all, *g_all, *tops, *norms),
-        [
-            episode,
-            blocks,
-            blocks,
-            pltpu.VMEM((HEAD, lats), F32),
-            pltpu.VMEM((toks, 2 * width), BF16),
-            pltpu.VMEM((2, half, 2 * width), F32),
-        ],
-        2,
-    )
+    grads = attended = ()
+    for h in range(heads):
+        grads = call(
+            functools.partial(grads_kernel, n, h, heads),
+            f"grads{h}",
+            [((width, rows), F32)] + [((half + 8, 2 * width), F32)] * 2 + [message] * (n - 1),
+            (boundaries, slopes, inputs, keys, sums[2], dprod, q_turned, g_turned, *tops, *norms, *grads, *attended[1:]),
+            2,
+            [
+                pltpu.VMEM((toks, 128), F32),
+                partial,
+                pltpu.VMEM((2 * HEAD, toks), BF16),
+                pltpu.VMEM((2, half, 2 * HEAD), F32),
+            ],
+            2,
+            limit=LIM_G << 20,
+        )
+        if h == 0:
+            attended = call(
+                functools.partial(attended_kernel, n, heads),
+                "attended",
+                [((1, rows, width), BF16), ((8, 128), F32)],
+                (sums[1], *outs, *norms),
+                1,
+            )
     got = swap(grads[2], "dp", 1, 2)
     dqs = [swap(grads[2 + k], "seq", k, n) for k in peers]
-    (attended,) = call(
-        functools.partial(attended_kernel, n, heads),
-        "attended",
-        [((1, rows, width), BF16)],
-        (sums[1], *outs, *norms),
-    )
     piece = half // n
     pair = call(
         functools.partial(pair_kernel, n, heads),
         "pair",
         [((piece + 8, 2 * width), F32)] + [((piece + 16, 2 * width), I16)] * (n - 1),
         (grads[1], got),
+        0.3,
     )
     parts = [swap(pair[k], "seq", k, n) for k in peers]
-    query_grad, key_grad, value_grad, slope_grad = call(
+    last = call(
         functools.partial(last_kernel, n, heads),
         "last",
-        [((1, rows, width), BF16), ((piece, width), F32), ((piece, width), F32), ((8, 128), F32)],
+        [((1, rows, width), BF16), ((piece, width), F32), ((piece, width), F32), ((heads,), F32)],
         (grads[0], pair[0], *dqs, *parts),
-    )
-    return attended, query_grad, key_grad, value_grad, slope_grad[:heads, 0]
+        1,
+        out_specs=[VMEM] * 3 + [SMEM],
+    )
+    return (attended[0], *last)
 
 
 def carried_in(part, axis, combine, identity):

time: 70.3 us -> 57.7 us (0.82)
  waiting for transfers between devices: 15.3 us -> 9.57 us
  local copies, waits for them, and re-layouts: 6.11 us -> 3 us
  Pallas kernels: 20.8 us -> 18.9 us
  starting transfers between devices: 27 us -> 25.2 us
    ppermute x22, waiting for transfers between devices: 15.3 us -> 9.57 us  [swap(): return lax.ppermute(x, axis, [(i, i ^ k) for i in range(n)])]
    unnamed x18, local copies, waits for them, and re-layouts: 5.49 us -> 3 us
    pallas_call x7 -> x9, Pallas kernels: 20.8 us -> 18.9 us  [call(): pl.pallas_call(kernel, out_shape=[jax.ShapeDtypeStruct(shape, dtype) for...]
    ppermute x22, starting transfers between devices: 27 us -> 25.2 us  [swap(): return lax.ppermute(x, axis, [(i, i ^ k) for i in range(n)])]
  transfers between devices with their start and end apart: 22 -> 22, of which waited for: 11 -> 8; matrix products, arithmetic and copies ran while one was open for 0% -> 0% of each run, Pallas kernels for 7% -> 20%
where the time goes in v2:
time: 57.7 us; the launch traced here: 57.4 us
  starting transfers between devices  25.2 us (44%)
  Pallas kernels  18.9 us (33%)
  waiting for transfers between devices  9.57 us (17%)
  local copies, waits for them, and re-layouts  3 us (5%)
  between operations  0.8 us (1%)
    ppermute x22, starting transfers between devices, swap(): return lax.ppermute(x, axis, [(i, i ^ k) for i in range(n)])  25.2 us
    pallas_call x9, Pallas kernels, call(): pl.pallas_call(kernel, out_shape=[jax.ShapeDtypeStruct(shape, dtype) for...  18.9 us
    ppermute x22, waiting for transfers between devices, swap(): return lax.ppermute(x, axis, [(i, i ^ k) for i in range(n)])  9.57 us
    unnamed x18, local copies, waits for them, and re-layouts  3 us
  transfers between devices with their start and end apart: 22, of which 8 were waited for; matrix products, arithmetic and copies ran while one was open for 0% of the time, Pallas kernels for 20%

profile of v2, /device:TPU:0, one launch (start us, length us, event | category | flops | bytes accessed | tf_op | source)
XLA Modules:
  0.0 57.4 jit_solution(1609522438715524470)
XLA Ops:
  0.6 0.0 copy-start.7
  0.6 0.0 copy-start.5
  0.7 0.0 copy-start.6
  0.7 4.0 %collective-permute-start.2 = (bf16[1,256,256]{2,1,0:T(8,128)(2,1)}, bf16[1,256,256]{2,1,0:T(8,128)(2,1)S(1)}, u32[]{:S(2)}, u32[]{:S(2)}) collective-permute-start(bf16[1,256,256]{2,1,0:T(8,128)(2,1)} %refs_0_.3), channel_id=1, source_target_pairs={{0,12},{4,8},{8,4},{12,0},{1,13},{5,9},{9,5},{13,1},{2,14},{6,10},... | collective-permute-start | bytes 393224 | tf_op jit(solution)/shard_map/ppermute | solution.py:45
  4.6 0.5 collective-permute-start.1
  5.1 0.1 collective-permute-start
  5.3 5.1 %prep.1 = (bf16[1024,512]{1,0:T(8,128)(2,1)}, bf16[1024,256]{1,0:T(8,128)(2,1)}, bf16[1024,256]{1,0:T(8,128)(2,1)}, bf16[1,256,256]{2,1,0:T(8,128)(2,1)}) custom-call(bf16[1,1024,512]{2,1,0:T(8,128)(2,1)} %tok_hbm.1, s32[1,1024]{1,0:T(1,128)} %lev_hbm.1, f32[256,512]{1,0:T(8,128)} %table_hbm.1, bf16[512,256]{1,0:T(8,128)(2,1)} %wk_hbm.1, ...), custom_call_target="tpu_custom_call" | custom-call | flops 3300000000 | bytes 65536 | tf_op jit(solution)/shard_map/prep/pallas_call | solution.py:353
  10.4 2.9 %collective-permute-start.5 = (bf16[1,256,256]{2,1,0:T(8,128)(2,1)}, bf16[1,256,256]{2,1,0:T(8,128)(2,1)S(1)}, u32[]{:S(2)}, u32[]{:S(2)}) collective-permute-start(bf16[1,256,256]{2,1,0:T(8,128)(2,1)} %get-tuple-element.45.refs_4_), channel_id=1, source_target_pairs={{0,12},{4,8},{8,4},{12,0},{1,13},{5,9},{9,5},{13,1},{2,14},{6,10},... | collective-permute-start | bytes 393224 | tf_op jit(solution)/shard_map/ppermute | solution.py:45
  13.3 0.5 collective-permute-start.4
  13.8 0.0 collective-permute-done.2.refs_3_
  13.8 0.1 collective-permute-start.3
  13.9 0.0 collective-permute-done.1.refs_2_
  13.9 0.0 collective-permute-done.refs_1_
  13.9 0.0 copy-done.7
  13.9 0.0 copy-done.5
  14.0 0.0 copy-done.6
  14.0 0.0 copy-start.1
  14.0 1.0 %copy-done.1 = bf16[1024,256]{1,0:T(8,128)(2,1)S(1)} copy-done((bf16[1024,256]{1,0:T(8,128)(2,1)S(1)}, bf16[1024,256]{1,0:T(8,128)(2,1)}, u32[]{:S(2)}) %copy-start.1) | copy-done | bytes 524312
  15.0 1.9 %tops.1 = (f32[16,256]{1,0:T(8,128)S(1)}, f32[2,1024,1024]{2,1,0:T(8,128)S(1)}) custom-call(s32[1,8]{1,0:T(1,128)S(1)} %copy-done.6, f32[2]{0:T(128)S(1)} %copy-done.5, bf16[1024,256]{1,0:T(8,128)(2,1)S(1)} %copy-done.1, bf16[1,256,256]{2,1,0:T(8,128)(2,1)S(1)} %copy-done.7, bf16[1,256,256]{2,1,0:T(8,128)(2,1)S(1)} %collective-permute-done.refs_1_, ...), custom_call_target="tpu_custom_call" | custom-call | flops 2200000000 | bytes 65536 | tf_op jit(solution)/shard_map/tops/pallas_call | solution.py:353
  16.9 2.9 %collective-permute-start.8 = (f32[16,256]{1,0:T(8,128)S(1)}, f32[16,256]{1,0:T(8,128)S(1)}, u32[]{:S(2)}, u32[]{:S(2)}) collective-permute-start(f32[16,256]{1,0:T(8,128)S(1)} %get-tuple-element.47.refs_0_), channel_id=1, source_target_pairs={{0,12},{4,8},{8,4},{12,0},{1,13},{5,9},{9,5},{13,1},{2,14},{6,10},... | collective-permute-start | bytes 49160 | tf_op jit(solution)/shard_map/ppermute | solution.py:45
  19.8 0.5 collective-permute-start.7
  20.3 0.0 collective-permute-done.5.refs_7_
  20.3 0.1 collective-permute-start.6
  20.4 0.0 collective-permute-done.4.refs_6_
  20.4 0.0 collective-permute-done.3.refs_5_
  20.5 1.0 %copy-done.3 = bf16[1024,256]{1,0:T(8,128)(2,1)S(1)} copy-done((bf16[1024,256]{1,0:T(8,128)(2,1)S(1)}, bf16[1024,256]{1,0:T(8,128)(2,1)}, u32[]{:S(2)}) %copy-start.3) | copy-done | bytes 524312
  21.5 0.9 %copy-done.8 = bf16[1,256,256]{2,1,0:T(8,128)(2,1)S(1)} copy-done((bf16[1,256,256]{2,1,0:T(8,128)(2,1)S(1)}, bf16[1,256,256]{2,1,0:T(8,128)(2,1)}, u32[]{:S(2)}) %copy-start.8) | copy-done | bytes 131096
  22.4 1.3 %dprod.1 = (f32[2,1024,1024]{2,1,0:T(8,128)S(1)}, bf16[256,1024]{1,0:T(8,128)(2,1)S(1)}, bf16[256,1024]{1,0:T(8,128)(2,1)S(1)}) custom-call(bf16[1024,256]{1,0:T(8,128)(2,1)S(1)} %copy-done.3, bf16[1,256,256]{2,1,0:T(8,128)(2,1)S(1)} %copy-done.7, bf16[1,256,256]{2,1,0:T(8,128)(2,1)S(1)} %collective-permute-done.refs_1_, ...), custom_call_target="tpu_custom_call" | custom-call | flops 2200000000 | bytes 65536 | tf_op jit(solution)/shard_map/dprod/pallas_call | solution.py:353
  23.7 0.0 collective-permute-done.8.refs_3_
  23.7 0.0 collective-permute-done.7.refs_2_
  23.7 0.3 collective-permute-done.6.refs_1_
  24.0 0.0 copy-done.4
  24.0 2.5 %sums.1 = (f32[16,256]{1,0:T(8,128)S(1)}, f32[256,256]{1,0:T(8,128)S(1)}, f32[2,1024,1024]{2,1,0:T(8,128)S(1)}, s16[288,256]{1,0:T(8,128)(2,1)S(1)}, s16[288,256...) custom-call(f32[2]{0:T(128)S(1)} %copy-done.5, bf16[1024,256]{1,0:T(8,128)(2,1)S(1)} %copy-done.4, ...), custom_call_target="tpu_custom_call" | custom-call | flops 2200000000 | bytes 65536 | tf_op jit(solution)/shard_map/sums/pallas_call | solution.py:353
  26.5 2.6 %collective-permute-start.14 = (f32[16,256]{1,0:T(8,128)S(1)}, f32[16,256]{1,0:T(8,128)S(1)}, u32[]{:S(2)}, u32[]{:S(2)}) collective-permute-start(f32[16,256]{1,0:T(8,128)S(1)} %get-tuple-element.52.refs_3_.refs_4_), channel_id=1, source_target_pairs={{0,12},{4,8},{8,4},{12,0},{1,13},{5,9},{9,5},{13,1},{2,14},{6,10},... | collective-permute-start | bytes 49160 | tf_op jit(solution)/shard_map/ppermute | solution.py:45
  29.1 0.5 collective-permute-start.13
  29.6 0.5 collective-permute-start.12
  30.1 1.6 %collective-permute-start.9 = (s16[288,256]{1,0:T(8,128)(2,1)S(1)}, s16[288,256]{1,0:T(8,128)(2,1)S(1)}, u32[]{:S(2)}, u32[]{:S(2)}) collective-permute-start(s16[288,256]{1,0:T(8,128)(2,1)S(1)} %get-tuple-element.49), channel_id=1, source_target_pairs={{0,4},{4,0},{8,12},{12,8},{1,5},{5,1},{9,13},{13,9},{2,6},{6,2},{1... | collective-permute-start | bytes 442376 | tf_op jit(solution)/shard_map/ppermute | solution.py:45
  31.7 1.5 %collective-permute-start.10 = (s16[288,256]{1,0:T(8,128)(2,1)S(1)}, s16[288,256]{1,0:T(8,128)(2,1)S(1)}, u32[]{:S(2)}, u32[]{:S(2)}) collective-permute-start(s16[288,256]{1,0:T(8,128)(2,1)S(1)} %get-tuple-element.50), channel_id=1, source_target_pairs={{0,8},{4,12},{8,0},{12,4},{1,9},{5,13},{9,1},{13,5},{2,10},{6,14},... | collective-permute-start | bytes 442376 | tf_op jit(solution)/shard_map/ppermute | solution.py:45
  33.2 0.0 collective-permute-done.14.refs_6_.refs_7_
  33.2 0.9 %collective-permute-start.11 = (s16[288,256]{1,0:T(8,128)(2,1)S(1)}, s16[288,256]{1,0:T(8,128)(2,1)S(1)}, u32[]{:S(2)}, u32[]{:S(2)}) collective-permute-start(s16[288,256]{1,0:T(8,128)(2,1)S(1)} %get-tuple-element.51), channel_id=1, source_target_pairs={{0,12},{4,8},{8,4},{12,0},{1,13},{5,9},{9,5},{13,1},{2,14},{6,10},... | collective-permute-start | bytes 442376 | tf_op jit(solution)/shard_map/ppermute | solution.py:45
  34.0 0.3 collective-permute-done.13.refs_5_.refs_6_
  34.3 0.0 collective-permute-done.12.refs_4_.refs_5_
  34.4 3.1 %grads0.1 = (f32[256,256]{1,0:T(8,128)S(1)}, f32[264,512]{1,0:T(8,128)S(1)}, f32[264,512]{1,0:T(8,128)S(1)}, s16[288,256]{1,0:T(8,128)(2,1)S(1)}, s16[288,256]{1...) custom-call(s32[1,8]{1,0:T(1,128)S(1)} %copy-done.6, f32[2]{0:T(128)S(1)} %copy-done.5, bf16[1024,512]{1,0:T(8,128)(2,1)S(1)} %copy-done, ...), custom_call_target="tpu_custom_call" | custom-call | flops 2200000000 | bytes 65536 | tf_op jit(solution)/shard_map/grads0/pallas_call | solution.py:353
  37.5 0.0 collective-permute-done.9.refs_0_
  37.5 0.0 collective-permute-done.10.refs_1_
  37.5 1.7 %collective-permute-done.11.refs_2_ = s16[288,256]{1,0:T(8,128)(2,1)S(1)} collective-permute-done((s16[288,256]{1,0:T(8,128)(2,1)S(1)}, s16[288,256]{1,0:T(8,128)(2,1)S(1)}, u32[]{:S(2)}, u32[]{:S(2)}) %collective-permute-start.11) | collective-permute-done | bytes 147488 | tf_op jit(solution)/shard_map/ppermute | solution.py:45
  39.2 0.9 %attended.1 = (bf16[1,256,256]{2,1,0:T(8,128)(2,1)}, f32[8,128]{1,0:T(8,128)S(1)}) custom-call(f32[256,256]{1,0:T(8,128)S(1)} %get-tuple-element.48.own_ref, s16[288,256]{1,0:T(8,128)(2,1)S(1)} %collective-permute-done.9.refs_0_, s16[288,256]{1,0:T(8,128)(2,1)S(1)} %collective-permute-done.10.refs_1_, s16[288,256]{1,0:T(8,128)(2,1)S(1)} %collective-permute-done.11.refs_2_, ...), custom_call_target="tpu_custom_call" | custom-call | flops 1100000000 | bytes 65536 | tf_op jit(solution)/shard_map/attended/pallas_call | solution.py:353
  40.1 3.1 %grads1.1 = (f32[256,256]{1,0:T(8,128)S(1)}, f32[264,512]{1,0:T(8,128)S(1)}, f32[264,512]{1,0:T(8,128)S(1)}, s16[288,256]{1,0:T(8,128)(2,1)S(1)}, s16[288,256]{1...) custom-call(s32[1,8]{1,0:T(1,128)S(1)} %copy-done.6, f32[2]{0:T(128)S(1)} %copy-done.5, bf16[1024,512]{1,0:T(8,128)(2,1)S(1)} %copy-done, ...), custom_call_target="tpu_custom_call" | custom-call | flops 2200000000 | bytes 65536 | tf_op jit(solution)/shard_map/grads1/pallas_call | solution.py:353
  43.2 0.1 collective-permute-start.15
  43.3 0.6 %collective-permute-start.16 = (s16[288,256]{1,0:T(8,128)(2,1)S(1)}, s16[288,256]{1,0:T(8,128)(2,1)S(1)}, u32[]{:S(2)}, u32[]{:S(2)}) collective-permute-start(s16[288,256]{1,0:T(8,128)(2,1)S(1)} %get-tuple-element.69), channel_id=1, source_target_pairs={{0,4},{4,0},{8,12},{12,8},{1,5},{5,1},{9,13},{13,9},{2,6},{6,2},{1... | collective-permute-start | bytes 442376 | tf_op jit(solution)/shard_map/ppermute | solution.py:45
  43.9 0.9 %collective-permute-start.17 = (s16[288,256]{1,0:T(8,128)(2,1)S(1)}, s16[288,256]{1,0:T(8,128)(2,1)S(1)}, u32[]{:S(2)}, u32[]{:S(2)}) collective-permute-start(s16[288,256]{1,0:T(8,128)(2,1)S(1)} %get-tuple-element.70), channel_id=1, source_target_pairs={{0,8},{4,12},{8,0},{12,4},{1,9},{5,13},{9,1},{13,5},{2,10},{6,14},... | collective-permute-start | bytes 442376 | tf_op jit(solution)/shard_map/ppermute | solution.py:45
  44.8 2.1 %collective-permute-start.18 = (s16[288,256]{1,0:T(8,128)(2,1)S(1)}, s16[288,256]{1,0:T(8,128)(2,1)S(1)}, u32[]{:S(2)}, u32[]{:S(2)}) collective-permute-start(s16[288,256]{1,0:T(8,128)(2,1)S(1)} %get-tuple-element.71), channel_id=1, source_target_pairs={{0,12},{4,8},{8,4},{12,0},{1,13},{5,9},{9,5},{13,1},{2,14},{6,10},... | collective-permute-start | bytes 442376 | tf_op jit(solution)/shard_map/ppermute | solution.py:45
  46.8 0.0 collective-permute-done.15.got_ref
  46.8 0.2 pair.1
  47.0 0.6 %collective-permute-start.19 = (s16[80,512]{1,0:T(8,128)(2,1)S(1)}, s16[80,512]{1,0:T(8,128)(2,1)S(1)}, u32[]{:S(2)}, u32[]{:S(2)}) collective-permute-start(s16[80,512]{1,0:T(8,128)(2,1)S(1)} %get-tuple-element.72), channel_id=1, source_target_pairs={{0,4},{4,0},{8,12},{12,8},{1,5},{5,1},{9,13},{13,9},{2,6},{6,2},{1... | collective-permute-start | bytes 245768 | tf_op jit(solution)/shard_map/ppermute | solution.py:45
  47.6 0.9 %collective-permute-start.20 = (s16[80,512]{1,0:T(8,128)(2,1)S(1)}, s16[80,512]{1,0:T(8,128)(2,1)S(1)}, u32[]{:S(2)}, u32[]{:S(2)}) collective-permute-start(s16[80,512]{1,0:T(8,128)(2,1)S(1)} %get-tuple-element.73), channel_id=1, source_target_pairs={{0,8},{4,12},{8,0},{12,4},{1,9},{5,13},{9,1},{13,5},{2,10},{6,14},... | collective-permute-start | bytes 245768 | tf_op jit(solution)/shard_map/ppermute | solution.py:45
  48.5 1.5 %collective-permute-done.16.refs_0_ = s16[288,256]{1,0:T(8,128)(2,1)S(1)} collective-permute-done((s16[288,256]{1,0:T(8,128)(2,1)S(1)}, s16[288,256]{1,0:T(8,128)(2,1)S(1)}, u32[]{:S(2)}, u32[]{:S(2)}) %collective-permute-start.16) | collective-permute-done | bytes 147488 | tf_op jit(solution)/shard_map/ppermute | solution.py:45
  50.0 0.9 %collective-permute-start.21 = (s16[80,512]{1,0:T(8,128)(2,1)S(1)}, s16[80,512]{1,0:T(8,128)(2,1)S(1)}, u32[]{:S(2)}, u32[]{:S(2)}) collective-permute-start(s16[80,512]{1,0:T(8,128)(2,1)S(1)} %get-tuple-element.74), channel_id=1, source_target_pairs={{0,12},{4,8},{8,4},{12,0},{1,13},{5,9},{9,5},{13,1},{2,14},{6,10},... | collective-permute-start | bytes 245768 | tf_op jit(solution)/shard_map/ppermute | solution.py:45
  50.9 2.5 %collective-permute-done.17.refs_1_ = s16[288,256]{1,0:T(8,128)(2,1)S(1)} collective-permute-done((s16[288,256]{1,0:T(8,128)(2,1)S(1)}, s16[288,256]{1,0:T(8,128)(2,1)S(1)}, u32[]{:S(2)}, u32[]{:S(2)}) %collective-permute-start.17) | collective-permute-done | bytes 147488 | tf_op jit(solution)/shard_map/ppermute | solution.py:45
  53.3 0.0 collective-permute-done.18.refs_2_
  53.3 1.6 %collective-permute-done.19.refs_3_ = s16[80,512]{1,0:T(8,128)(2,1)S(1)} collective-permute-done((s16[80,512]{1,0:T(8,128)(2,1)S(1)}, s16[80,512]{1,0:T(8,128)(2,1)S(1)}, u32[]{:S(2)}, u32[]{:S(2)}) %collective-permute-start.19) | collective-permute-done | bytes 81952 | tf_op jit(solution)/shard_map/ppermute | solution.py:45
  55.0 0.2 collective-permute-done.20.refs_4_
  55.2 1.3 %collective-permute-done.21.refs_5_ = s16[80,512]{1,0:T(8,128)(2,1)S(1)} collective-permute-done((s16[80,512]{1,0:T(8,128)(2,1)S(1)}, s16[80,512]{1,0:T(8,128)(2,1)S(1)}, u32[]{:S(2)}, u32[]{:S(2)}) %collective-permute-start.21) | collective-permute-done | bytes 81952 | tf_op jit(solution)/shard_map/ppermute | solution.py:45
  56.5 0.9 %last.1 = (bf16[1,256,256]{2,1,0:T(8,128)(2,1)}, f32[64,256]{1,0:T(8,128)}, f32[64,256]{1,0:T(8,128)}, f32[2]{0:T(128)}) custom-call(f32[256,256]{1,0:T(8,128)S(1)} %get-tuple-element.65.own_ref, f32[72,512]{1,0:T(8,128)S(1)} %get-tuple-element.68.weight_ref, s16[288,256]{1,0:T(8,128)(2,1)S(1)} %collective-permute-done.16.refs_0_, ...), custom_call_target="tpu_custom_call" | custom-call | flops 1100000000 | bytes 65536 | tf_op jit(solution)/shard_map/last/pallas_call | solution.py:353
  (7 shorter events, 0.0 us)
Async XLA Ops:
  0.6 13.3 %copy-start.7 = (bf16[1,256,256]{2,1,0:T(8,128)(2,1)S(1)}, bf16[1,256,256]{2,1,0:T(8,128)(2,1)}, u32[]{:S(2)}) copy-start(bf16[1,256,256]{2,1,0:T(8,128)(2,1)} %refs_0_.3) | copy-start | bytes 393220
  0.6 13.3 %copy-start.5 = (f32[2]{0:T(128)S(1)}, f32[2]{0:T(128)}, u32[]{:S(2)}) copy-start(f32[2]{0:T(128)} %slopes_ref.7) | copy-start | bytes 28
  0.7 13.3 %copy-start.6 = (s32[1,8]{1,0:T(1,128)S(1)}, s32[1,8]{1,0:T(1,128)}, u32[]{:S(2)}) copy-start(s32[1,8]{1,0:T(1,128)} %bounds_ref.5) | copy-start | bytes 100
  0.7 13.1 %collective-permute-start.2 = (bf16[1,256,256]{2,1,0:T(8,128)(2,1)}, bf16[1,256,256]{2,1,0:T(8,128)(2,1)S(1)}, u32[]{:S(2)}, u32[]{:S(2)}) collective-permute-start(bf16[1,256,256]{2,1,0:T(8,128)(2,1)} %refs_0_.3), channel_id=1, source_target_pairs={{0,12},{4,8},{8,4},{12,0},{1,13},{5,9},{9,5},{13,1},{2,14},{6,10},... | collective-permute-start | bytes 393224 | tf_op jit(solution)/shard_map/ppermute | solution.py:45
  4.6 9.3 %collective-permute-start.1 = (bf16[1,256,256]{2,1,0:T(8,128)(2,1)}, bf16[1,256,256]{2,1,0:T(8,128)(2,1)S(1)}, u32[]{:S(2)}, u32[]{:S(2)}) collective-permute-start(bf16[1,256,256]{2,1,0:T(8,128)(2,1)} %refs_0_.3), channel_id=1, source_target_pairs={{0,8},{4,12},{8,0},{12,4},{1,9},{5,13},{9,1},{13,5},{2,10},{6,14},... | collective-permute-start | bytes 393224 | tf_op jit(solution)/shard_map/ppermute | solution.py:45
  5.1 8.8 %collective-permute-start = (bf16[1,256,256]{2,1,0:T(8,128)(2,1)}, bf16[1,256,256]{2,1,0:T(8,128)(2,1)S(1)}, u32[]{:S(2)}, u32[]{:S(2)}) collective-permute-start(bf16[1,256,256]{2,1,0:T(8,128)(2,1)} %refs_0_.3), channel_id=1, source_target_pairs={{0,4},{4,0},{8,12},{12,8},{1,5},{5,1},{9,13},{13,9},{2,6},{6,2},{1... | collective-permute-start | bytes 393224 | tf_op jit(solution)/shard_map/ppermute | solution.py:45
  10.4 9.9 %collective-permute-start.5 = (bf16[1,256,256]{2,1,0:T(8,128)(2,1)}, bf16[1,256,256]{2,1,0:T(8,128)(2,1)S(1)}, u32[]{:S(2)}, u32[]{:S(2)}) collective-permute-start(bf16[1,256,256]{2,1,0:T(8,128)(2,1)} %get-tuple-element.45.refs_4_), channel_id=1, source_target_pairs={{0,12},{4,8},{8,4},{12,0},{1,13},{5,9},{9,5},{13,1},{2,14},{6,10},... | collective-permute-start | bytes 393224 | tf_op jit(solution)/shard_map/ppermute | solution.py:45
  13.3 7.2 %collective-permute-start.4 = (bf16[1,256,256]{2,1,0:T(8,128)(2,1)}, bf16[1,256,256]{2,1,0:T(8,128)(2,1)S(1)}, u32[]{:S(2)}, u32[]{:S(2)}) collective-permute-start(bf16[1,256,256]{2,1,0:T(8,128)(2,1)} %get-tuple-element.45.refs_4_), channel_id=1, source_target_pairs={{0,8},{4,12},{8,0},{12,4},{1,9},{5,13},{9,1},{13,5},{2,10},{6,14},... | collective-permute-start | bytes 393224 | tf_op jit(solution)/shard_map/ppermute | solution.py:45
  13.8 6.7 %collective-permute-start.3 = (bf16[1,256,256]{2,1,0:T(8,128)(2,1)}, bf16[1,256,256]{2,1,0:T(8,128)(2,1)S(1)}, u32[]{:S(2)}, u32[]{:S(2)}) collective-permute-start(bf16[1,256,256]{2,1,0:T(8,128)(2,1)} %get-tuple-element.45.refs_4_), channel_id=1, source_target_pairs={{0,4},{4,0},{8,12},{12,8},{1,5},{5,1},{9,13},{13,9},{2,6},{6,2},{1... | collective-permute-start | bytes 393224 | tf_op jit(solution)/shard_map/ppermute | solution.py:45
  14.0 1.0 %copy-start.1 = (bf16[1024,256]{1,0:T(8,128)(2,1)S(1)}, bf16[1024,256]{1,0:T(8,128)(2,1)}, u32[]{:S(2)}) copy-start(bf16[1024,256]{1,0:T(8,128)(2,1)} %get-tuple-element.43.key_ref) | copy-start | bytes 1572868
  15.0 9.0 %copy-start.4 = (bf16[1024,256]{1,0:T(8,128)(2,1)S(1)}, bf16[1024,256]{1,0:T(8,128)(2,1)}, u32[]{:S(2)}) copy-start(bf16[1024,256]{1,0:T(8,128)(2,1)} %get-tuple-element.42.val_ref) | copy-start | bytes 1572868
  16.9 6.8 %collective-permute-start.8 = (f32[16,256]{1,0:T(8,128)S(1)}, f32[16,256]{1,0:T(8,128)S(1)}, u32[]{:S(2)}, u32[]{:S(2)}) collective-permute-start(f32[16,256]{1,0:T(8,128)S(1)} %get-tuple-element.47.refs_0_), channel_id=1, source_target_pairs={{0,12},{4,8},{8,4},{12,0},{1,13},{5,9},{9,5},{13,1},{2,14},{6,10},... | collective-permute-start | bytes 49160 | tf_op jit(solution)/shard_map/ppermute | solution.py:45
  19.8 3.9 %collective-permute-start.7 = (f32[16,256]{1,0:T(8,128)S(1)}, f32[16,256]{1,0:T(8,128)S(1)}, u32[]{:S(2)}, u32[]{:S(2)}) collective-permute-start(f32[16,256]{1,0:T(8,128)S(1)} %get-tuple-element.47.refs_0_), channel_id=1, source_target_pairs={{0,8},{4,12},{8,0},{12,4},{1,9},{5,13},{9,1},{13,5},{2,10},{6,14},... | collective-permute-start | bytes 49160 | tf_op jit(solution)/shard_map/ppermute | solution.py:45
  20.3 3.7 %collective-permute-start.6 = (f32[16,256]{1,0:T(8,128)S(1)}, f32[16,256]{1,0:T(8,128)S(1)}, u32[]{:S(2)}, u32[]{:S(2)}) collective-permute-start(f32[16,256]{1,0:T(8,128)S(1)} %get-tuple-element.47.refs_0_), channel_id=1, source_target_pairs={{0,4},{4,0},{8,12},{12,8},{1,5},{5,1},{9,13},{13,9},{2,6},{6,2},{1... | collective-permute-start | bytes 49160 | tf_op jit(solution)/shard_map/ppermute | solution.py:45
  20.5 1.0 %copy-start.3 = (bf16[1024,256]{1,0:T(8,128)(2,1)S(1)}, bf16[1024,256]{1,0:T(8,128)(2,1)}, u32[]{:S(2)}) copy-start(bf16[1024,256]{1,0:T(8,128)(2,1)} %get-tuple-element.42.val_ref) | copy-start | bytes 1572868
  21.5 0.9 %copy-start.8 = (bf16[1,256,256]{2,1,0:T(8,128)(2,1)S(1)}, bf16[1,256,256]{2,1,0:T(8,128)(2,1)}, u32[]{:S(2)}) copy-start(bf16[1,256,256]{2,1,0:T(8,128)(2,1)} %get-tuple-element.45.refs_4_) | copy-start | bytes 393220
  22.4 12.0 %copy-start = (bf16[1024,512]{1,0:T(8,128)(2,1)S(1)}, bf16[1024,512]{1,0:T(8,128)(2,1)}, u32[]{:S(2)}) copy-start(bf16[1024,512]{1,0:T(8,128)(2,1)} %get-tuple-element.54.inp_ref) | copy-start | bytes 3145732
  22.4 12.0 %copy-start.2 = (bf16[1024,256]{1,0:T(8,128)(2,1)S(1)}, bf16[1024,256]{1,0:T(8,128)(2,1)}, u32[]{:S(2)}) copy-start(bf16[1024,256]{1,0:T(8,128)(2,1)} %get-tuple-element.43.key_ref) | copy-start | bytes 1572868
  26.5 6.6 %collective-permute-start.14 = (f32[16,256]{1,0:T(8,128)S(1)}, f32[16,256]{1,0:T(8,128)S(1)}, u32[]{:S(2)}, u32[]{:S(2)}) collective-permute-start(f32[16,256]{1,0:T(8,128)S(1)} %get-tuple-element.52.refs_3_.refs_4_), channel_id=1, source_target_pairs={{0,12},{4,8},{8,4},{12,0},{1,13},{5,9},{9,5},{13,1},{2,14},{6,10},... | collective-permute-start | bytes 49160 | tf_op jit(solution)/shard_map/ppermute | solution.py:45
  29.1 5.2 %collective-permute-start.13 = (f32[16,256]{1,0:T(8,128)S(1)}, f32[16,256]{1,0:T(8,128)S(1)}, u32[]{:S(2)}, u32[]{:S(2)}) collective-permute-start(f32[16,256]{1,0:T(8,128)S(1)} %get-tuple-element.52.refs_3_.refs_4_), channel_id=1, source_target_pairs={{0,8},{4,12},{8,0},{12,4},{1,9},{5,13},{9,1},{13,5},{2,10},{6,14},... | collective-permute-start | bytes 49160 | tf_op jit(solution)/shard_map/ppermute | solution.py:45
  29.6 4.7 %collective-permute-start.12 = (f32[16,256]{1,0:T(8,128)S(1)}, f32[16,256]{1,0:T(8,128)S(1)}, u32[]{:S(2)}, u32[]{:S(2)}) collective-permute-start(f32[16,256]{1,0:T(8,128)S(1)} %get-tuple-element.52.refs_3_.refs_4_), channel_id=1, source_target_pairs={{0,4},{4,0},{8,12},{12,8},{1,5},{5,1},{9,13},{13,9},{2,6},{6,2},{1... | collective-permute-start | bytes 49160 | tf_op jit(solution)/shard_map/ppermute | solution.py:45
  30.1 7.4 %collective-permute-start.9 = (s16[288,256]{1,0:T(8,128)(2,1)S(1)}, s16[288,256]{1,0:T(8,128)(2,1)S(1)}, u32[]{:S(2)}, u32[]{:S(2)}) collective-permute-start(s16[288,256]{1,0:T(8,128)(2,1)S(1)} %get-tuple-element.49), channel_id=1, source_target_pairs={{0,4},{4,0},{8,12},{12,8},{1,5},{5,1},{9,13},{13,9},{2,6},{6,2},{1... | collective-permute-start | bytes 442376 | tf_op jit(solution)/shard_map/ppermute | solution.py:45
  31.7 5.8 %collective-permute-start.10 = (s16[288,256]{1,0:T(8,128)(2,1)S(1)}, s16[288,256]{1,0:T(8,128)(2,1)S(1)}, u32[]{:S(2)}, u32[]{:S(2)}) collective-permute-start(s16[288,256]{1,0:T(8,128)(2,1)S(1)} %get-tuple-element.50), channel_id=1, source_target_pairs={{0,8},{4,12},{8,0},{12,4},{1,9},{5,13},{9,1},{13,5},{2,10},{6,14},... | collective-permute-start | bytes 442376 | tf_op jit(solution)/shard_map/ppermute | solution.py:45
  33.2 6.0 %collective-permute-start.11 = (s16[288,256]{1,0:T(8,128)(2,1)S(1)}, s16[288,256]{1,0:T(8,128)(2,1)S(1)}, u32[]{:S(2)}, u32[]{:S(2)}) collective-permute-start(s16[288,256]{1,0:T(8,128)(2,1)S(1)} %get-tuple-element.51), channel_id=1, source_target_pairs={{0,12},{4,8},{8,4},{12,0},{1,13},{5,9},{9,5},{13,1},{2,14},{6,10},... | collective-permute-start | bytes 442376 | tf_op jit(solution)/shard_map/ppermute | solution.py:45
  43.2 3.6 %collective-permute-start.15 = (f32[264,512]{1,0:T(8,128)S(1)}, f32[264,512]{1,0:T(8,128)S(1)}, u32[]{:S(2)}, u32[]{:S(2)}) collective-permute-start(f32[264,512]{1,0:T(8,128)S(1)} %get-tuple-element.67), channel_id=1, source_target_pairs={{0,16},{16,0},{1,17},{17,1},{2,18},{18,2},{3,19},{19,3},{4,20},{20... | collective-permute-start | bytes 1622024 | tf_op jit(solution)/shard_map/ppermute | solution.py:45
  43.3 6.7 %collective-permute-start.16 = (s16[288,256]{1,0:T(8,128)(2,1)S(1)}, s16[288,256]{1,0:T(8,128)(2,1)S(1)}, u32[]{:S(2)}, u32[]{:S(2)}) collective-permute-start(s16[288,256]{1,0:T(8,128)(2,1)S(1)} %get-tuple-element.69), channel_id=1, source_target_pairs={{0,4},{4,0},{8,12},{12,8},{1,5},{5,1},{9,13},{13,9},{2,6},{6,2},{1... | collective-permute-start | bytes 442376 | tf_op jit(solution)/shard_map/ppermute | solution.py:45
  43.9 9.4 %collective-permute-start.17 = (s16[288,256]{1,0:T(8,128)(2,1)S(1)}, s16[288,256]{1,0:T(8,128)(2,1)S(1)}, u32[]{:S(2)}, u32[]{:S(2)}) collective-permute-start(s16[288,256]{1,0:T(8,128)(2,1)S(1)} %get-tuple-element.70), channel_id=1, source_target_pairs={{0,8},{4,12},{8,0},{12,4},{1,9},{5,13},{9,1},{13,5},{2,10},{6,14},... | collective-permute-start | bytes 442376 | tf_op jit(solution)/shard_map/ppermute | solution.py:45
  44.8 8.6 %collective-permute-start.18 = (s16[288,256]{1,0:T(8,128)(2,1)S(1)}, s16[288,256]{1,0:T(8,128)(2,1)S(1)}, u32[]{:S(2)}, u32[]{:S(2)}) collective-permute-start(s16[288,256]{1,0:T(8,128)(2,1)S(1)} %get-tuple-element.71), channel_id=1, source_target_pairs={{0,12},{4,8},{8,4},{12,0},{1,13},{5,9},{9,5},{13,1},{2,14},{6,10},... | collective-permute-start | bytes 442376 | tf_op jit(solution)/shard_map/ppermute | solution.py:45
  47.0 8.0 %collective-permute-start.19 = (s16[80,512]{1,0:T(8,128)(2,1)S(1)}, s16[80,512]{1,0:T(8,128)(2,1)S(1)}, u32[]{:S(2)}, u32[]{:S(2)}) collective-permute-start(s16[80,512]{1,0:T(8,128)(2,1)S(1)} %get-tuple-element.72), channel_id=1, source_target_pairs={{0,4},{4,0},{8,12},{12,8},{1,5},{5,1},{9,13},{13,9},{2,6},{6,2},{1... | collective-permute-start | bytes 245768 | tf_op jit(solution)/shard_map/ppermute | solution.py:45
  47.6 7.6 %collective-permute-start.20 = (s16[80,512]{1,0:T(8,128)(2,1)S(1)}, s16[80,512]{1,0:T(8,128)(2,1)S(1)}, u32[]{:S(2)}, u32[]{:S(2)}) collective-permute-start(s16[80,512]{1,0:T(8,128)(2,1)S(1)} %get-tuple-element.73), channel_id=1, source_target_pairs={{0,8},{4,12},{8,0},{12,4},{1,9},{5,13},{9,1},{13,5},{2,10},{6,14},... | collective-permute-start | bytes 245768 | tf_op jit(solution)/shard_map/ppermute | solution.py:45
  50.0 6.5 %collective-permute-start.21 = (s16[80,512]{1,0:T(8,128)(2,1)S(1)}, s16[80,512]{1,0:T(8,128)(2,1)S(1)}, u32[]{:S(2)}, u32[]{:S(2)}) collective-permute-start(s16[80,512]{1,0:T(8,128)(2,1)S(1)} %get-tuple-element.74), channel_id=1, source_target_pairs={{0,12},{4,8},{8,4},{12,0},{1,13},{5,9},{9,5},{13,1},{2,14},{6,10},... | collective-permute-start | bytes 245768 | tf_op jit(solution)/shard_map/ppermute | solution.py:45

commit v3 on v2

--- a/solution.py
+++ b/solution.py
@@ -12,7 +12,7 @@
 LOG2E = 1.4426950408889634
 CODE_MAX = 32000.0
 TINY = 1e-30
-CHUNK = 256
+CHUNK = 512
 STEP = 512
 LIM_P, LIM_T, LIM_D, LIM_S, LIM_G = 55, 8, 8, 16, 16
 SCALE = HEAD ** (-0.5)
@@ -53,11 +53,15 @@
 
 
 def decode(steps, exponent):
-    return steps.astype(jnp.int32).astype(F32) * (jnp.exp2(exponent.astype(jnp.int32).astype(F32)) * (1.0 / CODE_MAX))
+    return steps * (jnp.exp2(exponent) * (1.0 / CODE_MAX))
 
 
 def to_code(x):
     return x.astype(jnp.int32).astype(I16)
+
+
+def from_code(x):
+    return x.astype(jnp.int32).astype(F32)
 
 
 def stack_rows(rows, total, width):
@@ -141,15 +145,18 @@
     stats_ref[heads * n : heads * n + 1, :] = jnp.zeros((1, rows), F32) + starts.astype(F32)
 
 
-def dprod_kernel(n, val_ref, *refs):
-    q_refs, g_refs, (dprod_ref, qt_ref, gt_ref) = refs[:n], refs[n : 2 * n], refs[2 * n :]
+def turn_kernel(n, *refs):
+    q_refs, g_refs, (qt_ref, gt_ref) = refs[:n], refs[n : 2 * n], refs[2 * n :]
     rows = q_refs[0].shape[1]
     for j in range(n):
         cols = slice(j * rows, (j + 1) * rows)
         qt_ref[:, cols] = q_refs[j][0].astype(F32).T.astype(BF16)
         gt_ref[:, cols] = g_refs[j][0].astype(F32).T.astype(BF16)
-        for h in range(dprod_ref.shape[0]):
-            dprod_ref[h, :, cols] = nt(val_ref[:, head_cols(h)], g_refs[j][0, :, head_cols(h)])
+
+
+def dprod_kernel(val_ref, gt_ref, _, dprod_ref):
+    for h in range(dprod_ref.shape[0]):
+        dprod_ref[h] = nn(val_ref[:, head_cols(h)], gt_ref[head_cols(h), :])
 
 
 def merged_tops(n, heads, slopes_ref, stats_refs):
@@ -177,9 +184,7 @@
 
 
 def sums_kernel(n, slopes_ref, val_ref, score_ref, gt_ref, *refs):
-    top_refs, (stats_ref, own_ref, expo_ref) = refs[:n], refs[n : n + 3]
-    send_refs = refs[n + 3 : 2 * n + 2]
-    (out_ref,) = refs[2 * n + 2 :]
+    top_refs, (stats_ref, out_ref, expo_ref) = refs[:n], refs[n:]
     heads, tokens, lats = score_ref.shape
     rows = lats // n
     tops, base = merged_tops(n, heads, slopes_ref, top_refs)
@@ -195,28 +200,30 @@
             part_norm = jnp.sum(expo, axis=0, keepdims=True)
             out = term if out is None else out + term
             norm = part_norm if norm is None else norm + part_norm
-        out_ref[...] = out
+        out_ref[head_cols(h), :] = out
         delta = jnp.sum(gt_ref[head_cols(h), :].astype(F32) * out, axis=0, keepdims=True)
         for j in range(n):
             cols = slice(j * rows, (j + 1) * rows)
             stats_ref[h * n + j : h * n + j + 1, :] = norm[:, cols]
             place = heads * n + h * n + j
             stats_ref[place : place + 1, :] = delta[:, cols]
-        own_ref[head_cols(h), :] = out_ref[:, :rows]
-        write_messages(h, n, rows, heads, out_ref, send_refs)
-
-
-def write_messages(h, n, rows, heads, sums_ref, send_refs):
-    for j in range(1, n):
+
+
+def write_messages(i, rows, sums_ref, send_refs):
+    for j, ref in enumerate(send_refs, 1):
         steps, exponent = encode(sums_ref[:, j * rows : (j + 1) * rows])
-        send_refs[j - 1][head_cols(h), :] = to_code(steps)
-        place = heads * HEAD + h * 16
-        send_refs[j - 1][place : place + 16, :] = to_code(jnp.broadcast_to(exponent, (16, rows)))
-
-
-def read_message(ref, h, heads):
-    place = heads * HEAD + h * 16
-    return decode(ref[head_cols(h), :], ref[place : place + 16, :][0:1, :])
+        ref[head_cols(i), :] = to_code(steps)
+        place = slice(ref.shape[0] - 16, ref.shape[0])
+        exponents = jnp.broadcast_to(exponent, (16, rows))
+        if i:
+            row = lax.broadcasted_iota(jnp.int32, (16, rows), 0)
+            exponents = jnp.where(row < i, from_code(ref[place, :]), exponents)
+        ref[place, :] = to_code(exponents)
+
+
+def read_message(ref, i):
+    exponents = from_code(ref[ref.shape[0] - 16 :, :])
+    return decode(from_code(ref[head_cols(i), :]), exponents[i : i + 1, :])
 
 
 def merged_sums(n, heads, stats_refs):
@@ -238,92 +245,101 @@
     return norms, deltas
 
 
-def grads_kernel(n, h, heads, bounds_ref, slopes_ref, inp_ref, key_ref, expo_ref, dprod_ref, qt_ref, gt_ref, *refs):
+def rows_kernel(n, bounds_ref, slopes_ref, key_ref, expo_ref, dprod_ref, out_ref, *refs):
     top_refs, sum_refs, refs = refs[:n], refs[n : 2 * n], refs[2 * n :]
-    outs = n + 2
-    old, _, refs = (refs[:outs], refs[outs], refs[outs + 1 :]) if h else (None, None, refs)
-    own_ref, keep_ref, give_ref = refs[:3]
-    send_refs = refs[3:outs]
-    episode_ref, dq_ref, tok_ref, weight_ref = refs[outs:]
-    _, tokens, lats = expo_ref.shape
+    own_ref, grad_ref, slope_ref = refs[:3]
+    send_refs = refs[3 : n + 2]
+    (episode_ref,) = refs[n + 2 :]
+    heads, tokens, lats = expo_ref.shape
+    rows = lats // n
     _, base = merged_tops(n, heads, slopes_ref, top_refs)
     norms, deltas = merged_sums(n, heads, sum_refs)
     fill_episode(bounds_ref, episode_ref, base[:, :128])
-    inverse = 1.0 / norms[h]
-    mean = deltas[h] * inverse
-    slope = jnp.zeros((1, 128), F32)
-    dq = None
-    for c in range(tokens // STEP):
-        part = slice(c * STEP, (c + 1) * STEP)
-        probs = expo_ref[h, part, :] * inverse
-        tok_ref[HEAD:, part] = nt(gt_ref[head_cols(h), :], probs.astype(BF16)).astype(BF16)
-        score_grad = probs * (dprod_ref[h, part, :] - mean)
-        folded = score_grad[:, :128]
-        for i in range(1, lats // 128):
-            folded = folded + score_grad[:, i * 128 : (i + 1) * 128]
-        slope = slope + jnp.sum(folded * episode_ref[part, :], axis=0, keepdims=True)
-        score_grad_b = score_grad.astype(BF16)
-        tok_ref[:HEAD, part] = (SCALE * nt(qt_ref[head_cols(h), :], score_grad_b)).astype(BF16)
-        term = tn(key_ref[part, head_cols(h)], score_grad_b)
-        dq = term if dq is None else dq + term
-    dq_ref[...] = dq
-    if h:
-        done, cols = h * HEAD, h * 2 * HEAD
-        own_ref[:done, :] = old[0][:done, :]
-        keep_ref[:, :cols] = old[1][:, :cols]
-        give_ref[:, :cols] = old[2][:, :cols]
-        for ref, was in zip(send_refs, old[3:]):
-            ref[:done, :] = was[:done, :]
-            ref[heads * HEAD : heads * HEAD + 16 * h, :] = was[heads * HEAD : heads * HEAD + 16 * h, :]
-    rows = lats // n
-    own_ref[head_cols(h), :] = dq_ref[:, :rows]
-    write_messages(h, n, rows, heads, dq_ref, send_refs)
-    half = keep_ref.shape[0] - 8
+    for h in range(heads):
+        inverse = 1.0 / norms[h]
+        mean = deltas[h] * inverse
+        slope = jnp.zeros((1, 128), F32)
+        dq = None
+        for c in range(tokens // STEP):
+            part = slice(c * STEP, (c + 1) * STEP)
+            score_grad = expo_ref[h, part, :] * inverse * (dprod_ref[h, part, :] - mean)
+            folded = score_grad[:, :128]
+            for i in range(1, lats // 128):
+                folded = folded + score_grad[:, i * 128 : (i + 1) * 128]
+            slope = slope + jnp.sum(folded * episode_ref[part, :], axis=0, keepdims=True)
+            score_grad_b = score_grad.astype(BF16)
+            grad_ref[h, part, :] = score_grad_b
+            term = tn(key_ref[part, head_cols(h)], score_grad_b)
+            dq = term if dq is None else dq + term
+        own_ref[head_cols(h), :] = dq[:, :rows]
+        write_messages(2 * h, rows, dq, send_refs)
+        write_messages(2 * h + 1, rows, out_ref[head_cols(h), :], send_refs)
+        total = jnp.sum(slope, axis=1, keepdims=True)
+        slope_ref[:, h * 2 * HEAD : (h + 1) * 2 * HEAD] = jnp.broadcast_to(total, (8, 2 * HEAD))
+
+
+def tokens_kernel(n, expo_ref, grad_ref, qt_ref, gt_ref, *refs):
+    sum_refs, tok_ref = refs[:n], refs[-1]
+    heads, tokens, lats = expo_ref.shape
+    norms, _ = merged_sums(n, heads, sum_refs)
+    for h in range(heads):
+        inverse = 1.0 / norms[h]
+        at = h * 2 * HEAD
+        for c in range(tokens // STEP):
+            part = slice(c * STEP, (c + 1) * STEP)
+            probs = (expo_ref[h, part, :] * inverse).astype(BF16)
+            keys = SCALE * nt(qt_ref[head_cols(h), :], grad_ref[h, part, :])
+            tok_ref[at : at + HEAD, part] = keys.astype(BF16)
+            tok_ref[at + HEAD : at + 2 * HEAD, part] = nt(gt_ref[head_cols(h), :], probs).astype(BF16)
+
+
+def weights_kernel(n, inp_ref, tok_ref, slope_ref, _, keep_ref, *refs):
+    give_refs, weight_ref = refs[:n], refs[n]
+    _, half, _ = weight_ref.shape
+    piece = half // n
     for i in range(2):
         side = inp_ref[:, i * half : (i + 1) * half]
         weight_ref[i] = lax.dot_general(side, tok_ref[...], (((0,), (1,)), ((), ())), preferred_element_type=F32)
-    core = lax.axis_index("dp")
-    cols = slice(h * 2 * HEAD, (h + 1) * 2 * HEAD)
-    total = jnp.broadcast_to(jnp.sum(slope, axis=1, keepdims=True), (8, 2 * HEAD))
-    keep_ref[:half, cols] = weight_ref[core]
-    give_ref[:half, cols] = weight_ref[1 - core]
-    keep_ref[half:, cols] = total
-    give_ref[half:, cols] = total
-
-
-def pair_kernel(n, heads, keep_ref, got_ref, own_ref, *send_refs):
-    me = lax.axis_index("seq")
-    half = keep_ref.shape[0] - 8
-    piece = half // n
-    width = keep_ref.shape[1]
-    slopes = keep_ref[half:, :] + got_ref[half:, :]
-    value = slopes[0:1, :]
-    steps, exponent = encode(value)
-    left = value * (jnp.exp2(-exponent) * CODE_MAX) - steps
-    digits = [exponent, steps, jnp.round(left * CODE_MAX)]
-    for k in range(n):
+    core, me = lax.axis_index("dp"), lax.axis_index("seq")
+    for k, give_ref in enumerate(give_refs):
         rows = pl.ds(pl.multiple_of((me ^ k) * piece, piece), piece)
-        total = keep_ref[rows, :] + got_ref[rows, :]
-        if k == 0:
-            own_ref[:piece, :] = total
-            own_ref[piece:, :] = slopes
-        else:
-            steps, exponent = encode(total)
-            send_refs[k - 1][:piece, :] = to_code(steps)
-            send_refs[k - 1][piece:, :] = to_code(stack_rows([exponent] + digits, 16, width))
-
-
-def attended_kernel(n, heads, own_ref, *refs):
-    got_refs, sum_refs, out_ref = refs[: n - 1], refs[n - 1 : 2 * n - 1], refs[2 * n - 1]
-    refs[2 * n][...] = jnp.zeros_like(refs[2 * n])
-    rows = own_ref.shape[1]
+        keep_ref[k, :piece, :] = weight_ref[core, rows, :]
+        give_ref[:piece, :] = weight_ref[1 - core, rows, :]
+    keep_ref[0, piece:, :] = slope_ref[...]
+    give_refs[0][piece:, :] = slope_ref[...]
+
+
+def pair_kernel(n, heads, keep_ref, *refs):
+    got_refs, own_ref, send_refs = refs[:n], refs[-n], refs[1 - n :]
+    piece = keep_ref.shape[1] - 8
+    width = 2 * HEAD
+    own_ref[...] = keep_ref[0] + got_refs[0][...]
+    digits = []
+    for h in range(heads):
+        value = own_ref[piece : piece + 1, h * width : (h + 1) * width]
+        steps, exponent = encode(value)
+        left = value * (jnp.exp2(-exponent) * CODE_MAX) - steps
+        digits += [exponent, steps, jnp.round(left * CODE_MAX)]
+    for k in range(1, n):
+        total = keep_ref[k, :piece, :] + got_refs[k][...]
+        exponents = []
+        for h in range(heads):
+            steps, exponent = encode(total[:, h * width : (h + 1) * width])
+            send_refs[k - 1][h * piece : (h + 1) * piece, :] = to_code(steps)
+            exponents.append(exponent)
+        send_refs[k - 1][heads * piece :, :] = to_code(stack_rows(exponents + digits, 16, width))
+
+
+def attended_kernel(n, heads, out_ref, *refs):
+    got_refs, sum_refs, att_ref = refs[: n - 1], refs[n - 1 : 2 * n - 1], refs[2 * n - 1]
+    rows = att_ref.shape[1]
     norms, _ = merged_sums(n, heads, sum_refs)
     for h in range(heads):
-        total = own_ref[head_cols(h), :]
+        total = out_ref[head_cols(h), :rows]
         for ref in got_refs:
-            total = total + read_message(ref, h, heads)
+            total = total + read_message(ref, 2 * h + 1)
         total = total / norms[h][:, :rows]
-        out_ref[0, :, head_cols(h)] = total.T.astype(BF16)
+        att_ref[0, :, head_cols(h)] = total.T.astype(BF16)
 
 
 def last_kernel(n, heads, own_ref, weight_ref, *refs):
@@ -332,24 +348,26 @@
     for h in range(heads):
         total = own_ref[head_cols(h), :]
         for ref in got_refs:
-            total = total + read_message(ref, h, heads)
+            total = total + read_message(ref, 2 * h)
         grad_ref[0, :, head_cols(h)] = (SCALE * total).T.astype(BF16)
     piece = weight_ref.shape[0] - 8
-    total = weight_ref[:piece, :]
-    slopes = weight_ref[piece : piece + 1, :]
-    for ref in part_refs:
-        extra = ref[piece:, :].astype(jnp.int32).astype(F32)
-        total = total + ref[:piece, :].astype(jnp.int32).astype(F32) * (jnp.exp2(extra[0:1, :]) * (1.0 / CODE_MAX))
-        exponent, steps, left = (extra[i : i + 1, :] for i in range(1, 4))
-        slopes = slopes + (steps + left * (1.0 / CODE_MAX)) * (jnp.exp2(exponent) * (1.0 / CODE_MAX))
-    for h in range(heads):
-        at = h * 2 * HEAD
-        key_ref[:, head_cols(h)] = total[:, at : at + HEAD]
-        val_ref[:, head_cols(h)] = total[:, at + HEAD : at + 2 * HEAD]
-        slope_ref[h] = slopes[0, at]
-
-
-def call(kernel, name, outs, args, us, scratch=(), smem=0, limit=8 << 20, ins=None, out_specs=None):
+    width = 2 * HEAD
+    extras = [from_code(ref[heads * piece :, :]) for ref in part_refs]
+    for h in range(heads):
+        cols = slice(h * width, (h + 1) * width)
+        total = weight_ref[:piece, cols]
+        slope = weight_ref[piece : piece + 1, cols]
+        for ref, extra in zip(part_refs, extras):
+            total = total + decode(from_code(ref[h * piece : (h + 1) * piece, :]), extra[h : h + 1, :])
+            place = heads + 3 * h
+            exponent, steps, left = (extra[place + i : place + i + 1, :] for i in range(3))
+            slope = slope + decode(steps + left * (1.0 / CODE_MAX), exponent)
+        key_ref[:, head_cols(h)] = total[:, :HEAD]
+        val_ref[:, head_cols(h)] = total[:, HEAD:]
+        slope_ref[h] = slope[0, 0]
+
+
+def call(kernel, name, outs, args, us, scratch=(), smem=0, limit=12 << 20, ins=None, out_specs=None):
     return pl.pallas_call(
         kernel,
         out_shape=[jax.ShapeDtypeStruct(shape, dtype) for shape, dtype in outs],
@@ -374,10 +392,9 @@
         prep_kernel,
         "prep",
         [((toks, channels), BF16), ((toks, width), BF16), ((toks, width), BF16), (cotangent.shape, BF16)],
-        (*prep_args, cotangent),
+        [pltpu.with_memory_space_constraint(x, pltpu.HBM) for x in (*prep_args, cotangent)],
         3,
         [pltpu.VMEM(a.shape, a.dtype) for a in prep_args] + [pltpu.SemaphoreType.DMA((5 + toks // CHUNK,))],
-        limit=LIM_P << 20,
         ins=[pl.BlockSpec(memory_space=pltpu.HBM)] * 6,
     )
     g_all = [grad] + [swap(grad, "seq", k, n) for k in peers]
@@ -394,62 +411,68 @@
         limit=LIM_T << 20,
     )
     tops = [top_own] + [swap(top_own, "seq", k, n) for k in peers]
-    dprod, q_turned, g_turned = call(
-        functools.partial(dprod_kernel, n),
-        "dprod",
-        [square, ((width, lats), BF16), ((width, lats), BF16)],
-        (values, *q_all, *g_all),
-        2,
-        limit=LIM_D << 20,
-    )
-    message = ((heads * HEAD + 16 * heads, rows), I16)
-    partial = pltpu.VMEM((HEAD, lats), F32)
+    q_turned, g_turned = call(
+        functools.partial(turn_kernel, n),
+        "turn",
+        [((width, lats), BF16), ((width, lats), BF16)],
+        (*q_all, cotangent, *g_all[1:]),
+        1,
+    )
     sums = call(
         functools.partial(sums_kernel, n),
         "sums",
-        [((2 * heads * n, rows), F32), ((width, rows), F32), square] + [message] * (n - 1),
+        [((2 * heads * n, rows), F32), ((width, lats), F32), square],
         (slopes, values, scores, g_turned, *tops),
         2,
-        [partial],
+        smem=1,
+        limit=LIM_S << 20,
+    )
+    norms = [sums[0]] + [swap(sums[0], "seq", k, n) for k in peers]
+    (dprod,) = call(dprod_kernel, "dprod", [square], (values, g_turned, sums[0]), 2, limit=LIM_D << 20)
+    own_dq, score_grads, slope_terms, *sends = call(
+        functools.partial(rows_kernel, n),
+        "rows",
+        [((width, rows), F32), ((heads, toks, lats), BF16), ((8, 2 * width), F32)]
+        + [((2 * width + 16, rows), I16)] * (n - 1),
+        (boundaries, slopes, keys, sums[2], dprod, sums[1], *tops, *norms),
+        3,
+        [pltpu.VMEM((toks, 128), F32)],
+        2,
+        limit=LIM_G << 20,
+    )
+    blocks = [swap(x, "seq", k, n) for k, x in zip(peers, sends)]
+    half = channels // 2
+    (tok_grads,) = call(
+        functools.partial(tokens_kernel, n),
+        "tokens",
+        [((2 * width, toks), BF16)],
+        (sums[2], score_grads, q_turned, g_turned, *norms),
+        3,
+        limit=LIM_G << 20,
+    )
+    piece = half // n
+    weights = call(
+        functools.partial(weights_kernel, n),
+        "weights",
+        [((n, piece + 8, 2 * width), F32), ((piece + 8, 2 * width), F32)] + [((piece, 2 * width), F32)] * (n - 1),
+        (inputs, tok_grads, slope_terms, blocks[0]),
         1,
-        limit=LIM_S << 20,
-    )
-    norms = [sums[0]] + [swap(sums[0], "seq", k, n) for k in peers]
-    outs = [swap(sums[2 + k], "seq", k, n) for k in peers]
-    half = channels // 2
-    grads = attended = ()
-    for h in range(heads):
-        grads = call(
-            functools.partial(grads_kernel, n, h, heads),
-            f"grads{h}",
-            [((width, rows), F32)] + [((half + 8, 2 * width), F32)] * 2 + [message] * (n - 1),
-            (boundaries, slopes, inputs, keys, sums[2], dprod, q_turned, g_turned, *tops, *norms, *grads, *attended[1:]),
-            2,
-            [
-                pltpu.VMEM((toks, 128), F32),
-                partial,
-                pltpu.VMEM((2 * HEAD, toks), BF16),
-                pltpu.VMEM((2, half, 2 * HEAD), F32),
-            ],
-            2,
-            limit=LIM_G << 20,
-        )
-        if h == 0:
-            attended = call(
-                functools.partial(attended_kernel, n, heads),
-                "attended",
-                [((1, rows, width), BF16), ((8, 128), F32)],
-                (sums[1], *outs, *norms),
-                1,
-            )
-    got = swap(grads[2], "dp", 1, 2)
-    dqs = [swap(grads[2 + k], "seq", k, n) for k in peers]
-    piece = half // n
+        [pltpu.VMEM((2, half, 2 * width), F32)],
+        limit=LIM_G << 20,
+    )
+    got = [swap(x, "dp", 1, 2) for x in weights[1:]]
+    (attended,) = call(
+        functools.partial(attended_kernel, n, heads),
+        "attended",
+        [((1, rows, width), BF16)],
+        (sums[1], *blocks, *norms),
+        1,
+    )
     pair = call(
         functools.partial(pair_kernel, n, heads),
         "pair",
-        [((piece + 8, 2 * width), F32)] + [((piece + 16, 2 * width), I16)] * (n - 1),
-        (grads[1], got),
+        [((piece + 8, 2 * width), F32)] + [((heads * piece + 16, 2 * HEAD), I16)] * (n - 1),
+        (weights[0], *got, blocks[1]),
         0.3,
     )
     parts = [swap(pair[k], "seq", k, n) for k in peers]
@@ -457,11 +480,11 @@
         functools.partial(last_kernel, n, heads),
         "last",
         [((1, rows, width), BF16), ((piece, width), F32), ((piece, width), F32), ((heads,), F32)],
-        (grads[0], pair[0], *dqs, *parts),
+        (own_dq, pair[0], *blocks, *parts),
         1,
         out_specs=[VMEM] * 3 + [SMEM],
     )
-    return (attended[0], *last)
+    return (attended, *last)
 
 
 def carried_in(part, axis, combine, identity):

time: 57.7 us -> 53.2 us (0.922)
  local copies, waits for them, and re-layouts: 3 us -> 0.02 us
  waiting for transfers between devices: 9.57 us -> 11.8 us
  starting transfers between devices: 25.2 us -> 23 us
  Pallas kernels: 18.9 us -> 17.5 us
    unnamed x18 -> x8, local copies, waits for them, and re-layouts: 3 us -> 0.02 us
    ppermute x22, waiting for transfers between devices: 9.57 us -> 11.8 us  [swap(): return lax.ppermute(x, axis, [(i, i ^ k) for i in range(n)])]
    ppermute x22, starting transfers between devices: 25.2 us -> 23 us  [swap(): return lax.ppermute(x, axis, [(i, i ^ k) for i in range(n)])]
    pallas_call x9 -> x11, Pallas kernels: 18.9 us -> 17.5 us  [call(): pl.pallas_call(kernel, out_shape=[jax.ShapeDtypeStruct(shape, dtype) for...]
  transfers between devices with their start and end apart: 22 -> 22, of which waited for: 8 -> 11; matrix products, arithmetic and copies ran while one was open for 0% -> 0% of each run, Pallas kernels for 20% -> 21%
where the time goes in v3:
time: 53.2 us; the launch traced here: 53.1 us
  starting transfers between devices  23 us (43%)
  Pallas kernels  17.5 us (33%)
  waiting for transfers between devices  11.8 us (22%)
  between operations  0.79 us (1%)
    ppermute x22, starting transfers between devices, swap(): return lax.ppermute(x, axis, [(i, i ^ k) for i in range(n)])  23 us
    pallas_call x11, Pallas kernels, call(): pl.pallas_call(kernel, out_shape=[jax.ShapeDtypeStruct(shape, dtype) for...  17.5 us
    ppermute x22, waiting for transfers between devices, swap(): return lax.ppermute(x, axis, [(i, i ^ k) for i in range(n)])  11.8 us
  transfers between devices with their start and end apart: 22, of which 11 were waited for; matrix products, arithmetic and copies ran while one was open for 0% of the time, Pallas kernels for 21%

profile of v3, /device:TPU:0, one launch (start us, length us, event | category | flops | bytes accessed | tf_op | source)
XLA Modules:
  0.0 53.1 jit_solution(16675902601666691550)
XLA Ops:
  0.6 0.0 copy-start.3
  0.6 0.0 copy-start.2
  0.7 0.0 copy-start
  0.7 0.0 copy-start.1
  0.7 4.0 %collective-permute-start.2 = (bf16[1,256,256]{2,1,0:T(8,128)(2,1)}, bf16[1,256,256]{2,1,0:T(8,128)(2,1)S(1)}, u32[]{:S(2)}, u32[]{:S(2)}) collective-permute-start(bf16[1,256,256]{2,1,0:T(8,128)(2,1)} %refs_0_.3), channel_id=1, source_target_pairs={{0,12},{4,8},{8,4},{12,0},{1,13},{5,9},{9,5},{13,1},{2,14},{6,10},... | collective-permute-start | bytes 393224 | tf_op jit(solution)/shard_map/ppermute | solution.py:45
  4.6 0.5 collective-permute-start.1
  5.1 0.1 collective-permute-start
  5.3 3.3 %prep.1 = (bf16[1024,512]{1,0:T(8,128)(2,1)S(1)}, bf16[1024,256]{1,0:T(8,128)(2,1)S(1)}, bf16[1024,256]{1,0:T(8,128)(2,1)S(1)}, bf16[1,256,256]{2,1,0:T(8,128)(2,1)S(1)}) custom-call(bf16[1,1024,512]{2,1,0:T(8,128)(2,1)} %tok_hbm.1, s32[1,1024]{1,0:T(1,128)} %lev_hbm.1, f32[256,512]{1,0:T(8,128)} %table_hbm.1, bf16[512,256]{1,0:T(8,128)(2,1)} %wk_hbm.1, ...), custom_call_target="tpu_custom_call" | custom-call | flops 3300000000 | bytes 65536 | tf_op jit(solution)/shard_map/prep/pallas_call | solution.py:371
  8.6 2.9 %collective-permute-start.5 = (bf16[1,256,256]{2,1,0:T(8,128)(2,1)S(1)}, bf16[1,256,256]{2,1,0:T(8,128)(2,1)S(1)}, u32[]{:S(2)}, u32[]{:S(2)}) collective-permute-start(bf16[1,256,256]{2,1,0:T(8,128)(2,1)S(1)} %get-tuple-element.38), channel_id=1, source_target_pairs={{0,12},{4,8},{8,4},{12,0},{1,13},{5,9},{9,5},{13,1},{2,14},{6,10},... | collective-permute-start | bytes 393224 | tf_op jit(solution)/shard_map/ppermute | solution.py:45
  11.5 0.5 collective-permute-start.4
  12.0 0.0 collective-permute-done.2.refs_3_
  12.0 0.1 collective-permute-start.3
  12.1 0.0 collective-permute-done.1.refs_2_
  12.1 0.0 collective-permute-done.refs_1_
  12.1 0.0 copy-done.3
  12.1 0.0 copy-done
  12.1 0.0 copy-done.1
  12.2 1.9 %tops.1 = (f32[16,256]{1,0:T(8,128)S(1)}, f32[2,1024,1024]{2,1,0:T(8,128)S(1)}) custom-call(s32[1,8]{1,0:T(1,128)S(1)} %copy-done.1, f32[2]{0:T(128)S(1)} %copy-done, bf16[1024,256]{1,0:T(8,128)(2,1)S(1)} %get-tuple-element.36.key_ref, bf16[1,256,256]{2,1,0:T(8,128)(2,1)S(1)} %copy-done.3, bf16[1,256,256]{2,1,0:T(8,128)(2,1)S(1)} %collective-permute-done.refs_1_, ...), custom_call_target="tpu_custom_call" | custom-call | flops 2200000000 | bytes 65536 | tf_op jit(solution)/shard_map/tops/pallas_call | solution.py:371
  14.0 2.9 %collective-permute-start.8 = (f32[16,256]{1,0:T(8,128)S(1)}, f32[16,256]{1,0:T(8,128)S(1)}, u32[]{:S(2)}, u32[]{:S(2)}) collective-permute-start(f32[16,256]{1,0:T(8,128)S(1)} %get-tuple-element.40.refs_0_), channel_id=1, source_target_pairs={{0,12},{4,8},{8,4},{12,0},{1,13},{5,9},{9,5},{13,1},{2,14},{6,10},... | collective-permute-start | bytes 49160 | tf_op jit(solution)/shard_map/ppermute | solution.py:45
  16.9 0.5 collective-permute-start.7
  17.4 0.0 collective-permute-done.5.refs_7_
  17.4 0.1 collective-permute-start.6
  17.6 0.0 collective-permute-done.4.refs_6_
  17.6 0.0 collective-permute-done.3.refs_5_
  17.6 0.0 copy-done.2
  17.6 0.3 turn.1
  17.9 0.9 %collective-permute-done.8.refs_3_ = f32[16,256]{1,0:T(8,128)S(1)} collective-permute-done((f32[16,256]{1,0:T(8,128)S(1)}, f32[16,256]{1,0:T(8,128)S(1)}, u32[]{:S(2)}, u32[]{:S(2)}) %collective-permute-start.8) | collective-permute-done | bytes 16416 | tf_op jit(solution)/shard_map/ppermute | solution.py:45
  18.9 1.8 %collective-permute-done.7.refs_2_ = f32[16,256]{1,0:T(8,128)S(1)} collective-permute-done((f32[16,256]{1,0:T(8,128)S(1)}, f32[16,256]{1,0:T(8,128)S(1)}, u32[]{:S(2)}, u32[]{:S(2)}) %collective-permute-start.7) | collective-permute-done | bytes 16416 | tf_op jit(solution)/shard_map/ppermute | solution.py:45
  20.7 0.5 collective-permute-done.6.refs_1_
  21.2 2.4 %sums.1 = (f32[16,256]{1,0:T(8,128)S(1)}, f32[256,1024]{1,0:T(8,128)S(1)}, f32[2,1024,1024]{2,1,0:T(8,128)S(1)}) custom-call(f32[2]{0:T(128)S(1)} %copy-done, bf16[1024,256]{1,0:T(8,128)(2,1)S(1)} %get-tuple-element.35.val_ref, f32[2,1024,1024]{2,1,0:T(8,128)S(1)} %get-tuple-element.37.score_ref, bf16[256,1024]{1,0:T(8,128)(2,1)S(1)} %get-tuple-element.39.gt_ref, ...), custom_call_target="tpu_custom_call" | custom-call | flops 2200000000 | bytes 65536 | tf_op jit(solution)/shard_map/sums/pallas_call | solution.py:371
  23.6 1.6 %collective-permute-start.11 = (f32[16,256]{1,0:T(8,128)S(1)}, f32[16,256]{1,0:T(8,128)S(1)}, u32[]{:S(2)}, u32[]{:S(2)}) collective-permute-start(f32[16,256]{1,0:T(8,128)S(1)} %get-tuple-element.43._.refs_4_.refs_3_.refs_0_), channel_id=1, source_target_pairs={{0,12},{4,8},{8,4},{12,0},{1,13},{5,9},{9,5},{13,1},{2,14},{6,10},... | collective-permute-start | bytes 49160 | tf_op jit(solution)/shard_map/ppermute | solution.py:45
  25.1 0.1 collective-permute-start.10
  25.2 1.9 %collective-permute-start.9 = (f32[16,256]{1,0:T(8,128)S(1)}, f32[16,256]{1,0:T(8,128)S(1)}, u32[]{:S(2)}, u32[]{:S(2)}) collective-permute-start(f32[16,256]{1,0:T(8,128)S(1)} %get-tuple-element.43._.refs_4_.refs_3_.refs_0_), channel_id=1, source_target_pairs={{0,4},{4,0},{8,12},{12,8},{1,5},{5,1},{9,13},{13,9},{2,6},{6,2},{1... | collective-permute-start | bytes 49160 | tf_op jit(solution)/shard_map/ppermute | solution.py:45
  27.1 1.2 %dprod.1.dprod_ref = f32[2,1024,1024]{2,1,0:T(8,128)S(1)} custom-call(bf16[1024,256]{1,0:T(8,128)(2,1)S(1)} %get-tuple-element.35.val_ref, bf16[256,1024]{1,0:T(8,128)(2,1)S(1)} %get-tuple-element.39.gt_ref, f32[16,256]{1,0:T(8,128)S(1)} %get-tuple-element.43._.refs_4_.refs_3_.refs_0_), custom_call_target="tpu_custom_call" | custom-call | flops 2200000000 | bytes 65536 | tf_op jit(solution)/shard_map/dprod/pallas_call | solution.py:371
  28.4 0.0 collective-permute-done.11.refs_7_.refs_6_.refs_3_
  28.4 0.5 collective-permute-done.10.refs_6_.refs_5_.refs_2_
  28.9 0.1 collective-permute-done.9.refs_5_.refs_4_.refs_1_
  29.0 2.8 %rows.1 = (f32[256,256]{1,0:T(8,128)S(1)}, bf16[2,1024,1024]{2,1,0:T(8,128)(2,1)S(1)}, f32[8,512]{1,0:T(8,128)S(1)}, s16[528,256]{1,0:T(8,128)(2,1)S(1)}, s16[52...) custom-call(s32[1,8]{1,0:T(1,128)S(1)} %copy-done.1, f32[2]{0:T(128)S(1)} %copy-done, ...), custom_call_target="tpu_custom_call" | custom-call | flops 3300000000 | bytes 65536 | tf_op jit(solution)/shard_map/rows/pallas_call | solution.py:371
  31.8 2.0 %collective-permute-start.12 = (s16[528,256]{1,0:T(8,128)(2,1)S(1)}, s16[528,256]{1,0:T(8,128)(2,1)S(1)}, u32[]{:S(2)}, u32[]{:S(2)}) collective-permute-start(s16[528,256]{1,0:T(8,128)(2,1)S(1)} %get-tuple-element.44), channel_id=1, source_target_pairs={{0,4},{4,0},{8,12},{12,8},{1,5},{5,1},{9,13},{13,9},{2,6},{6,2},{1... | collective-permute-start | bytes 811016 | tf_op jit(solution)/shard_map/ppermute | solution.py:45
  33.7 1.5 %collective-permute-start.13 = (s16[528,256]{1,0:T(8,128)(2,1)S(1)}, s16[528,256]{1,0:T(8,128)(2,1)S(1)}, u32[]{:S(2)}, u32[]{:S(2)}) collective-permute-start(s16[528,256]{1,0:T(8,128)(2,1)S(1)} %get-tuple-element.45), channel_id=1, source_target_pairs={{0,8},{4,12},{8,0},{12,4},{1,9},{5,13},{9,1},{13,5},{2,10},{6,14},... | collective-permute-start | bytes 811016 | tf_op jit(solution)/shard_map/ppermute | solution.py:45
  35.3 0.1 collective-permute-start.14
  35.3 2.9 %tokens.1.tok_ref = bf16[512,1024]{1,0:T(8,128)(2,1)S(1)} custom-call(f32[2,1024,1024]{2,1,0:T(8,128)S(1)} %get-tuple-element.42.expo_ref, bf16[2,1024,1024]{2,1,0:T(8,128)(2,1)S(1)} %get-tuple-element.49.grad_ref, bf16[256,1024]{1,0:T(8,128)(2,1)S(1)} %get-tuple-element.50.qt_ref, bf16[256,1024]{1,0:T(8,128)(2,1)S(1)} %get-tuple-element.39.gt_ref, ...), custom_call_target="tpu_custom_call" | custom-call | flops 3300000000 | bytes 65536 | tf_op jit(solution)/shard_map/tokens/pallas_call | solution.py:371
  38.2 1.1 %collective-permute-done.12.refs_0_._ = s16[528,256]{1,0:T(8,128)(2,1)S(1)} collective-permute-done((s16[528,256]{1,0:T(8,128)(2,1)S(1)}, s16[528,256]{1,0:T(8,128)(2,1)S(1)}, u32[]{:S(2)}, u32[]{:S(2)}) %collective-permute-start.12) | collective-permute-done | bytes 270368 | tf_op jit(solution)/shard_map/ppermute | solution.py:45
  39.3 0.8 %weights.1 = (f32[4,72,512]{2,1,0:T(8,128)S(1)}, f32[72,512]{1,0:T(8,128)S(1)}, f32[64,512]{1,0:T(8,128)S(1)}, f32[64,512]{1,0:T(8,128)S(1)}, f32[64,512]{1,0:T(8,128)S(1)}) custom-call(bf16[1024,512]{1,0:T(8,128)(2,1)S(1)} %get-tuple-element.48.inp_ref, bf16[512,1024]{1,0:T(8,128)(2,1)S(1)} %tokens.1.tok_ref, f32[8,512]{1,0:T(8,128)S(1)} %get-tuple-element.51.slope_ref, ...), custom_call_target="tpu_custom_call" | custom-call | flops 1100000000 | bytes 65536 | tf_op jit(solution)/shard_map/weights/pallas_call | solution.py:371
  40.1 0.1 collective-permute-start.15
  40.2 0.5 collective-permute-start.16
  40.7 0.1 collective-permute-start.17
  40.8 2.6 %collective-permute-done.13.refs_1_.refs_4_ = s16[528,256]{1,0:T(8,128)(2,1)S(1)} collective-permute-done((s16[528,256]{1,0:T(8,128)(2,1)S(1)}, s16[528,256]{1,0:T(8,128)(2,1)S(1)}, u32[]{:S(2)}, u32[]{:S(2)}) %collective-permute-start.13) | collective-permute-done | bytes 270368 | tf_op jit(solution)/shard_map/ppermute | solution.py:45
  43.4 0.0 collective-permute-start.18
  43.4 0.0 collective-permute-done.16.refs_1_
  43.4 0.0 collective-permute-done.17.refs_2_
  43.4 1.3 %collective-permute-done.18.refs_3_ = f32[64,512]{1,0:T(8,128)S(1)} collective-permute-done((f32[64,512]{1,0:T(8,128)S(1)}, f32[64,512]{1,0:T(8,128)S(1)}, u32[]{:S(2)}, u32[]{:S(2)}) %collective-permute-start.18) | collective-permute-done | bytes 131104 | tf_op jit(solution)/shard_map/ppermute | solution.py:45
  44.7 0.0 collective-permute-done.15.refs_0_
  44.7 0.1 pair.1
  44.8 0.1 collective-permute-start.19
  44.9 2.0 %collective-permute-start.20 = (s16[144,256]{1,0:T(8,128)(2,1)S(1)}, s16[144,256]{1,0:T(8,128)(2,1)S(1)}, u32[]{:S(2)}, u32[]{:S(2)}) collective-permute-start(s16[144,256]{1,0:T(8,128)(2,1)S(1)} %get-tuple-element.59), channel_id=1, source_target_pairs={{0,8},{4,12},{8,0},{12,4},{1,9},{5,13},{9,1},{13,5},{2,10},{6,14},... | collective-permute-start | bytes 221192 | tf_op jit(solution)/shard_map/ppermute | solution.py:45
  46.9 1.5 %collective-permute-start.21 = (s16[144,256]{1,0:T(8,128)(2,1)S(1)}, s16[144,256]{1,0:T(8,128)(2,1)S(1)}, u32[]{:S(2)}, u32[]{:S(2)}) collective-permute-start(s16[144,256]{1,0:T(8,128)(2,1)S(1)} %get-tuple-element.60), channel_id=1, source_target_pairs={{0,12},{4,8},{8,4},{12,0},{1,13},{5,9},{9,5},{13,1},{2,14},{6,10},... | collective-permute-start | bytes 221192 | tf_op jit(solution)/shard_map/ppermute | solution.py:45
  48.4 0.0 collective-permute-done.14.refs_2_
  48.4 0.9 %attended.1 = bf16[1,256,256]{2,1,0:T(8,128)(2,1)} custom-call(f32[256,1024]{1,0:T(8,128)S(1)} %get-tuple-element.41.out_ref, s16[528,256]{1,0:T(8,128)(2,1)S(1)} %collective-permute-done.12.refs_0_._, s16[528,256]{1,0:T(8,128)(2,1)S(1)} %collective-permute-done.13.refs_1_.refs_4_, s16[528,256]{1,0:T(8,128)(2,1)S(1)} %collective-permute-done.14.refs_2_, ...), custom_call_target="tpu_custom_call" | custom-call | flops 1100000000 | bytes 65536 | tf_op jit(solution)/shard_map/attended/pallas_call | solution.py:371
  49.2 0.4 collective-permute-done.19.refs_3_
  49.7 0.6 %collective-permute-done.20.refs_4_ = s16[144,256]{1,0:T(8,128)(2,1)S(1)} collective-permute-done((s16[144,256]{1,0:T(8,128)(2,1)S(1)}, s16[144,256]{1,0:T(8,128)(2,1)S(1)}, u32[]{:S(2)}, u32[]{:S(2)}) %collective-permute-start.20) | collective-permute-done | bytes 73760 | tf_op jit(solution)/shard_map/ppermute | solution.py:45
  50.3 1.9 %collective-permute-done.21.refs_5_ = s16[144,256]{1,0:T(8,128)(2,1)S(1)} collective-permute-done((s16[144,256]{1,0:T(8,128)(2,1)S(1)}, s16[144,256]{1,0:T(8,128)(2,1)S(1)}, u32[]{:S(2)}, u32[]{:S(2)}) %collective-permute-start.21) | collective-permute-done | bytes 73760 | tf_op jit(solution)/shard_map/ppermute | solution.py:45
  52.2 0.9 %last.1 = (bf16[1,256,256]{2,1,0:T(8,128)(2,1)}, f32[64,256]{1,0:T(8,128)}, f32[64,256]{1,0:T(8,128)}, f32[2]{0:T(128)}) custom-call(f32[256,256]{1,0:T(8,128)S(1)} %get-tuple-element.47.own_ref, f32[72,512]{1,0:T(8,128)S(1)} %get-tuple-element.57.weight_ref, s16[528,256]{1,0:T(8,128)(2,1)S(1)} %collective-permute-done.12.refs_0_._, ...), custom_call_target="tpu_custom_call" | custom-call | flops 1100000000 | bytes 65536 | tf_op jit(solution)/shard_map/last/pallas_call | solution.py:371
Async XLA Ops:
  0.6 11.5 %copy-start.3 = (bf16[1,256,256]{2,1,0:T(8,128)(2,1)S(1)}, bf16[1,256,256]{2,1,0:T(8,128)(2,1)}, u32[]{:S(2)}) copy-start(bf16[1,256,256]{2,1,0:T(8,128)(2,1)} %refs_0_.3) | copy-start | bytes 393220
  0.6 16.9 %copy-start.2 = (bf16[1,256,256]{2,1,0:T(8,128)(2,1)S(1)}, bf16[1,256,256]{2,1,0:T(8,128)(2,1)}, u32[]{:S(2)}) copy-start(bf16[1,256,256]{2,1,0:T(8,128)(2,1)} %refs_4_.1) | copy-start | bytes 393220
  0.7 11.5 %copy-start = (f32[2]{0:T(128)S(1)}, f32[2]{0:T(128)}, u32[]{:S(2)}) copy-start(f32[2]{0:T(128)} %slopes_ref.5) | copy-start | bytes 28
  0.7 11.5 %copy-start.1 = (s32[1,8]{1,0:T(1,128)S(1)}, s32[1,8]{1,0:T(1,128)}, u32[]{:S(2)}) copy-start(s32[1,8]{1,0:T(1,128)} %bounds_ref.3) | copy-start | bytes 100
  0.7 11.3 %collective-permute-start.2 = (bf16[1,256,256]{2,1,0:T(8,128)(2,1)}, bf16[1,256,256]{2,1,0:T(8,128)(2,1)S(1)}, u32[]{:S(2)}, u32[]{:S(2)}) collective-permute-start(bf16[1,256,256]{2,1,0:T(8,128)(2,1)} %refs_0_.3), channel_id=1, source_target_pairs={{0,12},{4,8},{8,4},{12,0},{1,13},{5,9},{9,5},{13,1},{2,14},{6,10},... | collective-permute-start | bytes 393224 | tf_op jit(solution)/shard_map/ppermute | solution.py:45
  4.6 7.5 %collective-permute-start.1 = (bf16[1,256,256]{2,1,0:T(8,128)(2,1)}, bf16[1,256,256]{2,1,0:T(8,128)(2,1)S(1)}, u32[]{:S(2)}, u32[]{:S(2)}) collective-permute-start(bf16[1,256,256]{2,1,0:T(8,128)(2,1)} %refs_0_.3), channel_id=1, source_target_pairs={{0,8},{4,12},{8,0},{12,4},{1,9},{5,13},{9,1},{13,5},{2,10},{6,14},... | collective-permute-start | bytes 393224 | tf_op jit(solution)/shard_map/ppermute | solution.py:45
  5.1 7.0 %collective-permute-start = (bf16[1,256,256]{2,1,0:T(8,128)(2,1)}, bf16[1,256,256]{2,1,0:T(8,128)(2,1)S(1)}, u32[]{:S(2)}, u32[]{:S(2)}) collective-permute-start(bf16[1,256,256]{2,1,0:T(8,128)(2,1)} %refs_0_.3), channel_id=1, source_target_pairs={{0,4},{4,0},{8,12},{12,8},{1,5},{5,1},{9,13},{13,9},{2,6},{6,2},{1... | collective-permute-start | bytes 393224 | tf_op jit(solution)/shard_map/ppermute | solution.py:45
  8.6 8.9 %collective-permute-start.5 = (bf16[1,256,256]{2,1,0:T(8,128)(2,1)S(1)}, bf16[1,256,256]{2,1,0:T(8,128)(2,1)S(1)}, u32[]{:S(2)}, u32[]{:S(2)}) collective-permute-start(bf16[1,256,256]{2,1,0:T(8,128)(2,1)S(1)} %get-tuple-element.38), channel_id=1, source_target_pairs={{0,12},{4,8},{8,4},{12,0},{1,13},{5,9},{9,5},{13,1},{2,14},{6,10},... | collective-permute-start | bytes 393224 | tf_op jit(solution)/shard_map/ppermute | solution.py:45
  11.5 6.1 %collective-permute-start.4 = (bf16[1,256,256]{2,1,0:T(8,128)(2,1)S(1)}, bf16[1,256,256]{2,1,0:T(8,128)(2,1)S(1)}, u32[]{:S(2)}, u32[]{:S(2)}) collective-permute-start(bf16[1,256,256]{2,1,0:T(8,128)(2,1)S(1)} %get-tuple-element.38), channel_id=1, source_target_pairs={{0,8},{4,12},{8,0},{12,4},{1,9},{5,13},{9,1},{13,5},{2,10},{6,14},... | collective-permute-start | bytes 393224 | tf_op jit(solution)/shard_map/ppermute | solution.py:45
  12.0 5.6 %collective-permute-start.3 = (bf16[1,256,256]{2,1,0:T(8,128)(2,1)S(1)}, bf16[1,256,256]{2,1,0:T(8,128)(2,1)S(1)}, u32[]{:S(2)}, u32[]{:S(2)}) collective-permute-start(bf16[1,256,256]{2,1,0:T(8,128)(2,1)S(1)} %get-tuple-element.38), channel_id=1, source_target_pairs={{0,4},{4,0},{8,12},{12,8},{1,5},{5,1},{9,13},{13,9},{2,6},{6,2},{1... | collective-permute-start | bytes 393224 | tf_op jit(solution)/shard_map/ppermute | solution.py:45
  14.0 4.8 %collective-permute-start.8 = (f32[16,256]{1,0:T(8,128)S(1)}, f32[16,256]{1,0:T(8,128)S(1)}, u32[]{:S(2)}, u32[]{:S(2)}) collective-permute-start(f32[16,256]{1,0:T(8,128)S(1)} %get-tuple-element.40.refs_0_), channel_id=1, source_target_pairs={{0,12},{4,8},{8,4},{12,0},{1,13},{5,9},{9,5},{13,1},{2,14},{6,10},... | collective-permute-start | bytes 49160 | tf_op jit(solution)/shard_map/ppermute | solution.py:45
  16.9 3.7 %collective-permute-start.7 = (f32[16,256]{1,0:T(8,128)S(1)}, f32[16,256]{1,0:T(8,128)S(1)}, u32[]{:S(2)}, u32[]{:S(2)}) collective-permute-start(f32[16,256]{1,0:T(8,128)S(1)} %get-tuple-element.40.refs_0_), channel_id=1, source_target_pairs={{0,8},{4,12},{8,0},{12,4},{1,9},{5,13},{9,1},{13,5},{2,10},{6,14},... | collective-permute-start | bytes 49160 | tf_op jit(solution)/shard_map/ppermute | solution.py:45
  17.4 3.7 %collective-permute-start.6 = (f32[16,256]{1,0:T(8,128)S(1)}, f32[16,256]{1,0:T(8,128)S(1)}, u32[]{:S(2)}, u32[]{:S(2)}) collective-permute-start(f32[16,256]{1,0:T(8,128)S(1)} %get-tuple-element.40.refs_0_), channel_id=1, source_target_pairs={{0,4},{4,0},{8,12},{12,8},{1,5},{5,1},{9,13},{13,9},{2,6},{6,2},{1... | collective-permute-start | bytes 49160 | tf_op jit(solution)/shard_map/ppermute | solution.py:45
  23.6 4.8 %collective-permute-start.11 = (f32[16,256]{1,0:T(8,128)S(1)}, f32[16,256]{1,0:T(8,128)S(1)}, u32[]{:S(2)}, u32[]{:S(2)}) collective-permute-start(f32[16,256]{1,0:T(8,128)S(1)} %get-tuple-element.43._.refs_4_.refs_3_.refs_0_), channel_id=1, source_target_pairs={{0,12},{4,8},{8,4},{12,0},{1,13},{5,9},{9,5},{13,1},{2,14},{6,10},... | collective-permute-start | bytes 49160 | tf_op jit(solution)/shard_map/ppermute | solution.py:45
  25.1 3.7 %collective-permute-start.10 = (f32[16,256]{1,0:T(8,128)S(1)}, f32[16,256]{1,0:T(8,128)S(1)}, u32[]{:S(2)}, u32[]{:S(2)}) collective-permute-start(f32[16,256]{1,0:T(8,128)S(1)} %get-tuple-element.43._.refs_4_.refs_3_.refs_0_), channel_id=1, source_target_pairs={{0,8},{4,12},{8,0},{12,4},{1,9},{5,13},{9,1},{13,5},{2,10},{6,14},... | collective-permute-start | bytes 49160 | tf_op jit(solution)/shard_map/ppermute | solution.py:45
  25.2 3.7 %collective-permute-start.9 = (f32[16,256]{1,0:T(8,128)S(1)}, f32[16,256]{1,0:T(8,128)S(1)}, u32[]{:S(2)}, u32[]{:S(2)}) collective-permute-start(f32[16,256]{1,0:T(8,128)S(1)} %get-tuple-element.43._.refs_4_.refs_3_.refs_0_), channel_id=1, source_target_pairs={{0,4},{4,0},{8,12},{12,8},{1,5},{5,1},{9,13},{13,9},{2,6},{6,2},{1... | collective-permute-start | bytes 49160 | tf_op jit(solution)/shard_map/ppermute | solution.py:45
  31.8 7.5 %collective-permute-start.12 = (s16[528,256]{1,0:T(8,128)(2,1)S(1)}, s16[528,256]{1,0:T(8,128)(2,1)S(1)}, u32[]{:S(2)}, u32[]{:S(2)}) collective-permute-start(s16[528,256]{1,0:T(8,128)(2,1)S(1)} %get-tuple-element.44), channel_id=1, source_target_pairs={{0,4},{4,0},{8,12},{12,8},{1,5},{5,1},{9,13},{13,9},{2,6},{6,2},{1... | collective-permute-start | bytes 811016 | tf_op jit(solution)/shard_map/ppermute | solution.py:45
  33.7 9.6 %collective-permute-start.13 = (s16[528,256]{1,0:T(8,128)(2,1)S(1)}, s16[528,256]{1,0:T(8,128)(2,1)S(1)}, u32[]{:S(2)}, u32[]{:S(2)}) collective-permute-start(s16[528,256]{1,0:T(8,128)(2,1)S(1)} %get-tuple-element.45), channel_id=1, source_target_pairs={{0,8},{4,12},{8,0},{12,4},{1,9},{5,13},{9,1},{13,5},{2,10},{6,14},... | collective-permute-start | bytes 811016 | tf_op jit(solution)/shard_map/ppermute | solution.py:45
  35.3 13.1 %collective-permute-start.14 = (s16[528,256]{1,0:T(8,128)(2,1)S(1)}, s16[528,256]{1,0:T(8,128)(2,1)S(1)}, u32[]{:S(2)}, u32[]{:S(2)}) collective-permute-start(s16[528,256]{1,0:T(8,128)(2,1)S(1)} %get-tuple-element.46), channel_id=1, source_target_pairs={{0,12},{4,8},{8,4},{12,0},{1,13},{5,9},{9,5},{13,1},{2,14},{6,10},... | collective-permute-start | bytes 811016 | tf_op jit(solution)/shard_map/ppermute | solution.py:45
  40.1 4.6 %collective-permute-start.15 = (f32[72,512]{1,0:T(8,128)S(1)}, f32[72,512]{1,0:T(8,128)S(1)}, u32[]{:S(2)}, u32[]{:S(2)}) collective-permute-start(f32[72,512]{1,0:T(8,128)S(1)} %get-tuple-element.53), channel_id=1, source_target_pairs={{0,16},{16,0},{1,17},{17,1},{2,18},{18,2},{3,19},{19,3},{4,20},{20... | collective-permute-start | bytes 442376 | tf_op jit(solution)/shard_map/ppermute | solution.py:45
  40.2 3.1 %collective-permute-start.16 = (f32[64,512]{1,0:T(8,128)S(1)}, f32[64,512]{1,0:T(8,128)S(1)}, u32[]{:S(2)}, u32[]{:S(2)}) collective-permute-start(f32[64,512]{1,0:T(8,128)S(1)} %get-tuple-element.54), channel_id=1, source_target_pairs={{0,16},{16,0},{1,17},{17,1},{2,18},{18,2},{3,19},{19,3},{4,20},{20... | collective-permute-start | bytes 393224 | tf_op jit(solution)/shard_map/ppermute | solution.py:45
  40.7 2.6 %collective-permute-start.17 = (f32[64,512]{1,0:T(8,128)S(1)}, f32[64,512]{1,0:T(8,128)S(1)}, u32[]{:S(2)}, u32[]{:S(2)}) collective-permute-start(f32[64,512]{1,0:T(8,128)S(1)} %get-tuple-element.55), channel_id=1, source_target_pairs={{0,16},{16,0},{1,17},{17,1},{2,18},{18,2},{3,19},{19,3},{4,20},{20... | collective-permute-start | bytes 393224 | tf_op jit(solution)/shard_map/ppermute | solution.py:45
  43.4 1.3 %collective-permute-start.18 = (f32[64,512]{1,0:T(8,128)S(1)}, f32[64,512]{1,0:T(8,128)S(1)}, u32[]{:S(2)}, u32[]{:S(2)}) collective-permute-start(f32[64,512]{1,0:T(8,128)S(1)} %get-tuple-element.56), channel_id=1, source_target_pairs={{0,16},{16,0},{1,17},{17,1},{2,18},{18,2},{3,19},{19,3},{4,20},{20... | collective-permute-start | bytes 393224 | tf_op jit(solution)/shard_map/ppermute | solution.py:45
  44.8 4.8 %collective-permute-start.19 = (s16[144,256]{1,0:T(8,128)(2,1)S(1)}, s16[144,256]{1,0:T(8,128)(2,1)S(1)}, u32[]{:S(2)}, u32[]{:S(2)}) collective-permute-start(s16[144,256]{1,0:T(8,128)(2,1)S(1)} %get-tuple-element.58), channel_id=1, source_target_pairs={{0,4},{4,0},{8,12},{12,8},{1,5},{5,1},{9,13},{13,9},{2,6},{6,2},{1... | collective-permute-start | bytes 221192 | tf_op jit(solution)/shard_map/ppermute | solution.py:45
  44.9 5.4 %collective-permute-start.20 = (s16[144,256]{1,0:T(8,128)(2,1)S(1)}, s16[144,256]{1,0:T(8,128)(2,1)S(1)}, u32[]{:S(2)}, u32[]{:S(2)}) collective-permute-start(s16[144,256]{1,0:T(8,128)(2,1)S(1)} %get-tuple-element.59), channel_id=1, source_target_pairs={{0,8},{4,12},{8,0},{12,4},{1,9},{5,13},{9,1},{13,5},{2,10},{6,14},... | collective-permute-start | bytes 221192 | tf_op jit(solution)/shard_map/ppermute | solution.py:45
  46.9 5.3 %collective-permute-start.21 = (s16[144,256]{1,0:T(8,128)(2,1)S(1)}, s16[144,256]{1,0:T(8,128)(2,1)S(1)}, u32[]{:S(2)}, u32[]{:S(2)}) collective-permute-start(s16[144,256]{1,0:T(8,128)(2,1)S(1)} %get-tuple-element.60), channel_id=1, source_target_pairs={{0,12},{4,8},{8,4},{12,0},{1,13},{5,9},{9,5},{13,1},{2,14},{6,10},... | collective-permute-start | bytes 221192 | tf_op jit(solution)/shard_map/ppermute | solution.py:45

commit v4 on v3

--- a/solution.py
+++ b/solution.py
@@ -13,7 +13,7 @@
 CODE_MAX = 32000.0
 TINY = 1e-30
 CHUNK = 512
-STEP = 512
+STEP = 256
 LIM_P, LIM_T, LIM_D, LIM_S, LIM_G = 55, 8, 8, 16, 16
 SCALE = HEAD ** (-0.5)
 UNIT = SCALE * LOG2E
@@ -154,7 +154,7 @@
         gt_ref[:, cols] = g_refs[j][0].astype(F32).T.astype(BF16)
 
 
-def dprod_kernel(val_ref, gt_ref, _, dprod_ref):
+def dprod_kernel(val_ref, gt_ref, dprod_ref):
     for h in range(dprod_ref.shape[0]):
         dprod_ref[h] = nn(val_ref[:, head_cols(h)], gt_ref[head_cols(h), :])
 
@@ -183,8 +183,8 @@
     return tops, bases[0]
 
 
-def sums_kernel(n, slopes_ref, val_ref, score_ref, gt_ref, *refs):
-    top_refs, (stats_ref, out_ref, expo_ref) = refs[:n], refs[n:]
+def sums_kernel(n, slopes_ref, val_ref, score_ref, gt_ref, _, *refs):
+    top_refs, (stats_ref, own_ref, expo_ref), send_refs = refs[:n], refs[n : n + 3], refs[n + 3 :]
     heads, tokens, lats = score_ref.shape
     rows = lats // n
     tops, base = merged_tops(n, heads, slopes_ref, top_refs)
@@ -200,7 +200,8 @@
             part_norm = jnp.sum(expo, axis=0, keepdims=True)
             out = term if out is None else out + term
             norm = part_norm if norm is None else norm + part_norm
-        out_ref[head_cols(h), :] = out
+        own_ref[head_cols(h), :] = out[:, :rows]
+        write_messages(h, rows, out, send_refs)
         delta = jnp.sum(gt_ref[head_cols(h), :].astype(F32) * out, axis=0, keepdims=True)
         for j in range(n):
             cols = slice(j * rows, (j + 1) * rows)
@@ -245,7 +246,7 @@
     return norms, deltas
 
 
-def rows_kernel(n, bounds_ref, slopes_ref, key_ref, expo_ref, dprod_ref, out_ref, *refs):
+def rows_kernel(n, bounds_ref, slopes_ref, key_ref, expo_ref, dprod_ref, *refs):
     top_refs, sum_refs, refs = refs[:n], refs[n : 2 * n], refs[2 * n :]
     own_ref, grad_ref, slope_ref = refs[:3]
     send_refs = refs[3 : n + 2]
@@ -272,8 +273,7 @@
             term = tn(key_ref[part, head_cols(h)], score_grad_b)
             dq = term if dq is None else dq + term
         own_ref[head_cols(h), :] = dq[:, :rows]
-        write_messages(2 * h, rows, dq, send_refs)
-        write_messages(2 * h + 1, rows, out_ref[head_cols(h), :], send_refs)
+        write_messages(h, rows, dq, send_refs)
         total = jnp.sum(slope, axis=1, keepdims=True)
         slope_ref[:, h * 2 * HEAD : (h + 1) * 2 * HEAD] = jnp.broadcast_to(total, (8, 2 * HEAD))
 
@@ -330,26 +330,26 @@
         send_refs[k - 1][heads * piece :, :] = to_code(stack_rows(exponents + digits, 16, width))
 
 
-def attended_kernel(n, heads, out_ref, *refs):
-    got_refs, sum_refs, att_ref = refs[: n - 1], refs[n - 1 : 2 * n - 1], refs[2 * n - 1]
+def latents_kernel(n, heads, out_ref, own_ref, *refs):
+    others = n - 1
+    att_refs, dq_refs, sum_refs = refs[:others], refs[others : 2 * others], refs[2 * others : -2]
+    att_ref, grad_ref = refs[-2:]
     rows = att_ref.shape[1]
     norms, _ = merged_sums(n, heads, sum_refs)
     for h in range(heads):
-        total = out_ref[head_cols(h), :rows]
-        for ref in got_refs:
-            total = total + read_message(ref, 2 * h + 1)
+        total = out_ref[head_cols(h), :]
+        for ref in att_refs:
+            total = total + read_message(ref, h)
+        grad = own_ref[head_cols(h), :]
+        for ref in dq_refs:
+            grad = grad + read_message(ref, h)
         total = total / norms[h][:, :rows]
         att_ref[0, :, head_cols(h)] = total.T.astype(BF16)
-
-
-def last_kernel(n, heads, own_ref, weight_ref, *refs):
-    got_refs, part_refs = refs[: n - 1], refs[n - 1 : 2 * n - 2]
-    grad_ref, key_ref, val_ref, slope_ref = refs[2 * n - 2 :]
-    for h in range(heads):
-        total = own_ref[head_cols(h), :]
-        for ref in got_refs:
-            total = total + read_message(ref, 2 * h)
-        grad_ref[0, :, head_cols(h)] = (SCALE * total).T.astype(BF16)
+        grad_ref[0, :, head_cols(h)] = (SCALE * grad).T.astype(BF16)
+
+
+def last_kernel(n, heads, weight_ref, *refs):
+    part_refs, (key_ref, val_ref, slope_ref) = refs[: n - 1], refs[n - 1 :]
     piece = weight_ref.shape[0] - 8
     width = 2 * HEAD
     extras = [from_code(ref[heads * piece :, :]) for ref in part_refs]
@@ -400,6 +400,7 @@
     g_all = [grad] + [swap(grad, "seq", k, n) for k in peers]
     stat_rows = -(-(heads * n + 1) // 8) * 8
     square = ((heads, toks, lats), F32)
+    block = ((width + 16, rows), I16)
     top_own, scores = call(
         functools.partial(top_kernel, n),
         "tops",
@@ -418,35 +419,36 @@
         (*q_all, cotangent, *g_all[1:]),
         1,
     )
+    (dprod,) = call(dprod_kernel, "dprod", [square], (values, g_turned), 2, limit=LIM_D << 20)
     sums = call(
         functools.partial(sums_kernel, n),
         "sums",
-        [((2 * heads * n, rows), F32), ((width, lats), F32), square],
-        (slopes, values, scores, g_turned, *tops),
+        [((2 * heads * n, rows), F32), ((width, rows), F32), square] + [block] * (n - 1),
+        (slopes, values, scores, g_turned, dprod, *tops),
         2,
         smem=1,
         limit=LIM_S << 20,
     )
     norms = [sums[0]] + [swap(sums[0], "seq", k, n) for k in peers]
-    (dprod,) = call(dprod_kernel, "dprod", [square], (values, g_turned, sums[0]), 2, limit=LIM_D << 20)
+    outs = [swap(sums[2 + k], "seq", k, n) for k in peers]
     own_dq, score_grads, slope_terms, *sends = call(
         functools.partial(rows_kernel, n),
         "rows",
         [((width, rows), F32), ((heads, toks, lats), BF16), ((8, 2 * width), F32)]
-        + [((2 * width + 16, rows), I16)] * (n - 1),
-        (boundaries, slopes, keys, sums[2], dprod, sums[1], *tops, *norms),
+        + [block] * (n - 1),
+        (boundaries, slopes, keys, sums[2], dprod, *tops, *norms),
         3,
         [pltpu.VMEM((toks, 128), F32)],
         2,
         limit=LIM_G << 20,
     )
-    blocks = [swap(x, "seq", k, n) for k, x in zip(peers, sends)]
+    dqs = [swap(x, "seq", k, n) for k, x in zip(peers, sends)]
     half = channels // 2
     (tok_grads,) = call(
         functools.partial(tokens_kernel, n),
         "tokens",
         [((2 * width, toks), BF16)],
-        (sums[2], score_grads, q_turned, g_turned, *norms),
+        (sums[2], score_grads, q_turned, g_turned, *norms, *outs),
         3,
         limit=LIM_G << 20,
     )
@@ -455,36 +457,36 @@
         functools.partial(weights_kernel, n),
         "weights",
         [((n, piece + 8, 2 * width), F32), ((piece + 8, 2 * width), F32)] + [((piece, 2 * width), F32)] * (n - 1),
-        (inputs, tok_grads, slope_terms, blocks[0]),
+        (inputs, tok_grads, slope_terms, dqs[0]),
         1,
         [pltpu.VMEM((2, half, 2 * width), F32)],
         limit=LIM_G << 20,
     )
     got = [swap(x, "dp", 1, 2) for x in weights[1:]]
-    (attended,) = call(
-        functools.partial(attended_kernel, n, heads),
-        "attended",
-        [((1, rows, width), BF16)],
-        (sums[1], *blocks, *norms),
+    latents = call(
+        functools.partial(latents_kernel, n, heads),
+        "latents",
+        [((1, rows, width), BF16)] * 2,
+        (sums[1], own_dq, *outs, *dqs, *norms),
         1,
     )
     pair = call(
         functools.partial(pair_kernel, n, heads),
         "pair",
         [((piece + 8, 2 * width), F32)] + [((heads * piece + 16, 2 * HEAD), I16)] * (n - 1),
-        (weights[0], *got, blocks[1]),
+        (weights[0], *got, dqs[1]),
         0.3,
     )
     parts = [swap(pair[k], "seq", k, n) for k in peers]
     last = call(
         functools.partial(last_kernel, n, heads),
         "last",
-        [((1, rows, width), BF16), ((piece, width), F32), ((piece, width), F32), ((heads,), F32)],
-        (own_dq, pair[0], *blocks, *parts),
+        [((piece, width), F32), ((piece, width), F32), ((heads,), F32)],
+        (pair[0], *parts),
         1,
-        out_specs=[VMEM] * 3 + [SMEM],
-    )
-    return (attended, *last)
+        out_specs=[VMEM] * 2 + [SMEM],
+    )
+    return (*latents, *last)
 
 
 def carried_in(part, axis, combine, identity):

time: 53.2 us -> 51.4 us (0.966)
  waiting for transfers between devices: 11.8 us -> 5.81 us
  starting transfers between devices: 23 us -> 27.3 us
    ppermute x22 -> x25, waiting for transfers between devices: 11.8 us -> 5.81 us  [swap(): return lax.ppermute(x, axis, [(i, i ^ k) for i in range(n)])]
    ppermute x22 -> x25, starting transfers between devices: 23 us -> 27.3 us  [swap(): return lax.ppermute(x, axis, [(i, i ^ k) for i in range(n)])]
  transfers between devices with their start and end apart: 22 -> 25, of which waited for: 11 -> 7; matrix products, arithmetic and copies ran while one was open for 0% -> 0% of each run, Pallas kernels for 21% -> 27%
where the time goes in v4:
time: 51.4 us; the launch traced here: 51.2 us
  starting transfers between devices  27.3 us (53%)
  Pallas kernels  17.3 us (34%)
  waiting for transfers between devices  5.81 us (11%)
  between operations  0.8 us (2%)
    ppermute x25, starting transfers between devices, swap(): return lax.ppermute(x, axis, [(i, i ^ k) for i in range(n)])  27.3 us
    pallas_call x11, Pallas kernels, call(): pl.pallas_call(kernel, out_shape=[jax.ShapeDtypeStruct(shape, dtype) for...  17.3 us
    ppermute x25, waiting for transfers between devices, swap(): return lax.ppermute(x, axis, [(i, i ^ k) for i in range(n)])  5.81 us
  transfers between devices with their start and end apart: 25, of which 7 were waited for; matrix products, arithmetic and copies ran while one was open for 0% of the time, Pallas kernels for 27%

profile of v4, /device:TPU:0, one launch (start us, length us, event | category | flops | bytes accessed | tf_op | source)
XLA Modules:
  0.0 51.2 jit_solution(7648059545890945204)
XLA Ops:
  0.6 0.0 copy-start.3
  0.6 0.0 copy-start.2
  0.7 0.0 copy-start
  0.7 4.0 %collective-permute-start.2 = (bf16[1,256,256]{2,1,0:T(8,128)(2,1)}, bf16[1,256,256]{2,1,0:T(8,128)(2,1)S(1)}, u32[]{:S(2)}, u32[]{:S(2)}) collective-permute-start(bf16[1,256,256]{2,1,0:T(8,128)(2,1)} %refs_0_.3), channel_id=1, source_target_pairs={{0,12},{4,8},{8,4},{12,0},{1,13},{5,9},{9,5},{13,1},{2,14},{6,10},... | collective-permute-start | bytes 393224 | tf_op jit(solution)/shard_map/ppermute | solution.py:45
  4.6 0.5 collective-permute-start.1
  5.1 0.1 collective-permute-start
  5.3 3.3 %prep.1 = (bf16[1024,512]{1,0:T(8,128)(2,1)S(1)}, bf16[1024,256]{1,0:T(8,128)(2,1)S(1)}, bf16[1024,256]{1,0:T(8,128)(2,1)S(1)}, bf16[1,256,256]{2,1,0:T(8,128)(2,1)S(1)}) custom-call(bf16[1,1024,512]{2,1,0:T(8,128)(2,1)} %tok_hbm.1, s32[1,1024]{1,0:T(1,128)} %lev_hbm.1, f32[256,512]{1,0:T(8,128)} %table_hbm.1, bf16[512,256]{1,0:T(8,128)(2,1)} %wk_hbm.1, ...), custom_call_target="tpu_custom_call" | custom-call | flops 3300000000 | bytes 65536 | tf_op jit(solution)/shard_map/prep/pallas_call | solution.py:371
  8.6 2.9 %collective-permute-start.5 = (bf16[1,256,256]{2,1,0:T(8,128)(2,1)S(1)}, bf16[1,256,256]{2,1,0:T(8,128)(2,1)S(1)}, u32[]{:S(2)}, u32[]{:S(2)}) collective-permute-start(bf16[1,256,256]{2,1,0:T(8,128)(2,1)S(1)} %get-tuple-element.42), channel_id=1, source_target_pairs={{0,12},{4,8},{8,4},{12,0},{1,13},{5,9},{9,5},{13,1},{2,14},{6,10},... | collective-permute-start | bytes 393224 | tf_op jit(solution)/shard_map/ppermute | solution.py:45
  11.5 0.5 %collective-permute-start.4 = (bf16[1,256,256]{2,1,0:T(8,128)(2,1)S(1)}, bf16[1,256,256]{2,1,0:T(8,128)(2,1)S(1)}, u32[]{:S(2)}, u32[]{:S(2)}) collective-permute-start(bf16[1,256,256]{2,1,0:T(8,128)(2,1)S(1)} %get-tuple-element.42), channel_id=1, source_target_pairs={{0,8},{4,12},{8,0},{12,4},{1,9},{5,13},{9,1},{13,5},{2,10},{6,14},... | collective-permute-start | bytes 393224 | tf_op jit(solution)/shard_map/ppermute | solution.py:45
  12.0 0.0 collective-permute-done.2.refs_3_
  12.0 0.1 collective-permute-start.3
  12.1 0.0 collective-permute-done.1.refs_2_
  12.1 0.0 collective-permute-done.refs_1_
  12.2 1.9 %tops.1 = (f32[16,256]{1,0:T(8,128)S(1)}, f32[2,1024,1024]{2,1,0:T(8,128)S(1)}) custom-call(s32[1,8]{1,0:T(1,128)S(1)} %copy-done.1, f32[2]{0:T(128)S(1)} %copy-done, bf16[1024,256]{1,0:T(8,128)(2,1)S(1)} %get-tuple-element.40.key_ref, bf16[1,256,256]{2,1,0:T(8,128)(2,1)S(1)} %copy-done.3, bf16[1,256,256]{2,1,0:T(8,128)(2,1)S(1)} %collective-permute-done.refs_1_, ...), custom_call_target="tpu_custom_call" | custom-call | flops 2200000000 | bytes 65536 | tf_op jit(solution)/shard_map/tops/pallas_call | solution.py:371
  14.0 2.9 %collective-permute-start.8 = (f32[16,256]{1,0:T(8,128)S(1)}, f32[16,256]{1,0:T(8,128)S(1)}, u32[]{:S(2)}, u32[]{:S(2)}) collective-permute-start(f32[16,256]{1,0:T(8,128)S(1)} %get-tuple-element.44.refs_0_), channel_id=1, source_target_pairs={{0,12},{4,8},{8,4},{12,0},{1,13},{5,9},{9,5},{13,1},{2,14},{6,10},... | collective-permute-start | bytes 49160 | tf_op jit(solution)/shard_map/ppermute | solution.py:45
  16.9 0.5 %collective-permute-start.7 = (f32[16,256]{1,0:T(8,128)S(1)}, f32[16,256]{1,0:T(8,128)S(1)}, u32[]{:S(2)}, u32[]{:S(2)}) collective-permute-start(f32[16,256]{1,0:T(8,128)S(1)} %get-tuple-element.44.refs_0_), channel_id=1, source_target_pairs={{0,8},{4,12},{8,0},{12,4},{1,9},{5,13},{9,1},{13,5},{2,10},{6,14},... | collective-permute-start | bytes 49160 | tf_op jit(solution)/shard_map/ppermute | solution.py:45
  17.5 0.0 collective-permute-done.5.refs_7_
  17.5 0.1 collective-permute-start.6
  17.6 0.0 collective-permute-done.4.refs_6_
  17.6 0.0 collective-permute-done.3.refs_5_
  17.6 0.3 turn.1
  17.9 1.2 %dprod.1._.dprod_ref = f32[2,1024,1024]{2,1,0:T(8,128)S(1)} custom-call(bf16[1024,256]{1,0:T(8,128)(2,1)S(1)} %get-tuple-element.39.val_ref, bf16[256,1024]{1,0:T(8,128)(2,1)S(1)} %get-tuple-element.43.gt_ref), custom_call_target="tpu_custom_call" | custom-call | flops 2200000000 | bytes 65536 | tf_op jit(solution)/shard_map/dprod/pallas_call | solution.py:371
  19.2 0.0 collective-permute-done.8.refs_3_
  19.2 1.5 %collective-permute-done.7.refs_2_ = f32[16,256]{1,0:T(8,128)S(1)} collective-permute-done((f32[16,256]{1,0:T(8,128)S(1)}, f32[16,256]{1,0:T(8,128)S(1)}, u32[]{:S(2)}, u32[]{:S(2)}) %collective-permute-start.7) | collective-permute-done | bytes 16416 | tf_op jit(solution)/shard_map/ppermute | solution.py:45
  20.7 0.5 %collective-permute-done.6.refs_1_ = f32[16,256]{1,0:T(8,128)S(1)} collective-permute-done((f32[16,256]{1,0:T(8,128)S(1)}, f32[16,256]{1,0:T(8,128)S(1)}, u32[]{:S(2)}, u32[]{:S(2)}) %collective-permute-start.6) | collective-permute-done | bytes 16416 | tf_op jit(solution)/shard_map/ppermute | solution.py:45
  21.2 2.5 %sums.1 = (f32[16,256]{1,0:T(8,128)S(1)}, f32[256,256]{1,0:T(8,128)S(1)}, f32[2,1024,1024]{2,1,0:T(8,128)S(1)}, s16[272,256]{1,0:T(8,128)(2,1)S(1)}, s16[272,256...) custom-call(f32[2]{0:T(128)S(1)} %copy-done, bf16[1024,256]{1,0:T(8,128)(2,1)S(1)} %get-tuple-element.39.val_ref, ...), custom_call_target="tpu_custom_call" | custom-call | flops 2200000000 | bytes 65536 | tf_op jit(solution)/shard_map/sums/pallas_call | solution.py:371
  23.7 1.6 %collective-permute-start.11 = (f32[16,256]{1,0:T(8,128)S(1)}, f32[16,256]{1,0:T(8,128)S(1)}, u32[]{:S(2)}, u32[]{:S(2)}) collective-permute-start(f32[16,256]{1,0:T(8,128)S(1)} %get-tuple-element.47.refs_4_.refs_6_.refs_0_), channel_id=1, source_target_pairs={{0,12},{4,8},{8,4},{12,0},{1,13},{5,9},{9,5},{13,1},{2,14},{6,10},... | collective-permute-start | bytes 49160 | tf_op jit(solution)/shard_map/ppermute | solution.py:45
  25.3 0.1 collective-permute-start.10
  25.4 1.9 %collective-permute-start.9 = (f32[16,256]{1,0:T(8,128)S(1)}, f32[16,256]{1,0:T(8,128)S(1)}, u32[]{:S(2)}, u32[]{:S(2)}) collective-permute-start(f32[16,256]{1,0:T(8,128)S(1)} %get-tuple-element.47.refs_4_.refs_6_.refs_0_), channel_id=1, source_target_pairs={{0,4},{4,0},{8,12},{12,8},{1,5},{5,1},{9,13},{13,9},{2,6},{6,2},{1... | collective-permute-start | bytes 49160 | tf_op jit(solution)/shard_map/ppermute | solution.py:45
  27.3 0.1 collective-permute-start.12
  27.4 1.9 %collective-permute-start.13 = (s16[272,256]{1,0:T(8,128)(2,1)S(1)}, s16[272,256]{1,0:T(8,128)(2,1)S(1)}, u32[]{:S(2)}, u32[]{:S(2)}) collective-permute-start(s16[272,256]{1,0:T(8,128)(2,1)S(1)} %get-tuple-element.50), channel_id=1, source_target_pairs={{0,8},{4,12},{8,0},{12,4},{1,9},{5,13},{9,1},{13,5},{2,10},{6,14},... | collective-permute-start | bytes 417800 | tf_op jit(solution)/shard_map/ppermute | solution.py:45
  29.3 0.0 collective-permute-done.11.refs_7_.refs_9_.refs_3_
  29.3 1.4 %collective-permute-start.14 = (s16[272,256]{1,0:T(8,128)(2,1)S(1)}, s16[272,256]{1,0:T(8,128)(2,1)S(1)}, u32[]{:S(2)}, u32[]{:S(2)}) collective-permute-start(s16[272,256]{1,0:T(8,128)(2,1)S(1)} %get-tuple-element.51), channel_id=1, source_target_pairs={{0,12},{4,8},{8,4},{12,0},{1,13},{5,9},{9,5},{13,1},{2,14},{6,10},... | collective-permute-start | bytes 417800 | tf_op jit(solution)/shard_map/ppermute | solution.py:45
  30.8 0.0 collective-permute-done.10.refs_6_.refs_8_.refs_2_
  30.8 0.0 collective-permute-done.9.refs_5_.refs_7_.refs_1_
  30.8 2.7 %rows.1 = (f32[256,256]{1,0:T(8,128)S(1)}, bf16[2,1024,1024]{2,1,0:T(8,128)(2,1)S(1)}, f32[8,512]{1,0:T(8,128)S(1)}, s16[272,256]{1,0:T(8,128)(2,1)S(1)}, s16[27...) custom-call(s32[1,8]{1,0:T(1,128)S(1)} %copy-done.1, f32[2]{0:T(128)S(1)} %copy-done, ...), custom_call_target="tpu_custom_call" | custom-call | flops 3300000000 | bytes 65536 | tf_op jit(solution)/shard_map/rows/pallas_call | solution.py:371
  33.5 0.9 %collective-permute-start.15 = (s16[272,256]{1,0:T(8,128)(2,1)S(1)}, s16[272,256]{1,0:T(8,128)(2,1)S(1)}, u32[]{:S(2)}, u32[]{:S(2)}) collective-permute-start(s16[272,256]{1,0:T(8,128)(2,1)S(1)} %get-tuple-element.52), channel_id=1, source_target_pairs={{0,4},{4,0},{8,12},{12,8},{1,5},{5,1},{9,13},{13,9},{2,6},{6,2},{1... | collective-permute-start | bytes 417800 | tf_op jit(solution)/shard_map/ppermute | solution.py:45
  34.4 1.3 %collective-permute-start.16 = (s16[272,256]{1,0:T(8,128)(2,1)S(1)}, s16[272,256]{1,0:T(8,128)(2,1)S(1)}, u32[]{:S(2)}, u32[]{:S(2)}) collective-permute-start(s16[272,256]{1,0:T(8,128)(2,1)S(1)} %get-tuple-element.53), channel_id=1, source_target_pairs={{0,8},{4,12},{8,0},{12,4},{1,9},{5,13},{9,1},{13,5},{2,10},{6,14},... | collective-permute-start | bytes 417800 | tf_op jit(solution)/shard_map/ppermute | solution.py:45
  35.6 0.0 collective-permute-done.12.refs_0_.refs_4_
  35.6 0.0 collective-permute-done.13.refs_1_.refs_5_
  35.6 0.6 %collective-permute-done.14.refs_2_.refs_6_ = s16[272,256]{1,0:T(8,128)(2,1)S(1)} collective-permute-done((s16[272,256]{1,0:T(8,128)(2,1)S(1)}, s16[272,256]{1,0:T(8,128)(2,1)S(1)}, u32[]{:S(2)}, u32[]{:S(2)}) %collective-permute-start.14) | collective-permute-done | bytes 139296 | tf_op jit(solution)/shard_map/ppermute | solution.py:45
  36.2 2.6 %tokens.1.tok_ref = bf16[512,1024]{1,0:T(8,128)(2,1)S(1)} custom-call(f32[2,1024,1024]{2,1,0:T(8,128)S(1)} %get-tuple-element.46.expo_ref, bf16[2,1024,1024]{2,1,0:T(8,128)(2,1)S(1)} %get-tuple-element.58.grad_ref, bf16[256,1024]{1,0:T(8,128)(2,1)S(1)} %get-tuple-element.59.qt_ref, bf16[256,1024]{1,0:T(8,128)(2,1)S(1)} %get-tuple-element.43.gt_ref, ...), custom_call_target="tpu_custom_call" | custom-call | flops 3300000000 | bytes 65536 | tf_op jit(solution)/shard_map/tokens/pallas_call | solution.py:371
  38.9 0.0 collective-permute-done.15.refs_3_._
  38.9 0.8 %weights.1 = (f32[4,72,512]{2,1,0:T(8,128)S(1)}, f32[72,512]{1,0:T(8,128)S(1)}, f32[64,512]{1,0:T(8,128)S(1)}, f32[64,512]{1,0:T(8,128)S(1)}, f32[64,512]{1,0:T(8,128)S(1)}) custom-call(bf16[1024,512]{1,0:T(8,128)(2,1)S(1)} %get-tuple-element.57.inp_ref, bf16[512,1024]{1,0:T(8,128)(2,1)S(1)} %tokens.1.tok_ref, f32[8,512]{1,0:T(8,128)S(1)} %get-tuple-element.60.slope_ref, ...), custom_call_target="tpu_custom_call" | custom-call | flops 1100000000 | bytes 65536 | tf_op jit(solution)/shard_map/weights/pallas_call | solution.py:371
  39.7 0.1 collective-permute-start.18
  39.8 0.5 collective-permute-start.19
  40.3 0.1 collective-permute-start.20
  40.4 0.4 collective-permute-start.21
  40.8 0.0 collective-permute-done.16.refs_4_
  40.8 1.8 %collective-permute-start.17 = (s16[272,256]{1,0:T(8,128)(2,1)S(1)}, s16[272,256]{1,0:T(8,128)(2,1)S(1)}, u32[]{:S(2)}, u32[]{:S(2)}) collective-permute-start(s16[272,256]{1,0:T(8,128)(2,1)S(1)} %get-tuple-element.54), channel_id=1, source_target_pairs={{0,12},{4,8},{8,4},{12,0},{1,13},{5,9},{9,5},{13,1},{2,14},{6,10},... | collective-permute-start | bytes 417800 | tf_op jit(solution)/shard_map/ppermute | solution.py:45
  42.6 0.0 collective-permute-done.19.refs_1_
  42.6 0.0 collective-permute-done.20.refs_2_
  42.6 0.0 collective-permute-done.21.refs_3_
  42.6 0.0 collective-permute-done.18.refs_0_
  42.6 0.1 pair.1
  42.8 1.0 %collective-permute-start.22 = (s16[144,256]{1,0:T(8,128)(2,1)S(1)}, s16[144,256]{1,0:T(8,128)(2,1)S(1)}, u32[]{:S(2)}, u32[]{:S(2)}) collective-permute-start(s16[144,256]{1,0:T(8,128)(2,1)S(1)} %get-tuple-element.67), channel_id=1, source_target_pairs={{0,4},{4,0},{8,12},{12,8},{1,5},{5,1},{9,13},{13,9},{2,6},{6,2},{1... | collective-permute-start | bytes 221192 | tf_op jit(solution)/shard_map/ppermute | solution.py:45
  43.8 0.8 %collective-permute-start.23 = (s16[144,256]{1,0:T(8,128)(2,1)S(1)}, s16[144,256]{1,0:T(8,128)(2,1)S(1)}, u32[]{:S(2)}, u32[]{:S(2)}) collective-permute-start(s16[144,256]{1,0:T(8,128)(2,1)S(1)} %get-tuple-element.68), channel_id=1, source_target_pairs={{0,8},{4,12},{8,0},{12,4},{1,9},{5,13},{9,1},{13,5},{2,10},{6,14},... | collective-permute-start | bytes 221192 | tf_op jit(solution)/shard_map/ppermute | solution.py:45
  44.5 1.8 %collective-permute-start.24 = (s16[144,256]{1,0:T(8,128)(2,1)S(1)}, s16[144,256]{1,0:T(8,128)(2,1)S(1)}, u32[]{:S(2)}, u32[]{:S(2)}) collective-permute-start(s16[144,256]{1,0:T(8,128)(2,1)S(1)} %get-tuple-element.69), channel_id=1, source_target_pairs={{0,12},{4,8},{8,4},{12,0},{1,13},{5,9},{9,5},{13,1},{2,14},{6,10},... | collective-permute-start | bytes 221192 | tf_op jit(solution)/shard_map/ppermute | solution.py:45
  46.3 1.9 %collective-permute-done.17.refs_5_ = s16[272,256]{1,0:T(8,128)(2,1)S(1)} collective-permute-done((s16[272,256]{1,0:T(8,128)(2,1)S(1)}, s16[272,256]{1,0:T(8,128)(2,1)S(1)}, u32[]{:S(2)}, u32[]{:S(2)}) %collective-permute-start.17) | collective-permute-done | bytes 139296 | tf_op jit(solution)/shard_map/ppermute | solution.py:45
  48.2 1.0 %latents.1 = (bf16[1,256,256]{2,1,0:T(8,128)(2,1)}, bf16[1,256,256]{2,1,0:T(8,128)(2,1)}) custom-call(f32[256,256]{1,0:T(8,128)S(1)} %get-tuple-element.45.out_ref, f32[256,256]{1,0:T(8,128)S(1)} %get-tuple-element.48.own_ref, s16[272,256]{1,0:T(8,128)(2,1)S(1)} %collective-permute-done.12.refs_0_.refs_4_, ...), custom_call_target="tpu_custom_call" | custom-call | flops 1100000000 | bytes 65536 | tf_op jit(solution)/shard_map/latents/pallas_call | solution.py:371
  49.3 0.3 collective-permute-done.22.refs_0_
  49.5 0.2 collective-permute-done.23.refs_1_
  49.7 0.8 %collective-permute-done.24.refs_2_ = s16[144,256]{1,0:T(8,128)(2,1)S(1)} collective-permute-done((s16[144,256]{1,0:T(8,128)(2,1)S(1)}, s16[144,256]{1,0:T(8,128)(2,1)S(1)}, u32[]{:S(2)}, u32[]{:S(2)}) %collective-permute-start.24) | collective-permute-done | bytes 73760 | tf_op jit(solution)/shard_map/ppermute | solution.py:45
  50.5 0.7 %last.1 = (f32[64,256]{1,0:T(8,128)}, f32[64,256]{1,0:T(8,128)}, f32[2]{0:T(128)}) custom-call(f32[72,512]{1,0:T(8,128)S(1)} %get-tuple-element.66.weight_ref, s16[144,256]{1,0:T(8,128)(2,1)S(1)} %collective-permute-done.22.refs_0_, s16[144,256]{1,0:T(8,128)(2,1)S(1)} %collective-permute-done.23.refs_1_, s16[144,256]{1,0:T(8,128)(2,1)S(1)} %collective-permute-done.24.refs_2_), custom_call_target="tpu_custom_call" | custom-call | flops 1100000000 | bytes 65536 | tf_op jit(solution)/shard_map/last/pallas_call | solution.py:371
  (5 shorter events, 0.0 us)
Async XLA Ops:
  0.6 11.5 %copy-start.3 = (bf16[1,256,256]{2,1,0:T(8,128)(2,1)S(1)}, bf16[1,256,256]{2,1,0:T(8,128)(2,1)}, u32[]{:S(2)}) copy-start(bf16[1,256,256]{2,1,0:T(8,128)(2,1)} %refs_0_.3) | copy-start | bytes 393220
  0.6 17.0 %copy-start.2 = (bf16[1,256,256]{2,1,0:T(8,128)(2,1)S(1)}, bf16[1,256,256]{2,1,0:T(8,128)(2,1)}, u32[]{:S(2)}) copy-start(bf16[1,256,256]{2,1,0:T(8,128)(2,1)} %refs_4_.1) | copy-start | bytes 393220
  0.7 11.5 %copy-start = (f32[2]{0:T(128)S(1)}, f32[2]{0:T(128)}, u32[]{:S(2)}) copy-start(f32[2]{0:T(128)} %slopes_ref.5) | copy-start | bytes 28
  0.7 11.5 %copy-start.1 = (s32[1,8]{1,0:T(1,128)S(1)}, s32[1,8]{1,0:T(1,128)}, u32[]{:S(2)}) copy-start(s32[1,8]{1,0:T(1,128)} %bounds_ref.3) | copy-start | bytes 100
  0.7 11.3 %collective-permute-start.2 = (bf16[1,256,256]{2,1,0:T(8,128)(2,1)}, bf16[1,256,256]{2,1,0:T(8,128)(2,1)S(1)}, u32[]{:S(2)}, u32[]{:S(2)}) collective-permute-start(bf16[1,256,256]{2,1,0:T(8,128)(2,1)} %refs_0_.3), channel_id=1, source_target_pairs={{0,12},{4,8},{8,4},{12,0},{1,13},{5,9},{9,5},{13,1},{2,14},{6,10},... | collective-permute-start | bytes 393224 | tf_op jit(solution)/shard_map/ppermute | solution.py:45
  4.6 7.5 %collective-permute-start.1 = (bf16[1,256,256]{2,1,0:T(8,128)(2,1)}, bf16[1,256,256]{2,1,0:T(8,128)(2,1)S(1)}, u32[]{:S(2)}, u32[]{:S(2)}) collective-permute-start(bf16[1,256,256]{2,1,0:T(8,128)(2,1)} %refs_0_.3), channel_id=1, source_target_pairs={{0,8},{4,12},{8,0},{12,4},{1,9},{5,13},{9,1},{13,5},{2,10},{6,14},... | collective-permute-start | bytes 393224 | tf_op jit(solution)/shard_map/ppermute | solution.py:45
  5.1 7.0 %collective-permute-start = (bf16[1,256,256]{2,1,0:T(8,128)(2,1)}, bf16[1,256,256]{2,1,0:T(8,128)(2,1)S(1)}, u32[]{:S(2)}, u32[]{:S(2)}) collective-permute-start(bf16[1,256,256]{2,1,0:T(8,128)(2,1)} %refs_0_.3), channel_id=1, source_target_pairs={{0,4},{4,0},{8,12},{12,8},{1,5},{5,1},{9,13},{13,9},{2,6},{6,2},{1... | collective-permute-start | bytes 393224 | tf_op jit(solution)/shard_map/ppermute | solution.py:45
  8.6 8.9 %collective-permute-start.5 = (bf16[1,256,256]{2,1,0:T(8,128)(2,1)S(1)}, bf16[1,256,256]{2,1,0:T(8,128)(2,1)S(1)}, u32[]{:S(2)}, u32[]{:S(2)}) collective-permute-start(bf16[1,256,256]{2,1,0:T(8,128)(2,1)S(1)} %get-tuple-element.42), channel_id=1, source_target_pairs={{0,12},{4,8},{8,4},{12,0},{1,13},{5,9},{9,5},{13,1},{2,14},{6,10},... | collective-permute-start | bytes 393224 | tf_op jit(solution)/shard_map/ppermute | solution.py:45
  11.5 6.1 %collective-permute-start.4 = (bf16[1,256,256]{2,1,0:T(8,128)(2,1)S(1)}, bf16[1,256,256]{2,1,0:T(8,128)(2,1)S(1)}, u32[]{:S(2)}, u32[]{:S(2)}) collective-permute-start(bf16[1,256,256]{2,1,0:T(8,128)(2,1)S(1)} %get-tuple-element.42), channel_id=1, source_target_pairs={{0,8},{4,12},{8,0},{12,4},{1,9},{5,13},{9,1},{13,5},{2,10},{6,14},... | collective-permute-start | bytes 393224 | tf_op jit(solution)/shard_map/ppermute | solution.py:45
  12.0 5.6 %collective-permute-start.3 = (bf16[1,256,256]{2,1,0:T(8,128)(2,1)S(1)}, bf16[1,256,256]{2,1,0:T(8,128)(2,1)S(1)}, u32[]{:S(2)}, u32[]{:S(2)}) collective-permute-start(bf16[1,256,256]{2,1,0:T(8,128)(2,1)S(1)} %get-tuple-element.42), channel_id=1, source_target_pairs={{0,4},{4,0},{8,12},{12,8},{1,5},{5,1},{9,13},{13,9},{2,6},{6,2},{1... | collective-permute-start | bytes 393224 | tf_op jit(solution)/shard_map/ppermute | solution.py:45
  14.0 5.2 %collective-permute-start.8 = (f32[16,256]{1,0:T(8,128)S(1)}, f32[16,256]{1,0:T(8,128)S(1)}, u32[]{:S(2)}, u32[]{:S(2)}) collective-permute-start(f32[16,256]{1,0:T(8,128)S(1)} %get-tuple-element.44.refs_0_), channel_id=1, source_target_pairs={{0,12},{4,8},{8,4},{12,0},{1,13},{5,9},{9,5},{13,1},{2,14},{6,10},... | collective-permute-start | bytes 49160 | tf_op jit(solution)/shard_map/ppermute | solution.py:45
  16.9 3.7 %collective-permute-start.7 = (f32[16,256]{1,0:T(8,128)S(1)}, f32[16,256]{1,0:T(8,128)S(1)}, u32[]{:S(2)}, u32[]{:S(2)}) collective-permute-start(f32[16,256]{1,0:T(8,128)S(1)} %get-tuple-element.44.refs_0_), channel_id=1, source_target_pairs={{0,8},{4,12},{8,0},{12,4},{1,9},{5,13},{9,1},{13,5},{2,10},{6,14},... | collective-permute-start | bytes 49160 | tf_op jit(solution)/shard_map/ppermute | solution.py:45
  17.5 3.7 %collective-permute-start.6 = (f32[16,256]{1,0:T(8,128)S(1)}, f32[16,256]{1,0:T(8,128)S(1)}, u32[]{:S(2)}, u32[]{:S(2)}) collective-permute-start(f32[16,256]{1,0:T(8,128)S(1)} %get-tuple-element.44.refs_0_), channel_id=1, source_target_pairs={{0,4},{4,0},{8,12},{12,8},{1,5},{5,1},{9,13},{13,9},{2,6},{6,2},{1... | collective-permute-start | bytes 49160 | tf_op jit(solution)/shard_map/ppermute | solution.py:45
  23.7 5.6 %collective-permute-start.11 = (f32[16,256]{1,0:T(8,128)S(1)}, f32[16,256]{1,0:T(8,128)S(1)}, u32[]{:S(2)}, u32[]{:S(2)}) collective-permute-start(f32[16,256]{1,0:T(8,128)S(1)} %get-tuple-element.47.refs_4_.refs_6_.refs_0_), channel_id=1, source_target_pairs={{0,12},{4,8},{8,4},{12,0},{1,13},{5,9},{9,5},{13,1},{2,14},{6,10},... | collective-permute-start | bytes 49160 | tf_op jit(solution)/shard_map/ppermute | solution.py:45
  25.3 5.5 %collective-permute-start.10 = (f32[16,256]{1,0:T(8,128)S(1)}, f32[16,256]{1,0:T(8,128)S(1)}, u32[]{:S(2)}, u32[]{:S(2)}) collective-permute-start(f32[16,256]{1,0:T(8,128)S(1)} %get-tuple-element.47.refs_4_.refs_6_.refs_0_), channel_id=1, source_target_pairs={{0,8},{4,12},{8,0},{12,4},{1,9},{5,13},{9,1},{13,5},{2,10},{6,14},... | collective-permute-start | bytes 49160 | tf_op jit(solution)/shard_map/ppermute | solution.py:45
  25.4 5.4 %collective-permute-start.9 = (f32[16,256]{1,0:T(8,128)S(1)}, f32[16,256]{1,0:T(8,128)S(1)}, u32[]{:S(2)}, u32[]{:S(2)}) collective-permute-start(f32[16,256]{1,0:T(8,128)S(1)} %get-tuple-element.47.refs_4_.refs_6_.refs_0_), channel_id=1, source_target_pairs={{0,4},{4,0},{8,12},{12,8},{1,5},{5,1},{9,13},{13,9},{2,6},{6,2},{1... | collective-permute-start | bytes 49160 | tf_op jit(solution)/shard_map/ppermute | solution.py:45
  27.3 8.4 %collective-permute-start.12 = (s16[272,256]{1,0:T(8,128)(2,1)S(1)}, s16[272,256]{1,0:T(8,128)(2,1)S(1)}, u32[]{:S(2)}, u32[]{:S(2)}) collective-permute-start(s16[272,256]{1,0:T(8,128)(2,1)S(1)} %get-tuple-element.49), channel_id=1, source_target_pairs={{0,4},{4,0},{8,12},{12,8},{1,5},{5,1},{9,13},{13,9},{2,6},{6,2},{1... | collective-permute-start | bytes 417800 | tf_op jit(solution)/shard_map/ppermute | solution.py:45
  27.4 8.2 %collective-permute-start.13 = (s16[272,256]{1,0:T(8,128)(2,1)S(1)}, s16[272,256]{1,0:T(8,128)(2,1)S(1)}, u32[]{:S(2)}, u32[]{:S(2)}) collective-permute-start(s16[272,256]{1,0:T(8,128)(2,1)S(1)} %get-tuple-element.50), channel_id=1, source_target_pairs={{0,8},{4,12},{8,0},{12,4},{1,9},{5,13},{9,1},{13,5},{2,10},{6,14},... | collective-permute-start | bytes 417800 | tf_op jit(solution)/shard_map/ppermute | solution.py:45
  29.3 6.9 %collective-permute-start.14 = (s16[272,256]{1,0:T(8,128)(2,1)S(1)}, s16[272,256]{1,0:T(8,128)(2,1)S(1)}, u32[]{:S(2)}, u32[]{:S(2)}) collective-permute-start(s16[272,256]{1,0:T(8,128)(2,1)S(1)} %get-tuple-element.51), channel_id=1, source_target_pairs={{0,12},{4,8},{8,4},{12,0},{1,13},{5,9},{9,5},{13,1},{2,14},{6,10},... | collective-permute-start | bytes 417800 | tf_op jit(solution)/shard_map/ppermute | solution.py:45
  33.5 5.3 %collective-permute-start.15 = (s16[272,256]{1,0:T(8,128)(2,1)S(1)}, s16[272,256]{1,0:T(8,128)(2,1)S(1)}, u32[]{:S(2)}, u32[]{:S(2)}) collective-permute-start(s16[272,256]{1,0:T(8,128)(2,1)S(1)} %get-tuple-element.52), channel_id=1, source_target_pairs={{0,4},{4,0},{8,12},{12,8},{1,5},{5,1},{9,13},{13,9},{2,6},{6,2},{1... | collective-permute-start | bytes 417800 | tf_op jit(solution)/shard_map/ppermute | solution.py:45
  34.4 6.4 %collective-permute-start.16 = (s16[272,256]{1,0:T(8,128)(2,1)S(1)}, s16[272,256]{1,0:T(8,128)(2,1)S(1)}, u32[]{:S(2)}, u32[]{:S(2)}) collective-permute-start(s16[272,256]{1,0:T(8,128)(2,1)S(1)} %get-tuple-element.53), channel_id=1, source_target_pairs={{0,8},{4,12},{8,0},{12,4},{1,9},{5,13},{9,1},{13,5},{2,10},{6,14},... | collective-permute-start | bytes 417800 | tf_op jit(solution)/shard_map/ppermute | solution.py:45
  39.7 2.9 %collective-permute-start.18 = (f32[72,512]{1,0:T(8,128)S(1)}, f32[72,512]{1,0:T(8,128)S(1)}, u32[]{:S(2)}, u32[]{:S(2)}) collective-permute-start(f32[72,512]{1,0:T(8,128)S(1)} %get-tuple-element.62), channel_id=1, source_target_pairs={{0,16},{16,0},{1,17},{17,1},{2,18},{18,2},{3,19},{19,3},{4,20},{20... | collective-permute-start | bytes 442376 | tf_op jit(solution)/shard_map/ppermute | solution.py:45
  39.8 2.8 %collective-permute-start.19 = (f32[64,512]{1,0:T(8,128)S(1)}, f32[64,512]{1,0:T(8,128)S(1)}, u32[]{:S(2)}, u32[]{:S(2)}) collective-permute-start(f32[64,512]{1,0:T(8,128)S(1)} %get-tuple-element.63), channel_id=1, source_target_pairs={{0,16},{16,0},{1,17},{17,1},{2,18},{18,2},{3,19},{19,3},{4,20},{20... | collective-permute-start | bytes 393224 | tf_op jit(solution)/shard_map/ppermute | solution.py:45
  40.3 2.3 %collective-permute-start.20 = (f32[64,512]{1,0:T(8,128)S(1)}, f32[64,512]{1,0:T(8,128)S(1)}, u32[]{:S(2)}, u32[]{:S(2)}) collective-permute-start(f32[64,512]{1,0:T(8,128)S(1)} %get-tuple-element.64), channel_id=1, source_target_pairs={{0,16},{16,0},{1,17},{17,1},{2,18},{18,2},{3,19},{19,3},{4,20},{20... | collective-permute-start | bytes 393224 | tf_op jit(solution)/shard_map/ppermute | solution.py:45
  40.4 2.3 %collective-permute-start.21 = (f32[64,512]{1,0:T(8,128)S(1)}, f32[64,512]{1,0:T(8,128)S(1)}, u32[]{:S(2)}, u32[]{:S(2)}) collective-permute-start(f32[64,512]{1,0:T(8,128)S(1)} %get-tuple-element.65), channel_id=1, source_target_pairs={{0,16},{16,0},{1,17},{17,1},{2,18},{18,2},{3,19},{19,3},{4,20},{20... | collective-permute-start | bytes 393224 | tf_op jit(solution)/shard_map/ppermute | solution.py:45
  40.8 7.4 %collective-permute-start.17 = (s16[272,256]{1,0:T(8,128)(2,1)S(1)}, s16[272,256]{1,0:T(8,128)(2,1)S(1)}, u32[]{:S(2)}, u32[]{:S(2)}) collective-permute-start(s16[272,256]{1,0:T(8,128)(2,1)S(1)} %get-tuple-element.54), channel_id=1, source_target_pairs={{0,12},{4,8},{8,4},{12,0},{1,13},{5,9},{9,5},{13,1},{2,14},{6,10},... | collective-permute-start | bytes 417800 | tf_op jit(solution)/shard_map/ppermute | solution.py:45
  42.8 6.8 %collective-permute-start.22 = (s16[144,256]{1,0:T(8,128)(2,1)S(1)}, s16[144,256]{1,0:T(8,128)(2,1)S(1)}, u32[]{:S(2)}, u32[]{:S(2)}) collective-permute-start(s16[144,256]{1,0:T(8,128)(2,1)S(1)} %get-tuple-element.67), channel_id=1, source_target_pairs={{0,4},{4,0},{8,12},{12,8},{1,5},{5,1},{9,13},{13,9},{2,6},{6,2},{1... | collective-permute-start | bytes 221192 | tf_op jit(solution)/shard_map/ppermute | solution.py:45
  43.8 6.0 %collective-permute-start.23 = (s16[144,256]{1,0:T(8,128)(2,1)S(1)}, s16[144,256]{1,0:T(8,128)(2,1)S(1)}, u32[]{:S(2)}, u32[]{:S(2)}) collective-permute-start(s16[144,256]{1,0:T(8,128)(2,1)S(1)} %get-tuple-element.68), channel_id=1, source_target_pairs={{0,8},{4,12},{8,0},{12,4},{1,9},{5,13},{9,1},{13,5},{2,10},{6,14},... | collective-permute-start | bytes 221192 | tf_op jit(solution)/shard_map/ppermute | solution.py:45
  44.5 6.0 %collective-permute-start.24 = (s16[144,256]{1,0:T(8,128)(2,1)S(1)}, s16[144,256]{1,0:T(8,128)(2,1)S(1)}, u32[]{:S(2)}, u32[]{:S(2)}) collective-permute-start(s16[144,256]{1,0:T(8,128)(2,1)S(1)} %get-tuple-element.69), channel_id=1, source_target_pairs={{0,12},{4,8},{8,4},{12,0},{1,13},{5,9},{9,5},{13,1},{2,14},{6,10},... | collective-permute-start | bytes 221192 | tf_op jit(solution)/shard_map/ppermute | solution.py:45

commit v5 on v4

--- a/solution.py
+++ b/solution.py
@@ -12,8 +12,10 @@
 LOG2E = 1.4426950408889634
 CODE_MAX = 32000.0
 TINY = 1e-30
+WHOLE = 1.5 * 2.0**23
 CHUNK = 512
 STEP = 256
+GIVES = 2
 LIM_P, LIM_T, LIM_D, LIM_S, LIM_G = 55, 8, 8, 16, 16
 SCALE = HEAD ** (-0.5)
 UNIT = SCALE * LOG2E
@@ -48,8 +50,11 @@
 def encode(x):
     most = jnp.maximum(jnp.max(jnp.abs(x), axis=0, keepdims=True), TINY)
     exponent = jnp.ceil(jnp.log2(most))
-    steps = jnp.round(x * (jnp.exp2(-exponent) * CODE_MAX))
-    return steps, exponent
+    return whole(x * (jnp.exp2(-exponent) * CODE_MAX)), exponent
+
+
+def whole(x):
+    return (x + WHOLE) - WHOLE
 
 
 def decode(steps, exponent):
@@ -184,7 +189,7 @@
 
 
 def sums_kernel(n, slopes_ref, val_ref, score_ref, gt_ref, _, *refs):
-    top_refs, (stats_ref, own_ref, expo_ref), send_refs = refs[:n], refs[n : n + 3], refs[n + 3 :]
+    top_refs, (stats_ref, out_ref, expo_ref) = refs[:n], refs[n:]
     heads, tokens, lats = score_ref.shape
     rows = lats // n
     tops, base = merged_tops(n, heads, slopes_ref, top_refs)
@@ -200,8 +205,7 @@
             part_norm = jnp.sum(expo, axis=0, keepdims=True)
             out = term if out is None else out + term
             norm = part_norm if norm is None else norm + part_norm
-        own_ref[head_cols(h), :] = out[:, :rows]
-        write_messages(h, rows, out, send_refs)
+        out_ref[head_cols(h), :] = out
         delta = jnp.sum(gt_ref[head_cols(h), :].astype(F32) * out, axis=0, keepdims=True)
         for j in range(n):
             cols = slice(j * rows, (j + 1) * rows)
@@ -246,7 +250,7 @@
     return norms, deltas
 
 
-def rows_kernel(n, bounds_ref, slopes_ref, key_ref, expo_ref, dprod_ref, *refs):
+def rows_kernel(n, bounds_ref, slopes_ref, key_ref, expo_ref, dprod_ref, out_ref, *refs):
     top_refs, sum_refs, refs = refs[:n], refs[n : 2 * n], refs[2 * n :]
     own_ref, grad_ref, slope_ref = refs[:3]
     send_refs = refs[3 : n + 2]
@@ -273,7 +277,8 @@
             term = tn(key_ref[part, head_cols(h)], score_grad_b)
             dq = term if dq is None else dq + term
         own_ref[head_cols(h), :] = dq[:, :rows]
-        write_messages(h, rows, dq, send_refs)
+        write_messages(2 * h, rows, dq, send_refs)
+        write_messages(2 * h + 1, rows, out_ref[head_cols(h), :], send_refs)
         total = jnp.sum(slope, axis=1, keepdims=True)
         slope_ref[:, h * 2 * HEAD : (h + 1) * 2 * HEAD] = jnp.broadcast_to(total, (8, 2 * HEAD))
 
@@ -293,56 +298,73 @@
             tok_ref[at + HEAD : at + 2 * HEAD, part] = nt(gt_ref[head_cols(h), :], probs).astype(BF16)
 
 
-def weights_kernel(n, inp_ref, tok_ref, slope_ref, _, keep_ref, *refs):
-    give_refs, weight_ref = refs[:n], refs[n]
-    _, half, _ = weight_ref.shape
+def digits_of(value):
+    steps, exponent = encode(value)
+    left = value * (jnp.exp2(-exponent) * CODE_MAX) - steps
+    return [exponent, steps, whole(left * CODE_MAX)]
+
+
+def value_of(rows):
+    return decode(rows[1] + rows[2] * (1.0 / CODE_MAX), rows[0])
+
+
+def give_place(k):
+    return min(k, GIVES - 1), max(k - GIVES + 1, 0)
+
+
+def weights_kernel(n, inp_ref, tok_ref, slope_ref, *refs):
+    keep_ref, *give_refs, weight_ref = refs[-2 - GIVES :]
+    _, half, width = weight_ref.shape
     piece = half // n
     for i in range(2):
         side = inp_ref[:, i * half : (i + 1) * half]
         weight_ref[i] = lax.dot_general(side, tok_ref[...], (((0,), (1,)), ((), ())), preferred_element_type=F32)
     core, me = lax.axis_index("dp"), lax.axis_index("seq")
-    for k, give_ref in enumerate(give_refs):
+    steps, exponent = encode(weight_ref[1 - core])
+    weight_ref[1 - core] = steps
+    for k in range(n):
         rows = pl.ds(pl.multiple_of((me ^ k) * piece, piece), piece)
-        keep_ref[k, :piece, :] = weight_ref[core, rows, :]
-        give_ref[:piece, :] = weight_ref[1 - core, rows, :]
-    keep_ref[0, piece:, :] = slope_ref[...]
-    give_refs[0][piece:, :] = slope_ref[...]
-
-
-def pair_kernel(n, heads, keep_ref, *refs):
-    got_refs, own_ref, send_refs = refs[:n], refs[-n], refs[1 - n :]
-    piece = keep_ref.shape[1] - 8
+        keep_ref[k * piece : (k + 1) * piece, :] = weight_ref[core, rows, :]
+        ref, at = give_refs[give_place(k)[0]], give_place(k)[1]
+        ref[at * piece : (at + 1) * piece, :] = to_code(weight_ref[1 - core, rows, :])
+    give_refs[0][piece : piece + 16, :] = to_code(stack_rows([exponent] + digits_of(slope_ref[0:1, :]), 16, width))
+
+
+def pair_kernel(n, heads, keep_ref, slope_ref, *refs):
+    got_refs, own_ref, send_refs = refs[:GIVES], refs[-n], refs[1 - n :]
+    half = keep_ref.shape[0]
+    piece = half // n
     width = 2 * HEAD
-    own_ref[...] = keep_ref[0] + got_refs[0][...]
-    digits = []
-    for h in range(heads):
-        value = own_ref[piece : piece + 1, h * width : (h + 1) * width]
-        steps, exponent = encode(value)
-        left = value * (jnp.exp2(-exponent) * CODE_MAX) - steps
-        digits += [exponent, steps, jnp.round(left * CODE_MAX)]
-    for k in range(1, n):
-        total = keep_ref[k, :piece, :] + got_refs[k][...]
-        exponents = []
+    extra = from_code(got_refs[0][piece : piece + 16, :])
+    slope = slope_ref[0:1, :] + value_of([extra[i : i + 1, :] for i in range(1, 4)])
+    own_ref[piece:, :] = jnp.broadcast_to(slope, (8, heads * width))
+    digits = digits_of(slope)
+    for k in range(n):
+        ref, at = got_refs[give_place(k)[0]], give_place(k)[1]
+        got = decode(from_code(ref[at * piece : (at + 1) * piece, :]), extra[0:1, :])
+        total = keep_ref[k * piece : (k + 1) * piece, :] + got
+        if k == 0:
+            own_ref[:piece, :] = total
+            continue
+        steps, exponent = encode(total)
+        rows = []
         for h in range(heads):
-            steps, exponent = encode(total[:, h * width : (h + 1) * width])
-            send_refs[k - 1][h * piece : (h + 1) * piece, :] = to_code(steps)
-            exponents.append(exponent)
-        send_refs[k - 1][heads * piece :, :] = to_code(stack_rows(exponents + digits, 16, width))
+            cols = slice(h * width, (h + 1) * width)
+            send_refs[k - 1][h * piece : (h + 1) * piece, :] = to_code(steps[:, cols])
+            rows += [x[:, cols] for x in (exponent, *digits)]
+        send_refs[k - 1][heads * piece :, :] = to_code(stack_rows(rows, 16, width))
 
 
 def latents_kernel(n, heads, out_ref, own_ref, *refs):
-    others = n - 1
-    att_refs, dq_refs, sum_refs = refs[:others], refs[others : 2 * others], refs[2 * others : -2]
-    att_ref, grad_ref = refs[-2:]
+    got_refs, sum_refs, (att_ref, grad_ref) = refs[: n - 1], refs[n - 1 : 2 * n - 1], refs[2 * n - 1 :]
     rows = att_ref.shape[1]
     norms, _ = merged_sums(n, heads, sum_refs)
     for h in range(heads):
-        total = out_ref[head_cols(h), :]
-        for ref in att_refs:
-            total = total + read_message(ref, h)
+        total = out_ref[head_cols(h), :rows]
         grad = own_ref[head_cols(h), :]
-        for ref in dq_refs:
-            grad = grad + read_message(ref, h)
+        for ref in got_refs:
+            grad = grad + read_message(ref, 2 * h)
+            total = total + read_message(ref, 2 * h + 1)
         total = total / norms[h][:, :rows]
         att_ref[0, :, head_cols(h)] = total.T.astype(BF16)
         grad_ref[0, :, head_cols(h)] = (SCALE * grad).T.astype(BF16)
@@ -358,10 +380,9 @@
         total = weight_ref[:piece, cols]
         slope = weight_ref[piece : piece + 1, cols]
         for ref, extra in zip(part_refs, extras):
-            total = total + decode(from_code(ref[h * piece : (h + 1) * piece, :]), extra[h : h + 1, :])
-            place = heads + 3 * h
-            exponent, steps, left = (extra[place + i : place + i + 1, :] for i in range(3))
-            slope = slope + decode(steps + left * (1.0 / CODE_MAX), exponent)
+            exponent, *digits = (extra[4 * h + i : 4 * h + i + 1, :] for i in range(4))
+            total = total + decode(from_code(ref[h * piece : (h + 1) * piece, :]), exponent)
+            slope = slope + value_of(digits)
         key_ref[:, head_cols(h)] = total[:, :HEAD]
         val_ref[:, head_cols(h)] = total[:, HEAD:]
         slope_ref[h] = slope[0, 0]
@@ -400,7 +421,7 @@
     g_all = [grad] + [swap(grad, "seq", k, n) for k in peers]
     stat_rows = -(-(heads * n + 1) // 8) * 8
     square = ((heads, toks, lats), F32)
-    block = ((width + 16, rows), I16)
+    block = ((2 * width + 16, rows), I16)
     top_own, scores = call(
         functools.partial(top_kernel, n),
         "tops",
@@ -423,32 +444,31 @@
     sums = call(
         functools.partial(sums_kernel, n),
         "sums",
-        [((2 * heads * n, rows), F32), ((width, rows), F32), square] + [block] * (n - 1),
+        [((2 * heads * n, rows), F32), ((width, lats), F32), square],
         (slopes, values, scores, g_turned, dprod, *tops),
         2,
         smem=1,
         limit=LIM_S << 20,
     )
     norms = [sums[0]] + [swap(sums[0], "seq", k, n) for k in peers]
-    outs = [swap(sums[2 + k], "seq", k, n) for k in peers]
     own_dq, score_grads, slope_terms, *sends = call(
         functools.partial(rows_kernel, n),
         "rows",
         [((width, rows), F32), ((heads, toks, lats), BF16), ((8, 2 * width), F32)]
         + [block] * (n - 1),
-        (boundaries, slopes, keys, sums[2], dprod, *tops, *norms),
+        (boundaries, slopes, keys, sums[2], dprod, sums[1], *tops, *norms),
         3,
         [pltpu.VMEM((toks, 128), F32)],
         2,
         limit=LIM_G << 20,
     )
-    dqs = [swap(x, "seq", k, n) for k, x in zip(peers, sends)]
+    blocks = [swap(x, "seq", k, n) for k, x in zip(peers, sends)]
     half = channels // 2
     (tok_grads,) = call(
         functools.partial(tokens_kernel, n),
         "tokens",
         [((2 * width, toks), BF16)],
-        (sums[2], score_grads, q_turned, g_turned, *norms, *outs),
+        (sums[2], score_grads, q_turned, g_turned, *norms),
         3,
         limit=LIM_G << 20,
     )
@@ -456,8 +476,10 @@
     weights = call(
         functools.partial(weights_kernel, n),
         "weights",
-        [((n, piece + 8, 2 * width), F32), ((piece + 8, 2 * width), F32)] + [((piece, 2 * width), F32)] * (n - 1),
-        (inputs, tok_grads, slope_terms, dqs[0]),
+        [((half, 2 * width), F32), ((piece + 16, 2 * width), I16)]
+        + [((piece, 2 * width), I16)] * (GIVES - 2)
+        + [(((n - GIVES + 1) * piece, 2 * width), I16)],
+        (inputs, tok_grads, slope_terms),
         1,
         [pltpu.VMEM((2, half, 2 * width), F32)],
         limit=LIM_G << 20,
@@ -467,14 +489,14 @@
         functools.partial(latents_kernel, n, heads),
         "latents",
         [((1, rows, width), BF16)] * 2,
-        (sums[1], own_dq, *outs, *dqs, *norms),
+        (sums[1], own_dq, *blocks, *norms),
         1,
     )
     pair = call(
         functools.partial(pair_kernel, n, heads),
         "pair",
         [((piece + 8, 2 * width), F32)] + [((heads * piece + 16, 2 * HEAD), I16)] * (n - 1),
-        (weights[0], *got, dqs[1]),
+        (weights[0], slope_terms, *got, blocks[0]),
         0.3,
     )
     parts = [swap(pair[k], "seq", k, n) for k in peers]
@@ -594,8 +616,9 @@
     n = mesh.shape["seq"]
 
     def per_device(*args):
-        rows = args[7].shape[1]
-        if n in (2, 4, 8) and mesh.shape["dp"] == 2 and rows % 128 == 0:
+        toks, (rows, width) = args[0].shape[1], args[7].shape[1:]
+        fits = rows % 128 == 0 and toks % CHUNK == 0 and toks // BLOCK <= 256 and width // HEAD <= 4
+        if n in (2, 4, 8) and mesh.shape["dp"] == 2 and fits:
             return per_device_blocks(n, *args)
         return per_device_general(*args)
 

time: 51.4 us -> 50.5 us (0.982)
  starting transfers between devices: 27.3 us -> 22.9 us
  waiting for transfers between devices: 5.81 us -> 9.06 us
    ppermute x25 -> x20, starting transfers between devices: 27.3 us -> 22.9 us  [swap(): return lax.ppermute(x, axis, [(i, i ^ k) for i in range(n)])]
    ppermute x25 -> x20, waiting for transfers between devices: 5.81 us -> 9.06 us  [swap(): return lax.ppermute(x, axis, [(i, i ^ k) for i in range(n)])]
  transfers between devices with their start and end apart: 25 -> 20, of which waited for: 7 -> 8; matrix products, arithmetic and copies ran while one was open for 0% -> 0% of each run, Pallas kernels for 27% -> 23%
where the time goes in v5:
time: 50.5 us; the launch traced here: 50.4 us
  starting transfers between devices  22.9 us (45%)
  Pallas kernels  17.6 us (35%)
  waiting for transfers between devices  9.06 us (18%)
  between operations  0.78 us (2%)
    ppermute x20, starting transfers between devices, swap(): return lax.ppermute(x, axis, [(i, i ^ k) for i in range(n)])  22.9 us
    pallas_call x11, Pallas kernels, call(): pl.pallas_call(kernel, out_shape=[jax.ShapeDtypeStruct(shape, dtype) for...  17.6 us
    ppermute x20, waiting for transfers between devices, swap(): return lax.ppermute(x, axis, [(i, i ^ k) for i in range(n)])  9.06 us
  transfers between devices with their start and end apart: 20, of which 8 were waited for; matrix products, arithmetic and copies ran while one was open for 0% of the time, Pallas kernels for 23%

profile of v5, /device:TPU:0, one launch (start us, length us, event | category | flops | bytes accessed | tf_op | source)
XLA Modules:
  0.0 50.4 jit_solution(3922273255542343405)
XLA Ops:
  0.6 0.0 copy-start.3
  0.6 0.0 copy-start.2
  0.7 0.0 copy-start
  0.7 0.0 copy-start.1
  0.7 4.0 %collective-permute-start.2 = (bf16[1,256,256]{2,1,0:T(8,128)(2,1)}, bf16[1,256,256]{2,1,0:T(8,128)(2,1)S(1)}, u32[]{:S(2)}, u32[]{:S(2)}) collective-permute-start(bf16[1,256,256]{2,1,0:T(8,128)(2,1)} %refs_0_.3), channel_id=1, source_target_pairs={{0,12},{4,8},{8,4},{12,0},{1,13},{5,9},{9,5},{13,1},{2,14},{6,10},... | collective-permute-start | bytes 393224 | tf_op jit(solution)/shard_map/ppermute | solution.py:47
  4.6 0.5 %collective-permute-start.1 = (bf16[1,256,256]{2,1,0:T(8,128)(2,1)}, bf16[1,256,256]{2,1,0:T(8,128)(2,1)S(1)}, u32[]{:S(2)}, u32[]{:S(2)}) collective-permute-start(bf16[1,256,256]{2,1,0:T(8,128)(2,1)} %refs_0_.3), channel_id=1, source_target_pairs={{0,8},{4,12},{8,0},{12,4},{1,9},{5,13},{9,1},{13,5},{2,10},{6,14},... | collective-permute-start | bytes 393224 | tf_op jit(solution)/shard_map/ppermute | solution.py:47
  5.1 0.1 collective-permute-start
  5.3 3.3 %prep.1 = (bf16[1024,512]{1,0:T(8,128)(2,1)S(1)}, bf16[1024,256]{1,0:T(8,128)(2,1)S(1)}, bf16[1024,256]{1,0:T(8,128)(2,1)S(1)}, bf16[1,256,256]{2,1,0:T(8,128)(2,1)S(1)}) custom-call(bf16[1,1024,512]{2,1,0:T(8,128)(2,1)} %tok_hbm.1, s32[1,1024]{1,0:T(1,128)} %lev_hbm.1, f32[256,512]{1,0:T(8,128)} %table_hbm.1, bf16[512,256]{1,0:T(8,128)(2,1)} %wk_hbm.1, ...), custom_call_target="tpu_custom_call" | custom-call | flops 3300000000 | bytes 65536 | tf_op jit(solution)/shard_map/prep/pallas_call | solution.py:392
  8.6 2.9 %collective-permute-start.5 = (bf16[1,256,256]{2,1,0:T(8,128)(2,1)S(1)}, bf16[1,256,256]{2,1,0:T(8,128)(2,1)S(1)}, u32[]{:S(2)}, u32[]{:S(2)}) collective-permute-start(bf16[1,256,256]{2,1,0:T(8,128)(2,1)S(1)} %get-tuple-element.37), channel_id=1, source_target_pairs={{0,12},{4,8},{8,4},{12,0},{1,13},{5,9},{9,5},{13,1},{2,14},{6,10},... | collective-permute-start | bytes 393224 | tf_op jit(solution)/shard_map/ppermute | solution.py:47
  11.5 0.5 %collective-permute-start.4 = (bf16[1,256,256]{2,1,0:T(8,128)(2,1)S(1)}, bf16[1,256,256]{2,1,0:T(8,128)(2,1)S(1)}, u32[]{:S(2)}, u32[]{:S(2)}) collective-permute-start(bf16[1,256,256]{2,1,0:T(8,128)(2,1)S(1)} %get-tuple-element.37), channel_id=1, source_target_pairs={{0,8},{4,12},{8,0},{12,4},{1,9},{5,13},{9,1},{13,5},{2,10},{6,14},... | collective-permute-start | bytes 393224 | tf_op jit(solution)/shard_map/ppermute | solution.py:47
  12.0 0.0 collective-permute-done.2.refs_3_
  12.0 0.1 collective-permute-start.3
  12.1 0.0 collective-permute-done.1.refs_2_
  12.1 0.0 collective-permute-done.refs_1_
  12.1 0.0 copy-done.3
  12.1 0.0 copy-done
  12.1 0.0 copy-done.1
  12.2 1.9 %tops.1 = (f32[16,256]{1,0:T(8,128)S(1)}, f32[2,1024,1024]{2,1,0:T(8,128)S(1)}) custom-call(s32[1,8]{1,0:T(1,128)S(1)} %copy-done.1, f32[2]{0:T(128)S(1)} %copy-done, bf16[1024,256]{1,0:T(8,128)(2,1)S(1)} %get-tuple-element.35.key_ref, bf16[1,256,256]{2,1,0:T(8,128)(2,1)S(1)} %copy-done.3, bf16[1,256,256]{2,1,0:T(8,128)(2,1)S(1)} %collective-permute-done.refs_1_, ...), custom_call_target="tpu_custom_call" | custom-call | flops 2200000000 | bytes 65536 | tf_op jit(solution)/shard_map/tops/pallas_call | solution.py:392
  14.0 2.9 %collective-permute-start.8 = (f32[16,256]{1,0:T(8,128)S(1)}, f32[16,256]{1,0:T(8,128)S(1)}, u32[]{:S(2)}, u32[]{:S(2)}) collective-permute-start(f32[16,256]{1,0:T(8,128)S(1)} %get-tuple-element.39.refs_0_), channel_id=1, source_target_pairs={{0,12},{4,8},{8,4},{12,0},{1,13},{5,9},{9,5},{13,1},{2,14},{6,10},... | collective-permute-start | bytes 49160 | tf_op jit(solution)/shard_map/ppermute | solution.py:47
  16.9 0.5 %collective-permute-start.7 = (f32[16,256]{1,0:T(8,128)S(1)}, f32[16,256]{1,0:T(8,128)S(1)}, u32[]{:S(2)}, u32[]{:S(2)}) collective-permute-start(f32[16,256]{1,0:T(8,128)S(1)} %get-tuple-element.39.refs_0_), channel_id=1, source_target_pairs={{0,8},{4,12},{8,0},{12,4},{1,9},{5,13},{9,1},{13,5},{2,10},{6,14},... | collective-permute-start | bytes 49160 | tf_op jit(solution)/shard_map/ppermute | solution.py:47
  17.4 0.0 collective-permute-done.5.refs_7_
  17.5 0.1 collective-permute-start.6
  17.6 0.0 collective-permute-done.4.refs_6_
  17.6 0.0 collective-permute-done.3.refs_5_
  17.6 0.0 copy-done.2
  17.6 0.3 turn.1
  17.9 1.2 %dprod.1._.dprod_ref = f32[2,1024,1024]{2,1,0:T(8,128)S(1)} custom-call(bf16[1024,256]{1,0:T(8,128)(2,1)S(1)} %get-tuple-element.34.val_ref, bf16[256,1024]{1,0:T(8,128)(2,1)S(1)} %get-tuple-element.38.gt_ref), custom_call_target="tpu_custom_call" | custom-call | flops 2200000000 | bytes 65536 | tf_op jit(solution)/shard_map/dprod/pallas_call | solution.py:392
  19.2 0.0 collective-permute-done.8.refs_3_
  19.2 1.5 %collective-permute-done.7.refs_2_ = f32[16,256]{1,0:T(8,128)S(1)} collective-permute-done((f32[16,256]{1,0:T(8,128)S(1)}, f32[16,256]{1,0:T(8,128)S(1)}, u32[]{:S(2)}, u32[]{:S(2)}) %collective-permute-start.7) | collective-permute-done | bytes 16416 | tf_op jit(solution)/shard_map/ppermute | solution.py:47
  20.7 0.5 %collective-permute-done.6.refs_1_ = f32[16,256]{1,0:T(8,128)S(1)} collective-permute-done((f32[16,256]{1,0:T(8,128)S(1)}, f32[16,256]{1,0:T(8,128)S(1)}, u32[]{:S(2)}, u32[]{:S(2)}) %collective-permute-start.6) | collective-permute-done | bytes 16416 | tf_op jit(solution)/shard_map/ppermute | solution.py:47
  21.2 2.4 %sums.1 = (f32[16,256]{1,0:T(8,128)S(1)}, f32[256,1024]{1,0:T(8,128)S(1)}, f32[2,1024,1024]{2,1,0:T(8,128)S(1)}) custom-call(f32[2]{0:T(128)S(1)} %copy-done, bf16[1024,256]{1,0:T(8,128)(2,1)S(1)} %get-tuple-element.34.val_ref, f32[2,1024,1024]{2,1,0:T(8,128)S(1)} %get-tuple-element.36.score_ref, bf16[256,1024]{1,0:T(8,128)(2,1)S(1)} %get-tuple-element.38.gt_ref, ...), custom_call_target="tpu_custom_call" | custom-call | flops 2200000000 | bytes 65536 | tf_op jit(solution)/shard_map/sums/pallas_call | solution.py:392
  23.6 1.6 %collective-permute-start.11 = (f32[16,256]{1,0:T(8,128)S(1)}, f32[16,256]{1,0:T(8,128)S(1)}, u32[]{:S(2)}, u32[]{:S(2)}) collective-permute-start(f32[16,256]{1,0:T(8,128)S(1)} %get-tuple-element.42.refs_4_.refs_3_.refs_0_), channel_id=1, source_target_pairs={{0,12},{4,8},{8,4},{12,0},{1,13},{5,9},{9,5},{13,1},{2,14},{6,10},... | collective-permute-start | bytes 49160 | tf_op jit(solution)/shard_map/ppermute | solution.py:47
  25.2 0.1 collective-permute-start.10
  25.3 1.9 %collective-permute-start.9 = (f32[16,256]{1,0:T(8,128)S(1)}, f32[16,256]{1,0:T(8,128)S(1)}, u32[]{:S(2)}, u32[]{:S(2)}) collective-permute-start(f32[16,256]{1,0:T(8,128)S(1)} %get-tuple-element.42.refs_4_.refs_3_.refs_0_), channel_id=1, source_target_pairs={{0,4},{4,0},{8,12},{12,8},{1,5},{5,1},{9,13},{13,9},{2,6},{6,2},{1... | collective-permute-start | bytes 49160 | tf_op jit(solution)/shard_map/ppermute | solution.py:47
  27.2 1.1 %collective-permute-done.11.refs_7_.refs_6_.refs_3_ = f32[16,256]{1,0:T(8,128)S(1)} collective-permute-done((f32[16,256]{1,0:T(8,128)S(1)}, f32[16,256]{1,0:T(8,128)S(1)}, u32[]{:S(2)}, u32[]{:S(2)}) %collective-permute-start.11) | collective-permute-done | bytes 16416 | tf_op jit(solution)/shard_map/ppermute | solution.py:47
  28.3 0.6 %collective-permute-done.10.refs_6_.refs_5_.refs_2_ = f32[16,256]{1,0:T(8,128)S(1)} collective-permute-done((f32[16,256]{1,0:T(8,128)S(1)}, f32[16,256]{1,0:T(8,128)S(1)}, u32[]{:S(2)}, u32[]{:S(2)}) %collective-permute-start.10) | collective-permute-done | bytes 16416 | tf_op jit(solution)/shard_map/ppermute | solution.py:47
  28.9 0.1 collective-permute-done.9.refs_5_.refs_4_.refs_1_
  29.0 2.9 %rows.1 = (f32[256,256]{1,0:T(8,128)S(1)}, bf16[2,1024,1024]{2,1,0:T(8,128)(2,1)S(1)}, f32[8,512]{1,0:T(8,128)S(1)}, s16[528,256]{1,0:T(8,128)(2,1)S(1)}, s16[52...) custom-call(s32[1,8]{1,0:T(1,128)S(1)} %copy-done.1, f32[2]{0:T(128)S(1)} %copy-done, ...), custom_call_target="tpu_custom_call" | custom-call | flops 3300000000 | bytes 65536 | tf_op jit(solution)/shard_map/rows/pallas_call | solution.py:392
  31.9 2.0 %collective-permute-start.12 = (s16[528,256]{1,0:T(8,128)(2,1)S(1)}, s16[528,256]{1,0:T(8,128)(2,1)S(1)}, u32[]{:S(2)}, u32[]{:S(2)}) collective-permute-start(s16[528,256]{1,0:T(8,128)(2,1)S(1)} %get-tuple-element.44), channel_id=1, source_target_pairs={{0,4},{4,0},{8,12},{12,8},{1,5},{5,1},{9,13},{13,9},{2,6},{6,2},{1... | collective-permute-start | bytes 811016 | tf_op jit(solution)/shard_map/ppermute | solution.py:47
  33.9 1.5 %collective-permute-start.13 = (s16[528,256]{1,0:T(8,128)(2,1)S(1)}, s16[528,256]{1,0:T(8,128)(2,1)S(1)}, u32[]{:S(2)}, u32[]{:S(2)}) collective-permute-start(s16[528,256]{1,0:T(8,128)(2,1)S(1)} %get-tuple-element.45), channel_id=1, source_target_pairs={{0,8},{4,12},{8,0},{12,4},{1,9},{5,13},{9,1},{13,5},{2,10},{6,14},... | collective-permute-start | bytes 811016 | tf_op jit(solution)/shard_map/ppermute | solution.py:47
  35.4 0.1 collective-permute-start.14
  35.5 2.6 %tokens.1.tok_ref = bf16[512,1024]{1,0:T(8,128)(2,1)S(1)} custom-call(f32[2,1024,1024]{2,1,0:T(8,128)S(1)} %get-tuple-element.41.expo_ref, bf16[2,1024,1024]{2,1,0:T(8,128)(2,1)S(1)} %get-tuple-element.50.grad_ref, bf16[256,1024]{1,0:T(8,128)(2,1)S(1)} %get-tuple-element.51.qt_ref, bf16[256,1024]{1,0:T(8,128)(2,1)S(1)} %get-tuple-element.38.gt_ref, ...), custom_call_target="tpu_custom_call" | custom-call | flops 3300000000 | bytes 65536 | tf_op jit(solution)/shard_map/tokens/pallas_call | solution.py:392
  38.1 1.0 %weights.1 = (f32[256,512]{1,0:T(8,128)S(1)}, s16[80,512]{1,0:T(8,128)(2,1)S(1)}, s16[192,512]{1,0:T(8,128)(2,1)S(1)}) custom-call(bf16[1024,512]{1,0:T(8,128)(2,1)S(1)} %get-tuple-element.49.inp_ref, bf16[512,1024]{1,0:T(8,128)(2,1)S(1)} %tokens.1.tok_ref, f32[8,512]{1,0:T(8,128)S(1)} %get-tuple-element.52.slope_ref), custom_call_target="tpu_custom_call" | custom-call | flops 1100000000 | bytes 65536 | tf_op jit(solution)/shard_map/weights/pallas_call | solution.py:392
  39.1 0.1 collective-permute-start.16
  39.1 0.5 collective-permute-start.15
  39.6 1.0 %collective-permute-done.15.refs_0_ = s16[80,512]{1,0:T(8,128)(2,1)S(1)} collective-permute-done((s16[80,512]{1,0:T(8,128)(2,1)S(1)}, s16[80,512]{1,0:T(8,128)(2,1)S(1)}, u32[]{:S(2)}, u32[]{:S(2)}) %collective-permute-start.15) | collective-permute-done | bytes 81952 | tf_op jit(solution)/shard_map/ppermute | solution.py:47
  40.7 0.0 collective-permute-done.16.refs_1_
  40.7 0.0 collective-permute-done.12.refs_0_.refs_2_
  40.7 0.2 pair.1
  40.9 2.0 %collective-permute-start.17 = (s16[144,256]{1,0:T(8,128)(2,1)S(1)}, s16[144,256]{1,0:T(8,128)(2,1)S(1)}, u32[]{:S(2)}, u32[]{:S(2)}) collective-permute-start(s16[144,256]{1,0:T(8,128)(2,1)S(1)} %get-tuple-element.57), channel_id=1, source_target_pairs={{0,4},{4,0},{8,12},{12,8},{1,5},{5,1},{9,13},{13,9},{2,6},{6,2},{1... | collective-permute-start | bytes 221192 | tf_op jit(solution)/shard_map/ppermute | solution.py:47
  42.9 1.5 %collective-permute-start.18 = (s16[144,256]{1,0:T(8,128)(2,1)S(1)}, s16[144,256]{1,0:T(8,128)(2,1)S(1)}, u32[]{:S(2)}, u32[]{:S(2)}) collective-permute-start(s16[144,256]{1,0:T(8,128)(2,1)S(1)} %get-tuple-element.58), channel_id=1, source_target_pairs={{0,8},{4,12},{8,0},{12,4},{1,9},{5,13},{9,1},{13,5},{2,10},{6,14},... | collective-permute-start | bytes 221192 | tf_op jit(solution)/shard_map/ppermute | solution.py:47
  44.4 0.1 collective-permute-start.19
  44.5 0.0 collective-permute-done.13.refs_1_
  44.5 0.0 collective-permute-done.14.refs_2_
  44.5 1.0 %latents.1 = (bf16[1,256,256]{2,1,0:T(8,128)(2,1)}, bf16[1,256,256]{2,1,0:T(8,128)(2,1)}) custom-call(f32[256,1024]{1,0:T(8,128)S(1)} %get-tuple-element.40.out_ref, f32[256,256]{1,0:T(8,128)S(1)} %get-tuple-element.43.own_ref, s16[528,256]{1,0:T(8,128)(2,1)S(1)} %collective-permute-done.12.refs_0_.refs_2_, ...), custom_call_target="tpu_custom_call" | custom-call | flops 1100000000 | bytes 65536 | tf_op jit(solution)/shard_map/latents/pallas_call | solution.py:392
  45.5 0.0 collective-permute-done.17.refs_0_
  45.5 1.7 %collective-permute-done.18.refs_1_ = s16[144,256]{1,0:T(8,128)(2,1)S(1)} collective-permute-done((s16[144,256]{1,0:T(8,128)(2,1)S(1)}, s16[144,256]{1,0:T(8,128)(2,1)S(1)}, u32[]{:S(2)}, u32[]{:S(2)}) %collective-permute-start.18) | collective-permute-done | bytes 73760 | tf_op jit(solution)/shard_map/ppermute | solution.py:47
  47.2 2.4 %collective-permute-done.19.refs_2_ = s16[144,256]{1,0:T(8,128)(2,1)S(1)} collective-permute-done((s16[144,256]{1,0:T(8,128)(2,1)S(1)}, s16[144,256]{1,0:T(8,128)(2,1)S(1)}, u32[]{:S(2)}, u32[]{:S(2)}) %collective-permute-start.19) | collective-permute-done | bytes 73760 | tf_op jit(solution)/shard_map/ppermute | solution.py:47
  49.6 0.7 %last.1 = (f32[64,256]{1,0:T(8,128)}, f32[64,256]{1,0:T(8,128)}, f32[2]{0:T(128)}) custom-call(f32[72,512]{1,0:T(8,128)S(1)} %get-tuple-element.56.weight_ref, s16[144,256]{1,0:T(8,128)(2,1)S(1)} %collective-permute-done.17.refs_0_, s16[144,256]{1,0:T(8,128)(2,1)S(1)} %collective-permute-done.18.refs_1_, s16[144,256]{1,0:T(8,128)(2,1)S(1)} %collective-permute-done.19.refs_2_), custom_call_target="tpu_custom_call" | custom-call | flops 1100000000 | bytes 65536 | tf_op jit(solution)/shard_map/last/pallas_call | solution.py:392
Async XLA Ops:
  0.6 11.5 %copy-start.3 = (bf16[1,256,256]{2,1,0:T(8,128)(2,1)S(1)}, bf16[1,256,256]{2,1,0:T(8,128)(2,1)}, u32[]{:S(2)}) copy-start(bf16[1,256,256]{2,1,0:T(8,128)(2,1)} %refs_0_.3) | copy-start | bytes 393220
  0.6 17.0 %copy-start.2 = (bf16[1,256,256]{2,1,0:T(8,128)(2,1)S(1)}, bf16[1,256,256]{2,1,0:T(8,128)(2,1)}, u32[]{:S(2)}) copy-start(bf16[1,256,256]{2,1,0:T(8,128)(2,1)} %refs_4_.1) | copy-start | bytes 393220
  0.7 11.5 %copy-start = (f32[2]{0:T(128)S(1)}, f32[2]{0:T(128)}, u32[]{:S(2)}) copy-start(f32[2]{0:T(128)} %slopes_ref.5) | copy-start | bytes 28
  0.7 11.5 %copy-start.1 = (s32[1,8]{1,0:T(1,128)S(1)}, s32[1,8]{1,0:T(1,128)}, u32[]{:S(2)}) copy-start(s32[1,8]{1,0:T(1,128)} %bounds_ref.3) | copy-start | bytes 100
  0.7 11.3 %collective-permute-start.2 = (bf16[1,256,256]{2,1,0:T(8,128)(2,1)}, bf16[1,256,256]{2,1,0:T(8,128)(2,1)S(1)}, u32[]{:S(2)}, u32[]{:S(2)}) collective-permute-start(bf16[1,256,256]{2,1,0:T(8,128)(2,1)} %refs_0_.3), channel_id=1, source_target_pairs={{0,12},{4,8},{8,4},{12,0},{1,13},{5,9},{9,5},{13,1},{2,14},{6,10},... | collective-permute-start | bytes 393224 | tf_op jit(solution)/shard_map/ppermute | solution.py:47
  4.6 7.5 %collective-permute-start.1 = (bf16[1,256,256]{2,1,0:T(8,128)(2,1)}, bf16[1,256,256]{2,1,0:T(8,128)(2,1)S(1)}, u32[]{:S(2)}, u32[]{:S(2)}) collective-permute-start(bf16[1,256,256]{2,1,0:T(8,128)(2,1)} %refs_0_.3), channel_id=1, source_target_pairs={{0,8},{4,12},{8,0},{12,4},{1,9},{5,13},{9,1},{13,5},{2,10},{6,14},... | collective-permute-start | bytes 393224 | tf_op jit(solution)/shard_map/ppermute | solution.py:47
  5.1 7.0 %collective-permute-start = (bf16[1,256,256]{2,1,0:T(8,128)(2,1)}, bf16[1,256,256]{2,1,0:T(8,128)(2,1)S(1)}, u32[]{:S(2)}, u32[]{:S(2)}) collective-permute-start(bf16[1,256,256]{2,1,0:T(8,128)(2,1)} %refs_0_.3), channel_id=1, source_target_pairs={{0,4},{4,0},{8,12},{12,8},{1,5},{5,1},{9,13},{13,9},{2,6},{6,2},{1... | collective-permute-start | bytes 393224 | tf_op jit(solution)/shard_map/ppermute | solution.py:47
  8.6 8.9 %collective-permute-start.5 = (bf16[1,256,256]{2,1,0:T(8,128)(2,1)S(1)}, bf16[1,256,256]{2,1,0:T(8,128)(2,1)S(1)}, u32[]{:S(2)}, u32[]{:S(2)}) collective-permute-start(bf16[1,256,256]{2,1,0:T(8,128)(2,1)S(1)} %get-tuple-element.37), channel_id=1, source_target_pairs={{0,12},{4,8},{8,4},{12,0},{1,13},{5,9},{9,5},{13,1},{2,14},{6,10},... | collective-permute-start | bytes 393224 | tf_op jit(solution)/shard_map/ppermute | solution.py:47
  11.5 6.1 %collective-permute-start.4 = (bf16[1,256,256]{2,1,0:T(8,128)(2,1)S(1)}, bf16[1,256,256]{2,1,0:T(8,128)(2,1)S(1)}, u32[]{:S(2)}, u32[]{:S(2)}) collective-permute-start(bf16[1,256,256]{2,1,0:T(8,128)(2,1)S(1)} %get-tuple-element.37), channel_id=1, source_target_pairs={{0,8},{4,12},{8,0},{12,4},{1,9},{5,13},{9,1},{13,5},{2,10},{6,14},... | collective-permute-start | bytes 393224 | tf_op jit(solution)/shard_map/ppermute | solution.py:47
  12.0 5.6 %collective-permute-start.3 = (bf16[1,256,256]{2,1,0:T(8,128)(2,1)S(1)}, bf16[1,256,256]{2,1,0:T(8,128)(2,1)S(1)}, u32[]{:S(2)}, u32[]{:S(2)}) collective-permute-start(bf16[1,256,256]{2,1,0:T(8,128)(2,1)S(1)} %get-tuple-element.37), channel_id=1, source_target_pairs={{0,4},{4,0},{8,12},{12,8},{1,5},{5,1},{9,13},{13,9},{2,6},{6,2},{1... | collective-permute-start | bytes 393224 | tf_op jit(solution)/shard_map/ppermute | solution.py:47
  14.0 5.2 %collective-permute-start.8 = (f32[16,256]{1,0:T(8,128)S(1)}, f32[16,256]{1,0:T(8,128)S(1)}, u32[]{:S(2)}, u32[]{:S(2)}) collective-permute-start(f32[16,256]{1,0:T(8,128)S(1)} %get-tuple-element.39.refs_0_), channel_id=1, source_target_pairs={{0,12},{4,8},{8,4},{12,0},{1,13},{5,9},{9,5},{13,1},{2,14},{6,10},... | collective-permute-start | bytes 49160 | tf_op jit(solution)/shard_map/ppermute | solution.py:47
  16.9 3.7 %collective-permute-start.7 = (f32[16,256]{1,0:T(8,128)S(1)}, f32[16,256]{1,0:T(8,128)S(1)}, u32[]{:S(2)}, u32[]{:S(2)}) collective-permute-start(f32[16,256]{1,0:T(8,128)S(1)} %get-tuple-element.39.refs_0_), channel_id=1, source_target_pairs={{0,8},{4,12},{8,0},{12,4},{1,9},{5,13},{9,1},{13,5},{2,10},{6,14},... | collective-permute-start | bytes 49160 | tf_op jit(solution)/shard_map/ppermute | solution.py:47
  17.5 3.7 %collective-permute-start.6 = (f32[16,256]{1,0:T(8,128)S(1)}, f32[16,256]{1,0:T(8,128)S(1)}, u32[]{:S(2)}, u32[]{:S(2)}) collective-permute-start(f32[16,256]{1,0:T(8,128)S(1)} %get-tuple-element.39.refs_0_), channel_id=1, source_target_pairs={{0,4},{4,0},{8,12},{12,8},{1,5},{5,1},{9,13},{13,9},{2,6},{6,2},{1... | collective-permute-start | bytes 49160 | tf_op jit(solution)/shard_map/ppermute | solution.py:47
  23.6 4.7 %collective-permute-start.11 = (f32[16,256]{1,0:T(8,128)S(1)}, f32[16,256]{1,0:T(8,128)S(1)}, u32[]{:S(2)}, u32[]{:S(2)}) collective-permute-start(f32[16,256]{1,0:T(8,128)S(1)} %get-tuple-element.42.refs_4_.refs_3_.refs_0_), channel_id=1, source_target_pairs={{0,12},{4,8},{8,4},{12,0},{1,13},{5,9},{9,5},{13,1},{2,14},{6,10},... | collective-permute-start | bytes 49160 | tf_op jit(solution)/shard_map/ppermute | solution.py:47
  25.2 3.7 %collective-permute-start.10 = (f32[16,256]{1,0:T(8,128)S(1)}, f32[16,256]{1,0:T(8,128)S(1)}, u32[]{:S(2)}, u32[]{:S(2)}) collective-permute-start(f32[16,256]{1,0:T(8,128)S(1)} %get-tuple-element.42.refs_4_.refs_3_.refs_0_), channel_id=1, source_target_pairs={{0,8},{4,12},{8,0},{12,4},{1,9},{5,13},{9,1},{13,5},{2,10},{6,14},... | collective-permute-start | bytes 49160 | tf_op jit(solution)/shard_map/ppermute | solution.py:47
  25.3 3.7 %collective-permute-start.9 = (f32[16,256]{1,0:T(8,128)S(1)}, f32[16,256]{1,0:T(8,128)S(1)}, u32[]{:S(2)}, u32[]{:S(2)}) collective-permute-start(f32[16,256]{1,0:T(8,128)S(1)} %get-tuple-element.42.refs_4_.refs_3_.refs_0_), channel_id=1, source_target_pairs={{0,4},{4,0},{8,12},{12,8},{1,5},{5,1},{9,13},{13,9},{2,6},{6,2},{1... | collective-permute-start | bytes 49160 | tf_op jit(solution)/shard_map/ppermute | solution.py:47
  31.9 8.8 %collective-permute-start.12 = (s16[528,256]{1,0:T(8,128)(2,1)S(1)}, s16[528,256]{1,0:T(8,128)(2,1)S(1)}, u32[]{:S(2)}, u32[]{:S(2)}) collective-permute-start(s16[528,256]{1,0:T(8,128)(2,1)S(1)} %get-tuple-element.44), channel_id=1, source_target_pairs={{0,4},{4,0},{8,12},{12,8},{1,5},{5,1},{9,13},{13,9},{2,6},{6,2},{1... | collective-permute-start | bytes 811016 | tf_op jit(solution)/shard_map/ppermute | solution.py:47
  33.9 10.6 %collective-permute-start.13 = (s16[528,256]{1,0:T(8,128)(2,1)S(1)}, s16[528,256]{1,0:T(8,128)(2,1)S(1)}, u32[]{:S(2)}, u32[]{:S(2)}) collective-permute-start(s16[528,256]{1,0:T(8,128)(2,1)S(1)} %get-tuple-element.45), channel_id=1, source_target_pairs={{0,8},{4,12},{8,0},{12,4},{1,9},{5,13},{9,1},{13,5},{2,10},{6,14},... | collective-permute-start | bytes 811016 | tf_op jit(solution)/shard_map/ppermute | solution.py:47
  35.4 9.1 %collective-permute-start.14 = (s16[528,256]{1,0:T(8,128)(2,1)S(1)}, s16[528,256]{1,0:T(8,128)(2,1)S(1)}, u32[]{:S(2)}, u32[]{:S(2)}) collective-permute-start(s16[528,256]{1,0:T(8,128)(2,1)S(1)} %get-tuple-element.46), channel_id=1, source_target_pairs={{0,12},{4,8},{8,4},{12,0},{1,13},{5,9},{9,5},{13,1},{2,14},{6,10},... | collective-permute-start | bytes 811016 | tf_op jit(solution)/shard_map/ppermute | solution.py:47
  39.1 1.6 %collective-permute-start.16 = (s16[192,512]{1,0:T(8,128)(2,1)S(1)}, s16[192,512]{1,0:T(8,128)(2,1)S(1)}, u32[]{:S(2)}, u32[]{:S(2)}) collective-permute-start(s16[192,512]{1,0:T(8,128)(2,1)S(1)} %get-tuple-element.55), channel_id=1, source_target_pairs={{0,16},{16,0},{1,17},{17,1},{2,18},{18,2},{3,19},{19,3},{4,20},{20... | collective-permute-start | bytes 589832 | tf_op jit(solution)/shard_map/ppermute | solution.py:47
  39.1 1.5 %collective-permute-start.15 = (s16[80,512]{1,0:T(8,128)(2,1)S(1)}, s16[80,512]{1,0:T(8,128)(2,1)S(1)}, u32[]{:S(2)}, u32[]{:S(2)}) collective-permute-start(s16[80,512]{1,0:T(8,128)(2,1)S(1)} %get-tuple-element.54), channel_id=1, source_target_pairs={{0,16},{16,0},{1,17},{17,1},{2,18},{18,2},{3,19},{19,3},{4,20},{20... | collective-permute-start | bytes 245768 | tf_op jit(solution)/shard_map/ppermute | solution.py:47
  40.9 4.6 %collective-permute-start.17 = (s16[144,256]{1,0:T(8,128)(2,1)S(1)}, s16[144,256]{1,0:T(8,128)(2,1)S(1)}, u32[]{:S(2)}, u32[]{:S(2)}) collective-permute-start(s16[144,256]{1,0:T(8,128)(2,1)S(1)} %get-tuple-element.57), channel_id=1, source_target_pairs={{0,4},{4,0},{8,12},{12,8},{1,5},{5,1},{9,13},{13,9},{2,6},{6,2},{1... | collective-permute-start | bytes 221192 | tf_op jit(solution)/shard_map/ppermute | solution.py:47
  42.9 4.4 %collective-permute-start.18 = (s16[144,256]{1,0:T(8,128)(2,1)S(1)}, s16[144,256]{1,0:T(8,128)(2,1)S(1)}, u32[]{:S(2)}, u32[]{:S(2)}) collective-permute-start(s16[144,256]{1,0:T(8,128)(2,1)S(1)} %get-tuple-element.58), channel_id=1, source_target_pairs={{0,8},{4,12},{8,0},{12,4},{1,9},{5,13},{9,1},{13,5},{2,10},{6,14},... | collective-permute-start | bytes 221192 | tf_op jit(solution)/shard_map/ppermute | solution.py:47
  44.4 5.3 %collective-permute-start.19 = (s16[144,256]{1,0:T(8,128)(2,1)S(1)}, s16[144,256]{1,0:T(8,128)(2,1)S(1)}, u32[]{:S(2)}, u32[]{:S(2)}) collective-permute-start(s16[144,256]{1,0:T(8,128)(2,1)S(1)} %get-tuple-element.59), channel_id=1, source_target_pairs={{0,12},{4,8},{8,4},{12,0},{1,13},{5,9},{9,5},{13,1},{2,14},{6,10},... | collective-permute-start | bytes 221192 | tf_op jit(solution)/shard_map/ppermute | solution.py:47

commit v6 on v5

--- a/solution.py
+++ b/solution.py
@@ -250,7 +250,14 @@
     return norms, deltas
 
 
-def rows_kernel(n, bounds_ref, slopes_ref, key_ref, expo_ref, dprod_ref, out_ref, *refs):
+def pack_kernel(n, out_ref, *send_refs):
+    rows = out_ref.shape[1] // n
+    for h in range(out_ref.shape[0] // HEAD):
+        write_messages(h, rows, out_ref[head_cols(h), :], send_refs)
+
+
+def rows_kernel(n, bounds_ref, slopes_ref, key_ref, expo_ref, dprod_ref, *refs):
+    packed_refs, refs = refs[: n - 1], refs[n - 1 :]
     top_refs, sum_refs, refs = refs[:n], refs[n : 2 * n], refs[2 * n :]
     own_ref, grad_ref, slope_ref = refs[:3]
     send_refs = refs[3 : n + 2]
@@ -277,8 +284,12 @@
             term = tn(key_ref[part, head_cols(h)], score_grad_b)
             dq = term if dq is None else dq + term
         own_ref[head_cols(h), :] = dq[:, :rows]
-        write_messages(2 * h, rows, dq, send_refs)
-        write_messages(2 * h + 1, rows, out_ref[head_cols(h), :], send_refs)
+        if h == 0:
+            for ref, packed_ref in zip(send_refs, packed_refs):
+                full = packed_ref.shape[0] - 16
+                ref[:full, :] = packed_ref[:full, :]
+                ref[2 * full :, :] = packed_ref[full:, :]
+        write_messages(heads + h, rows, dq, send_refs)
         total = jnp.sum(slope, axis=1, keepdims=True)
         slope_ref[:, h * 2 * HEAD : (h + 1) * 2 * HEAD] = jnp.broadcast_to(total, (8, 2 * HEAD))
 
@@ -363,8 +374,8 @@
         total = out_ref[head_cols(h), :rows]
         grad = own_ref[head_cols(h), :]
         for ref in got_refs:
-            grad = grad + read_message(ref, 2 * h)
-            total = total + read_message(ref, 2 * h + 1)
+            grad = grad + read_message(ref, heads + h)
+            total = total + read_message(ref, h)
         total = total / norms[h][:, :rows]
         att_ref[0, :, head_cols(h)] = total.T.astype(BF16)
         grad_ref[0, :, head_cols(h)] = (SCALE * grad).T.astype(BF16)
@@ -451,12 +462,15 @@
         limit=LIM_S << 20,
     )
     norms = [sums[0]] + [swap(sums[0], "seq", k, n) for k in peers]
+    packed = call(
+        functools.partial(pack_kernel, n), "pack", [((width + 16, rows), I16)] * (n - 1), (sums[1],), 0.5
+    )
     own_dq, score_grads, slope_terms, *sends = call(
         functools.partial(rows_kernel, n),
         "rows",
         [((width, rows), F32), ((heads, toks, lats), BF16), ((8, 2 * width), F32)]
         + [block] * (n - 1),
-        (boundaries, slopes, keys, sums[2], dprod, sums[1], *tops, *norms),
+        (boundaries, slopes, keys, sums[2], dprod, *packed, *tops, *norms),
         3,
         [pltpu.VMEM((toks, 128), F32)],
         2,

time: 50.5 us -> 50.5 us (level)
    pallas_call x11 -> x12, Pallas kernels: 17.6 us -> 17.7 us  [call(): pl.pallas_call(kernel, out_shape=[jax.ShapeDtypeStruct(shape, dtype) for...]
where the time goes in v6:
time: 50.5 us; the launch traced here: 50.3 us
  starting transfers between devices  22.9 us (45%)
  Pallas kernels  17.7 us (35%)
  waiting for transfers between devices  8.85 us (18%)
  between operations  0.79 us (2%)
    ppermute x20, starting transfers between devices, swap(): return lax.ppermute(x, axis, [(i, i ^ k) for i in range(n)])  22.9 us
    pallas_call x12, Pallas kernels, call(): pl.pallas_call(kernel, out_shape=[jax.ShapeDtypeStruct(shape, dtype) for...  17.7 us
    ppermute x20, waiting for transfers between devices, swap(): return lax.ppermute(x, axis, [(i, i ^ k) for i in range(n)])  8.85 us
  transfers between devices with their start and end apart: 20, of which 8 were waited for; matrix products, arithmetic and copies ran while one was open for 0% of the time, Pallas kernels for 23%

profile of v6, /device:TPU:0, one launch (start us, length us, event | category | flops | bytes accessed | tf_op | source)
XLA Modules:
  0.0 50.3 jit_solution(15837039792826709747)
XLA Ops:
  0.6 0.0 copy-start.3
  0.6 0.0 copy-start.2
  0.7 0.0 copy-start
  0.7 0.0 copy-start.1
  0.7 4.0 %collective-permute-start.2 = (bf16[1,256,256]{2,1,0:T(8,128)(2,1)}, bf16[1,256,256]{2,1,0:T(8,128)(2,1)S(1)}, u32[]{:S(2)}, u32[]{:S(2)}) collective-permute-start(bf16[1,256,256]{2,1,0:T(8,128)(2,1)} %refs_0_.3), channel_id=1, source_target_pairs={{0,12},{4,8},{8,4},{12,0},{1,13},{5,9},{9,5},{13,1},{2,14},{6,10},... | collective-permute-start | bytes 393224 | tf_op jit(solution)/shard_map/ppermute | solution.py:47
  4.6 0.5 %collective-permute-start.1 = (bf16[1,256,256]{2,1,0:T(8,128)(2,1)}, bf16[1,256,256]{2,1,0:T(8,128)(2,1)S(1)}, u32[]{:S(2)}, u32[]{:S(2)}) collective-permute-start(bf16[1,256,256]{2,1,0:T(8,128)(2,1)} %refs_0_.3), channel_id=1, source_target_pairs={{0,8},{4,12},{8,0},{12,4},{1,9},{5,13},{9,1},{13,5},{2,10},{6,14},... | collective-permute-start | bytes 393224 | tf_op jit(solution)/shard_map/ppermute | solution.py:47
  5.1 0.1 collective-permute-start
  5.3 3.3 %prep.1 = (bf16[1024,512]{1,0:T(8,128)(2,1)S(1)}, bf16[1024,256]{1,0:T(8,128)(2,1)S(1)}, bf16[1024,256]{1,0:T(8,128)(2,1)S(1)}, bf16[1,256,256]{2,1,0:T(8,128)(2,1)S(1)}) custom-call(bf16[1,1024,512]{2,1,0:T(8,128)(2,1)} %tok_hbm.1, s32[1,1024]{1,0:T(1,128)} %lev_hbm.1, f32[256,512]{1,0:T(8,128)} %table_hbm.1, bf16[512,256]{1,0:T(8,128)(2,1)} %wk_hbm.1, ...), custom_call_target="tpu_custom_call" | custom-call | flops 3300000000 | bytes 65536 | tf_op jit(solution)/shard_map/prep/pallas_call | solution.py:403
  8.6 2.9 %collective-permute-start.5 = (bf16[1,256,256]{2,1,0:T(8,128)(2,1)S(1)}, bf16[1,256,256]{2,1,0:T(8,128)(2,1)S(1)}, u32[]{:S(2)}, u32[]{:S(2)}) collective-permute-start(bf16[1,256,256]{2,1,0:T(8,128)(2,1)S(1)} %get-tuple-element.40), channel_id=1, source_target_pairs={{0,12},{4,8},{8,4},{12,0},{1,13},{5,9},{9,5},{13,1},{2,14},{6,10},... | collective-permute-start | bytes 393224 | tf_op jit(solution)/shard_map/ppermute | solution.py:47
  11.5 0.5 %collective-permute-start.4 = (bf16[1,256,256]{2,1,0:T(8,128)(2,1)S(1)}, bf16[1,256,256]{2,1,0:T(8,128)(2,1)S(1)}, u32[]{:S(2)}, u32[]{:S(2)}) collective-permute-start(bf16[1,256,256]{2,1,0:T(8,128)(2,1)S(1)} %get-tuple-element.40), channel_id=1, source_target_pairs={{0,8},{4,12},{8,0},{12,4},{1,9},{5,13},{9,1},{13,5},{2,10},{6,14},... | collective-permute-start | bytes 393224 | tf_op jit(solution)/shard_map/ppermute | solution.py:47
  12.0 0.0 collective-permute-done.2.refs_3_
  12.0 0.1 collective-permute-start.3
  12.1 0.0 collective-permute-done.1.refs_2_
  12.1 0.0 collective-permute-done.refs_1_
  12.1 0.0 copy-done.3
  12.1 0.0 copy-done
  12.1 0.0 copy-done.1
  12.2 1.9 %tops.1 = (f32[16,256]{1,0:T(8,128)S(1)}, f32[2,1024,1024]{2,1,0:T(8,128)S(1)}) custom-call(s32[1,8]{1,0:T(1,128)S(1)} %copy-done.1, f32[2]{0:T(128)S(1)} %copy-done, bf16[1024,256]{1,0:T(8,128)(2,1)S(1)} %get-tuple-element.38.key_ref, bf16[1,256,256]{2,1,0:T(8,128)(2,1)S(1)} %copy-done.3, bf16[1,256,256]{2,1,0:T(8,128)(2,1)S(1)} %collective-permute-done.refs_1_, ...), custom_call_target="tpu_custom_call" | custom-call | flops 2200000000 | bytes 65536 | tf_op jit(solution)/shard_map/tops/pallas_call | solution.py:403
  14.0 2.9 %collective-permute-start.8 = (f32[16,256]{1,0:T(8,128)S(1)}, f32[16,256]{1,0:T(8,128)S(1)}, u32[]{:S(2)}, u32[]{:S(2)}) collective-permute-start(f32[16,256]{1,0:T(8,128)S(1)} %get-tuple-element.42.refs_0_.refs_3_), channel_id=1, source_target_pairs={{0,12},{4,8},{8,4},{12,0},{1,13},{5,9},{9,5},{13,1},{2,14},{6,10},... | collective-permute-start | bytes 49160 | tf_op jit(solution)/shard_map/ppermute | solution.py:47
  16.9 0.5 %collective-permute-start.7 = (f32[16,256]{1,0:T(8,128)S(1)}, f32[16,256]{1,0:T(8,128)S(1)}, u32[]{:S(2)}, u32[]{:S(2)}) collective-permute-start(f32[16,256]{1,0:T(8,128)S(1)} %get-tuple-element.42.refs_0_.refs_3_), channel_id=1, source_target_pairs={{0,8},{4,12},{8,0},{12,4},{1,9},{5,13},{9,1},{13,5},{2,10},{6,14},... | collective-permute-start | bytes 49160 | tf_op jit(solution)/shard_map/ppermute | solution.py:47
  17.5 0.0 collective-permute-done.5.refs_7_
  17.5 0.1 collective-permute-start.6
  17.6 0.0 collective-permute-done.4.refs_6_
  17.6 0.0 collective-permute-done.3.refs_5_
  17.6 0.0 copy-done.2
  17.6 0.3 turn.1
  17.9 1.2 %dprod.1._.dprod_ref = f32[2,1024,1024]{2,1,0:T(8,128)S(1)} custom-call(bf16[1024,256]{1,0:T(8,128)(2,1)S(1)} %get-tuple-element.37.val_ref, bf16[256,1024]{1,0:T(8,128)(2,1)S(1)} %get-tuple-element.41.gt_ref), custom_call_target="tpu_custom_call" | custom-call | flops 2200000000 | bytes 65536 | tf_op jit(solution)/shard_map/dprod/pallas_call | solution.py:403
  19.2 0.0 collective-permute-done.8.refs_3_.refs_6_
  19.2 1.5 %collective-permute-done.7.refs_2_.refs_5_ = f32[16,256]{1,0:T(8,128)S(1)} collective-permute-done((f32[16,256]{1,0:T(8,128)S(1)}, f32[16,256]{1,0:T(8,128)S(1)}, u32[]{:S(2)}, u32[]{:S(2)}) %collective-permute-start.7) | collective-permute-done | bytes 16416 | tf_op jit(solution)/shard_map/ppermute | solution.py:47
  20.7 0.5 %collective-permute-done.6.refs_1_.refs_4_ = f32[16,256]{1,0:T(8,128)S(1)} collective-permute-done((f32[16,256]{1,0:T(8,128)S(1)}, f32[16,256]{1,0:T(8,128)S(1)}, u32[]{:S(2)}, u32[]{:S(2)}) %collective-permute-start.6) | collective-permute-done | bytes 16416 | tf_op jit(solution)/shard_map/ppermute | solution.py:47
  21.2 2.4 %sums.1 = (f32[16,256]{1,0:T(8,128)S(1)}, f32[256,1024]{1,0:T(8,128)S(1)}, f32[2,1024,1024]{2,1,0:T(8,128)S(1)}) custom-call(f32[2]{0:T(128)S(1)} %copy-done, bf16[1024,256]{1,0:T(8,128)(2,1)S(1)} %get-tuple-element.37.val_ref, f32[2,1024,1024]{2,1,0:T(8,128)S(1)} %get-tuple-element.39.score_ref, bf16[256,1024]{1,0:T(8,128)(2,1)S(1)} %get-tuple-element.41.gt_ref, ...), custom_call_target="tpu_custom_call" | custom-call | flops 2200000000 | bytes 65536 | tf_op jit(solution)/shard_map/sums/pallas_call | solution.py:403
  23.6 1.5 %collective-permute-start.11 = (f32[16,256]{1,0:T(8,128)S(1)}, f32[16,256]{1,0:T(8,128)S(1)}, u32[]{:S(2)}, u32[]{:S(2)}) collective-permute-start(f32[16,256]{1,0:T(8,128)S(1)} %get-tuple-element.48.refs_7_.refs_3_.refs_0_), channel_id=1, source_target_pairs={{0,12},{4,8},{8,4},{12,0},{1,13},{5,9},{9,5},{13,1},{2,14},{6,10},... | collective-permute-start | bytes 49160 | tf_op jit(solution)/shard_map/ppermute | solution.py:47
  25.2 0.1 collective-permute-start.10
  25.3 1.9 %collective-permute-start.9 = (f32[16,256]{1,0:T(8,128)S(1)}, f32[16,256]{1,0:T(8,128)S(1)}, u32[]{:S(2)}, u32[]{:S(2)}) collective-permute-start(f32[16,256]{1,0:T(8,128)S(1)} %get-tuple-element.48.refs_7_.refs_3_.refs_0_), channel_id=1, source_target_pairs={{0,4},{4,0},{8,12},{12,8},{1,5},{5,1},{9,13},{13,9},{2,6},{6,2},{1... | collective-permute-start | bytes 49160 | tf_op jit(solution)/shard_map/ppermute | solution.py:47
  27.2 0.2 pack.1
  27.4 0.9 %collective-permute-done.11.refs_10_.refs_6_.refs_3_ = f32[16,256]{1,0:T(8,128)S(1)} collective-permute-done((f32[16,256]{1,0:T(8,128)S(1)}, f32[16,256]{1,0:T(8,128)S(1)}, u32[]{:S(2)}, u32[]{:S(2)}) %collective-permute-start.11) | collective-permute-done | bytes 16416 | tf_op jit(solution)/shard_map/ppermute | solution.py:47
  28.3 0.6 %collective-permute-done.10.refs_9_.refs_5_.refs_2_ = f32[16,256]{1,0:T(8,128)S(1)} collective-permute-done((f32[16,256]{1,0:T(8,128)S(1)}, f32[16,256]{1,0:T(8,128)S(1)}, u32[]{:S(2)}, u32[]{:S(2)}) %collective-permute-start.10) | collective-permute-done | bytes 16416 | tf_op jit(solution)/shard_map/ppermute | solution.py:47
  28.9 0.1 collective-permute-done.9.refs_8_.refs_4_.refs_1_
  29.0 2.8 %rows.1 = (f32[256,256]{1,0:T(8,128)S(1)}, bf16[2,1024,1024]{2,1,0:T(8,128)(2,1)S(1)}, f32[8,512]{1,0:T(8,128)S(1)}, s16[528,256]{1,0:T(8,128)(2,1)S(1)}, s16[52...) custom-call(s32[1,8]{1,0:T(1,128)S(1)} %copy-done.1, f32[2]{0:T(128)S(1)} %copy-done, ...), custom_call_target="tpu_custom_call" | custom-call | flops 3300000000 | bytes 65536 | tf_op jit(solution)/shard_map/rows/pallas_call | solution.py:403
  31.9 2.0 %collective-permute-start.12 = (s16[528,256]{1,0:T(8,128)(2,1)S(1)}, s16[528,256]{1,0:T(8,128)(2,1)S(1)}, u32[]{:S(2)}, u32[]{:S(2)}) collective-permute-start(s16[528,256]{1,0:T(8,128)(2,1)S(1)} %get-tuple-element.50), channel_id=1, source_target_pairs={{0,4},{4,0},{8,12},{12,8},{1,5},{5,1},{9,13},{13,9},{2,6},{6,2},{1... | collective-permute-start | bytes 811016 | tf_op jit(solution)/shard_map/ppermute | solution.py:47
  33.8 1.5 %collective-permute-start.13 = (s16[528,256]{1,0:T(8,128)(2,1)S(1)}, s16[528,256]{1,0:T(8,128)(2,1)S(1)}, u32[]{:S(2)}, u32[]{:S(2)}) collective-permute-start(s16[528,256]{1,0:T(8,128)(2,1)S(1)} %get-tuple-element.51), channel_id=1, source_target_pairs={{0,8},{4,12},{8,0},{12,4},{1,9},{5,13},{9,1},{13,5},{2,10},{6,14},... | collective-permute-start | bytes 811016 | tf_op jit(solution)/shard_map/ppermute | solution.py:47
  35.3 0.1 collective-permute-start.14
  35.4 2.6 %tokens.1.tok_ref = bf16[512,1024]{1,0:T(8,128)(2,1)S(1)} custom-call(f32[2,1024,1024]{2,1,0:T(8,128)S(1)} %get-tuple-element.44.expo_ref, bf16[2,1024,1024]{2,1,0:T(8,128)(2,1)S(1)} %get-tuple-element.56.grad_ref, bf16[256,1024]{1,0:T(8,128)(2,1)S(1)} %get-tuple-element.57.qt_ref, bf16[256,1024]{1,0:T(8,128)(2,1)S(1)} %get-tuple-element.41.gt_ref, ...), custom_call_target="tpu_custom_call" | custom-call | flops 3300000000 | bytes 65536 | tf_op jit(solution)/shard_map/tokens/pallas_call | solution.py:403
  38.0 1.0 %weights.1 = (f32[256,512]{1,0:T(8,128)S(1)}, s16[80,512]{1,0:T(8,128)(2,1)S(1)}, s16[192,512]{1,0:T(8,128)(2,1)S(1)}) custom-call(bf16[1024,512]{1,0:T(8,128)(2,1)S(1)} %get-tuple-element.55.inp_ref, bf16[512,1024]{1,0:T(8,128)(2,1)S(1)} %tokens.1.tok_ref, f32[8,512]{1,0:T(8,128)S(1)} %get-tuple-element.58.slope_ref), custom_call_target="tpu_custom_call" | custom-call | flops 1100000000 | bytes 65536 | tf_op jit(solution)/shard_map/weights/pallas_call | solution.py:403
  39.0 0.1 collective-permute-start.16
  39.1 0.5 collective-permute-start.15
  39.6 1.0 %collective-permute-done.15.refs_0_ = s16[80,512]{1,0:T(8,128)(2,1)S(1)} collective-permute-done((s16[80,512]{1,0:T(8,128)(2,1)S(1)}, s16[80,512]{1,0:T(8,128)(2,1)S(1)}, u32[]{:S(2)}, u32[]{:S(2)}) %collective-permute-start.15) | collective-permute-done | bytes 81952 | tf_op jit(solution)/shard_map/ppermute | solution.py:47
  40.6 0.0 collective-permute-done.16.refs_1_
  40.6 0.0 collective-permute-done.12.refs_0_.refs_2_
  40.6 0.2 pair.1
  40.9 2.0 %collective-permute-start.17 = (s16[144,256]{1,0:T(8,128)(2,1)S(1)}, s16[144,256]{1,0:T(8,128)(2,1)S(1)}, u32[]{:S(2)}, u32[]{:S(2)}) collective-permute-start(s16[144,256]{1,0:T(8,128)(2,1)S(1)} %get-tuple-element.63), channel_id=1, source_target_pairs={{0,4},{4,0},{8,12},{12,8},{1,5},{5,1},{9,13},{13,9},{2,6},{6,2},{1... | collective-permute-start | bytes 221192 | tf_op jit(solution)/shard_map/ppermute | solution.py:47
  42.8 1.5 %collective-permute-start.18 = (s16[144,256]{1,0:T(8,128)(2,1)S(1)}, s16[144,256]{1,0:T(8,128)(2,1)S(1)}, u32[]{:S(2)}, u32[]{:S(2)}) collective-permute-start(s16[144,256]{1,0:T(8,128)(2,1)S(1)} %get-tuple-element.64), channel_id=1, source_target_pairs={{0,8},{4,12},{8,0},{12,4},{1,9},{5,13},{9,1},{13,5},{2,10},{6,14},... | collective-permute-start | bytes 221192 | tf_op jit(solution)/shard_map/ppermute | solution.py:47
  44.3 0.1 collective-permute-start.19
  44.4 0.0 collective-permute-done.13.refs_1_
  44.4 0.0 collective-permute-done.14.refs_2_
  44.4 1.0 %latents.1 = (bf16[1,256,256]{2,1,0:T(8,128)(2,1)}, bf16[1,256,256]{2,1,0:T(8,128)(2,1)}) custom-call(f32[256,1024]{1,0:T(8,128)S(1)} %get-tuple-element.43.out_ref, f32[256,256]{1,0:T(8,128)S(1)} %get-tuple-element.49.own_ref, s16[528,256]{1,0:T(8,128)(2,1)S(1)} %collective-permute-done.12.refs_0_.refs_2_, ...), custom_call_target="tpu_custom_call" | custom-call | flops 1100000000 | bytes 65536 | tf_op jit(solution)/shard_map/latents/pallas_call | solution.py:403
  45.4 0.0 collective-permute-done.17.refs_0_
  45.5 1.7 %collective-permute-done.18.refs_1_ = s16[144,256]{1,0:T(8,128)(2,1)S(1)} collective-permute-done((s16[144,256]{1,0:T(8,128)(2,1)S(1)}, s16[144,256]{1,0:T(8,128)(2,1)S(1)}, u32[]{:S(2)}, u32[]{:S(2)}) %collective-permute-start.18) | collective-permute-done | bytes 73760 | tf_op jit(solution)/shard_map/ppermute | solution.py:47
  47.2 2.4 %collective-permute-done.19.refs_2_ = s16[144,256]{1,0:T(8,128)(2,1)S(1)} collective-permute-done((s16[144,256]{1,0:T(8,128)(2,1)S(1)}, s16[144,256]{1,0:T(8,128)(2,1)S(1)}, u32[]{:S(2)}, u32[]{:S(2)}) %collective-permute-start.19) | collective-permute-done | bytes 73760 | tf_op jit(solution)/shard_map/ppermute | solution.py:47
  49.6 0.7 %last.1 = (f32[64,256]{1,0:T(8,128)}, f32[64,256]{1,0:T(8,128)}, f32[2]{0:T(128)}) custom-call(f32[72,512]{1,0:T(8,128)S(1)} %get-tuple-element.62.weight_ref, s16[144,256]{1,0:T(8,128)(2,1)S(1)} %collective-permute-done.17.refs_0_, s16[144,256]{1,0:T(8,128)(2,1)S(1)} %collective-permute-done.18.refs_1_, s16[144,256]{1,0:T(8,128)(2,1)S(1)} %collective-permute-done.19.refs_2_), custom_call_target="tpu_custom_call" | custom-call | flops 1100000000 | bytes 65536 | tf_op jit(solution)/shard_map/last/pallas_call | solution.py:403
Async XLA Ops:
  0.6 11.5 %copy-start.3 = (bf16[1,256,256]{2,1,0:T(8,128)(2,1)S(1)}, bf16[1,256,256]{2,1,0:T(8,128)(2,1)}, u32[]{:S(2)}) copy-start(bf16[1,256,256]{2,1,0:T(8,128)(2,1)} %refs_0_.3) | copy-start | bytes 393220
  0.6 17.0 %copy-start.2 = (bf16[1,256,256]{2,1,0:T(8,128)(2,1)S(1)}, bf16[1,256,256]{2,1,0:T(8,128)(2,1)}, u32[]{:S(2)}) copy-start(bf16[1,256,256]{2,1,0:T(8,128)(2,1)} %refs_4_.1) | copy-start | bytes 393220
  0.7 11.5 %copy-start = (f32[2]{0:T(128)S(1)}, f32[2]{0:T(128)}, u32[]{:S(2)}) copy-start(f32[2]{0:T(128)} %slopes_ref.5) | copy-start | bytes 28
  0.7 11.5 %copy-start.1 = (s32[1,8]{1,0:T(1,128)S(1)}, s32[1,8]{1,0:T(1,128)}, u32[]{:S(2)}) copy-start(s32[1,8]{1,0:T(1,128)} %bounds_ref.3) | copy-start | bytes 100
  0.7 11.3 %collective-permute-start.2 = (bf16[1,256,256]{2,1,0:T(8,128)(2,1)}, bf16[1,256,256]{2,1,0:T(8,128)(2,1)S(1)}, u32[]{:S(2)}, u32[]{:S(2)}) collective-permute-start(bf16[1,256,256]{2,1,0:T(8,128)(2,1)} %refs_0_.3), channel_id=1, source_target_pairs={{0,12},{4,8},{8,4},{12,0},{1,13},{5,9},{9,5},{13,1},{2,14},{6,10},... | collective-permute-start | bytes 393224 | tf_op jit(solution)/shard_map/ppermute | solution.py:47
  4.6 7.5 %collective-permute-start.1 = (bf16[1,256,256]{2,1,0:T(8,128)(2,1)}, bf16[1,256,256]{2,1,0:T(8,128)(2,1)S(1)}, u32[]{:S(2)}, u32[]{:S(2)}) collective-permute-start(bf16[1,256,256]{2,1,0:T(8,128)(2,1)} %refs_0_.3), channel_id=1, source_target_pairs={{0,8},{4,12},{8,0},{12,4},{1,9},{5,13},{9,1},{13,5},{2,10},{6,14},... | collective-permute-start | bytes 393224 | tf_op jit(solution)/shard_map/ppermute | solution.py:47
  5.1 7.0 %collective-permute-start = (bf16[1,256,256]{2,1,0:T(8,128)(2,1)}, bf16[1,256,256]{2,1,0:T(8,128)(2,1)S(1)}, u32[]{:S(2)}, u32[]{:S(2)}) collective-permute-start(bf16[1,256,256]{2,1,0:T(8,128)(2,1)} %refs_0_.3), channel_id=1, source_target_pairs={{0,4},{4,0},{8,12},{12,8},{1,5},{5,1},{9,13},{13,9},{2,6},{6,2},{1... | collective-permute-start | bytes 393224 | tf_op jit(solution)/shard_map/ppermute | solution.py:47
  8.6 8.9 %collective-permute-start.5 = (bf16[1,256,256]{2,1,0:T(8,128)(2,1)S(1)}, bf16[1,256,256]{2,1,0:T(8,128)(2,1)S(1)}, u32[]{:S(2)}, u32[]{:S(2)}) collective-permute-start(bf16[1,256,256]{2,1,0:T(8,128)(2,1)S(1)} %get-tuple-element.40), channel_id=1, source_target_pairs={{0,12},{4,8},{8,4},{12,0},{1,13},{5,9},{9,5},{13,1},{2,14},{6,10},... | collective-permute-start | bytes 393224 | tf_op jit(solution)/shard_map/ppermute | solution.py:47
  11.5 6.1 %collective-permute-start.4 = (bf16[1,256,256]{2,1,0:T(8,128)(2,1)S(1)}, bf16[1,256,256]{2,1,0:T(8,128)(2,1)S(1)}, u32[]{:S(2)}, u32[]{:S(2)}) collective-permute-start(bf16[1,256,256]{2,1,0:T(8,128)(2,1)S(1)} %get-tuple-element.40), channel_id=1, source_target_pairs={{0,8},{4,12},{8,0},{12,4},{1,9},{5,13},{9,1},{13,5},{2,10},{6,14},... | collective-permute-start | bytes 393224 | tf_op jit(solution)/shard_map/ppermute | solution.py:47
  12.0 5.6 %collective-permute-start.3 = (bf16[1,256,256]{2,1,0:T(8,128)(2,1)S(1)}, bf16[1,256,256]{2,1,0:T(8,128)(2,1)S(1)}, u32[]{:S(2)}, u32[]{:S(2)}) collective-permute-start(bf16[1,256,256]{2,1,0:T(8,128)(2,1)S(1)} %get-tuple-element.40), channel_id=1, source_target_pairs={{0,4},{4,0},{8,12},{12,8},{1,5},{5,1},{9,13},{13,9},{2,6},{6,2},{1... | collective-permute-start | bytes 393224 | tf_op jit(solution)/shard_map/ppermute | solution.py:47
  14.0 5.2 %collective-permute-start.8 = (f32[16,256]{1,0:T(8,128)S(1)}, f32[16,256]{1,0:T(8,128)S(1)}, u32[]{:S(2)}, u32[]{:S(2)}) collective-permute-start(f32[16,256]{1,0:T(8,128)S(1)} %get-tuple-element.42.refs_0_.refs_3_), channel_id=1, source_target_pairs={{0,12},{4,8},{8,4},{12,0},{1,13},{5,9},{9,5},{13,1},{2,14},{6,10},... | collective-permute-start | bytes 49160 | tf_op jit(solution)/shard_map/ppermute | solution.py:47
  16.9 3.7 %collective-permute-start.7 = (f32[16,256]{1,0:T(8,128)S(1)}, f32[16,256]{1,0:T(8,128)S(1)}, u32[]{:S(2)}, u32[]{:S(2)}) collective-permute-start(f32[16,256]{1,0:T(8,128)S(1)} %get-tuple-element.42.refs_0_.refs_3_), channel_id=1, source_target_pairs={{0,8},{4,12},{8,0},{12,4},{1,9},{5,13},{9,1},{13,5},{2,10},{6,14},... | collective-permute-start | bytes 49160 | tf_op jit(solution)/shard_map/ppermute | solution.py:47
  17.5 3.7 %collective-permute-start.6 = (f32[16,256]{1,0:T(8,128)S(1)}, f32[16,256]{1,0:T(8,128)S(1)}, u32[]{:S(2)}, u32[]{:S(2)}) collective-permute-start(f32[16,256]{1,0:T(8,128)S(1)} %get-tuple-element.42.refs_0_.refs_3_), channel_id=1, source_target_pairs={{0,4},{4,0},{8,12},{12,8},{1,5},{5,1},{9,13},{13,9},{2,6},{6,2},{1... | collective-permute-start | bytes 49160 | tf_op jit(solution)/shard_map/ppermute | solution.py:47
  23.6 4.7 %collective-permute-start.11 = (f32[16,256]{1,0:T(8,128)S(1)}, f32[16,256]{1,0:T(8,128)S(1)}, u32[]{:S(2)}, u32[]{:S(2)}) collective-permute-start(f32[16,256]{1,0:T(8,128)S(1)} %get-tuple-element.48.refs_7_.refs_3_.refs_0_), channel_id=1, source_target_pairs={{0,12},{4,8},{8,4},{12,0},{1,13},{5,9},{9,5},{13,1},{2,14},{6,10},... | collective-permute-start | bytes 49160 | tf_op jit(solution)/shard_map/ppermute | solution.py:47
  25.2 3.7 %collective-permute-start.10 = (f32[16,256]{1,0:T(8,128)S(1)}, f32[16,256]{1,0:T(8,128)S(1)}, u32[]{:S(2)}, u32[]{:S(2)}) collective-permute-start(f32[16,256]{1,0:T(8,128)S(1)} %get-tuple-element.48.refs_7_.refs_3_.refs_0_), channel_id=1, source_target_pairs={{0,8},{4,12},{8,0},{12,4},{1,9},{5,13},{9,1},{13,5},{2,10},{6,14},... | collective-permute-start | bytes 49160 | tf_op jit(solution)/shard_map/ppermute | solution.py:47
  25.3 3.7 %collective-permute-start.9 = (f32[16,256]{1,0:T(8,128)S(1)}, f32[16,256]{1,0:T(8,128)S(1)}, u32[]{:S(2)}, u32[]{:S(2)}) collective-permute-start(f32[16,256]{1,0:T(8,128)S(1)} %get-tuple-element.48.refs_7_.refs_3_.refs_0_), channel_id=1, source_target_pairs={{0,4},{4,0},{8,12},{12,8},{1,5},{5,1},{9,13},{13,9},{2,6},{6,2},{1... | collective-permute-start | bytes 49160 | tf_op jit(solution)/shard_map/ppermute | solution.py:47
  31.9 8.8 %collective-permute-start.12 = (s16[528,256]{1,0:T(8,128)(2,1)S(1)}, s16[528,256]{1,0:T(8,128)(2,1)S(1)}, u32[]{:S(2)}, u32[]{:S(2)}) collective-permute-start(s16[528,256]{1,0:T(8,128)(2,1)S(1)} %get-tuple-element.50), channel_id=1, source_target_pairs={{0,4},{4,0},{8,12},{12,8},{1,5},{5,1},{9,13},{13,9},{2,6},{6,2},{1... | collective-permute-start | bytes 811016 | tf_op jit(solution)/shard_map/ppermute | solution.py:47
  33.8 10.6 %collective-permute-start.13 = (s16[528,256]{1,0:T(8,128)(2,1)S(1)}, s16[528,256]{1,0:T(8,128)(2,1)S(1)}, u32[]{:S(2)}, u32[]{:S(2)}) collective-permute-start(s16[528,256]{1,0:T(8,128)(2,1)S(1)} %get-tuple-element.51), channel_id=1, source_target_pairs={{0,8},{4,12},{8,0},{12,4},{1,9},{5,13},{9,1},{13,5},{2,10},{6,14},... | collective-permute-start | bytes 811016 | tf_op jit(solution)/shard_map/ppermute | solution.py:47
  35.3 9.1 %collective-permute-start.14 = (s16[528,256]{1,0:T(8,128)(2,1)S(1)}, s16[528,256]{1,0:T(8,128)(2,1)S(1)}, u32[]{:S(2)}, u32[]{:S(2)}) collective-permute-start(s16[528,256]{1,0:T(8,128)(2,1)S(1)} %get-tuple-element.52), channel_id=1, source_target_pairs={{0,12},{4,8},{8,4},{12,0},{1,13},{5,9},{9,5},{13,1},{2,14},{6,10},... | collective-permute-start | bytes 811016 | tf_op jit(solution)/shard_map/ppermute | solution.py:47
  39.0 1.6 %collective-permute-start.16 = (s16[192,512]{1,0:T(8,128)(2,1)S(1)}, s16[192,512]{1,0:T(8,128)(2,1)S(1)}, u32[]{:S(2)}, u32[]{:S(2)}) collective-permute-start(s16[192,512]{1,0:T(8,128)(2,1)S(1)} %get-tuple-element.61), channel_id=1, source_target_pairs={{0,16},{16,0},{1,17},{17,1},{2,18},{18,2},{3,19},{19,3},{4,20},{20... | collective-permute-start | bytes 589832 | tf_op jit(solution)/shard_map/ppermute | solution.py:47
  39.1 1.5 %collective-permute-start.15 = (s16[80,512]{1,0:T(8,128)(2,1)S(1)}, s16[80,512]{1,0:T(8,128)(2,1)S(1)}, u32[]{:S(2)}, u32[]{:S(2)}) collective-permute-start(s16[80,512]{1,0:T(8,128)(2,1)S(1)} %get-tuple-element.60), channel_id=1, source_target_pairs={{0,16},{16,0},{1,17},{17,1},{2,18},{18,2},{3,19},{19,3},{4,20},{20... | collective-permute-start | bytes 245768 | tf_op jit(solution)/shard_map/ppermute | solution.py:47
  40.9 4.6 %collective-permute-start.17 = (s16[144,256]{1,0:T(8,128)(2,1)S(1)}, s16[144,256]{1,0:T(8,128)(2,1)S(1)}, u32[]{:S(2)}, u32[]{:S(2)}) collective-permute-start(s16[144,256]{1,0:T(8,128)(2,1)S(1)} %get-tuple-element.63), channel_id=1, source_target_pairs={{0,4},{4,0},{8,12},{12,8},{1,5},{5,1},{9,13},{13,9},{2,6},{6,2},{1... | collective-permute-start | bytes 221192 | tf_op jit(solution)/shard_map/ppermute | solution.py:47
  42.8 4.4 %collective-permute-start.18 = (s16[144,256]{1,0:T(8,128)(2,1)S(1)}, s16[144,256]{1,0:T(8,128)(2,1)S(1)}, u32[]{:S(2)}, u32[]{:S(2)}) collective-permute-start(s16[144,256]{1,0:T(8,128)(2,1)S(1)} %get-tuple-element.64), channel_id=1, source_target_pairs={{0,8},{4,12},{8,0},{12,4},{1,9},{5,13},{9,1},{13,5},{2,10},{6,14},... | collective-permute-start | bytes 221192 | tf_op jit(solution)/shard_map/ppermute | solution.py:47
  44.3 5.3 %collective-permute-start.19 = (s16[144,256]{1,0:T(8,128)(2,1)S(1)}, s16[144,256]{1,0:T(8,128)(2,1)S(1)}, u32[]{:S(2)}, u32[]{:S(2)}) collective-permute-start(s16[144,256]{1,0:T(8,128)(2,1)S(1)} %get-tuple-element.65), channel_id=1, source_target_pairs={{0,12},{4,8},{8,4},{12,0},{1,13},{5,9},{9,5},{13,1},{2,14},{6,10},... | collective-permute-start | bytes 221192 | tf_op jit(solution)/shard_map/ppermute | solution.py:47
